TPU v7x, 256 devices: a whole 4x4x8 slice. The times are simulated.
256 devices in a mesh: dp: 16 (over z, core), tensor: 16 (over x, y).
Axes of the slice: x: 4, y: 4, z: 8, core: 2. Of those that a mesh axis runs over, the one named last changes fastest.
Arguments:
- input_acts: bfloat16 [14336, 8192], P('dp', 'tensor'), may hold values from -6 to 6
- out_grad: bfloat16 [14336, 8192], P('dp', 'tensor'), may hold values from -6 to 6
- base_weight: bfloat16 [8192, 8192], P(None, 'tensor'), may hold values from -0.0625 to 0.0625
- factor_a: bfloat16 [64, 32, 8192], P('dp', None, 'tensor'), may hold values from -6 to 6
- factor_b: bfloat16 [64, 32, 8192], P('dp', None, 'tensor'), may hold values from -6 to 6
- block_adapter: int32 [112], P('dp'), may hold values from 0 to 63, as said below
- adapter_slot: int32 [64], replicated, may hold values from 0 to 63, as said below
- rollout_map: int32 [16, 8], P('dp'), may hold values from 0 to 63
Outputs:
- input_gradient: bfloat16 [14336, 8192], P('dp', 'tensor')
- new_a: bfloat16 [64, 32, 8192], P('dp', None, 'tensor')
- new_b: bfloat16 [64, 32, 8192], P('dp', None, 'tensor')
- rollout_a: bfloat16 [128, 32, 8192], P('dp', None, 'tensor')
- rollout_b: bfloat16 [128, 32, 8192], P('dp', None, 'tensor')
Inputs may be any that keep to these rules, and one draw needn't show every extreme that they name: `block_adapter`: block b covers token rows b * 128 to (b + 1) * 128 - 1. The owner of an adapter is the dp index adapter_slot[adapter] // 4. Among the 7 blocks of one dp index, at most 1 have adapters of one owner. `adapter_slot`: each slot is taken by exactly one adapter.
All inputs are finite; a program needn't handle non-finite values.
Results may differ from a plain program's by a relative error of at most 0.02.
Values may be sent and summed in bfloat16 or wider, within the bound.
No kernel may reach another device: no remote copies, remote signals or barrier semaphores. Data moves between devices by JAX's collectives and lax.ppermute only.
A program may use at most 128 MiB of HBM per device.

v0:
```python
import functools
import math

import jax
import jax.numpy as jnp
from jax import lax
from jax.experimental import pallas as pl
from jax.experimental.pallas import tpu as pltpu
from jax.sharding import PartitionSpec as P

INPUT_FEATURES = 8192
ADAPTER_RANK = 32
BLOCK = 128
CORES = 2
SIDE = 4
LEARN_RATE = 0.25
SCALE = 1.0 / math.sqrt(INPUT_FEATURES * ADAPTER_RANK)

BF = jnp.bfloat16
F32 = jnp.float32
SMEM = functools.partial(pl.BlockSpec, memory_space=pltpu.SMEM)
VMEM = functools.partial(pl.BlockSpec, memory_space=pltpu.VMEM)
ANY = functools.partial(pl.BlockSpec, memory_space=pl.ANY)
PARAMS = pltpu.CompilerParams(vmem_limit_bytes=32 * 2**20)


def slot_lookup(adapter_ids, adapter_slot):
    matches = adapter_ids[:, None] == jnp.arange(adapter_slot.shape[0], dtype=jnp.int32)[None, :]
    return jnp.sum(jnp.where(matches, adapter_slot[None, :], 0), axis=1)


def z_hop(x, step):
    n = lax.axis_size("dp")
    chips = n // CORES
    perm = [(d, (d // CORES + step) % chips * CORES + d % CORES) for d in range(n)]
    return lax.ppermute(x, "dp", perm)


def core_swap(x):
    n = lax.axis_size("dp")
    return lax.ppermute(x, "dp", [(d, d ^ 1) for d in range(n)])


def plane_hop(x, step, axis):
    n = lax.axis_size("tensor")
    if axis == "y":
        perm = [(t, t // SIDE * SIDE + (t + step) % SIDE) for t in range(n)]
    else:
        perm = [(t, (t + step * SIDE) % n) for t in range(n)]
    return lax.ppermute(x, "tensor", perm)


def ring_gather(p, q):
    found = []
    last = []
    for x in (p, q):
        up = down = x
        parts = {0: x}
        for step in range(1, 4):
            up, down = z_hop(up, 1), z_hop(down, -1)
            parts[8 - step], parts[step] = up, down
        found.append(parts)
        last.append((up, down))
    found[0][4] = z_hop(last[0][0], 1)
    found[1][4] = z_hop(last[1][1], -1)
    return [[parts[place] for place in range(8)] for parts in found]


def fetch(sources, target, sems, first):
    copies, row = [], 0
    for k, ref in enumerate(sources):
        rows = ref.shape[0]
        copies.append(pltpu.make_async_copy(ref, target.at[pl.ds(row, rows)], sems.at[first + k]))
        row += rows
    for copy in copies:
        copy.start()
    return copies


def select_kernel(blocks, rolls, slots, rank, *refs):
    place, refs = refs[0], refs[1:]
    a_refs, b_refs = refs[:8], refs[8:16]
    mine_ref, other_ref, mine_roll, other_roll, ids_ref, hold_a, hold_b, sems = refs[16:]
    copies = fetch(a_refs, hold_a, sems, 0) + fetch(b_refs, hold_b, sems, 8)
    for copy in copies:
        copy.wait()
    need = blocks + rolls
    tail = b_refs[0].shape[0] - slots * rank

    def from_a(at):
        return hold_a[pl.ds(pl.multiple_of(place[at] * rank, rank), rank), :]

    def from_b(at):
        row = place[at] * rank + place[at] // slots * tail
        return hold_b[pl.ds(pl.multiple_of(row, 16), rank), :]

    for n in range(blocks):
        mine_ref[n] = from_a(n)
        mine_ref[blocks + n] = from_b(n)
        other_ref[n] = from_a(need + n)
        other_ref[blocks + n] = from_b(need + n)
    for n in range(rolls):
        mine_roll[n] = from_a(blocks + n)
        mine_roll[rolls + n] = from_b(blocks + n)
        other_roll[n] = from_a(need + blocks + n)
        other_roll[rolls + n] = from_b(need + blocks + n)
    for k in range(8):
        row = k * (slots * rank + tail) + slots * rank
        ids_ref[k] = hold_b[row : row + tail, : ids_ref.shape[2]]


def select(place, parts_a, parts_b, blocks, rolls, slots):
    rows, width = parts_a[0].shape
    rank = rows // slots
    tall = parts_b[0].shape[0]
    shape = lambda n: jax.ShapeDtypeStruct((n, rank, width), BF)
    return pl.pallas_call(
        functools.partial(select_kernel, blocks, rolls, slots, rank),
        out_shape=(
            shape(2 * blocks), shape(2 * blocks), shape(2 * rolls), shape(2 * rolls),
            jax.ShapeDtypeStruct((8, tall - rows, 128), BF),
        ),
        in_specs=[SMEM()] + [ANY()] * 16,
        out_specs=(VMEM(),) * 5,
        scratch_shapes=[
            pltpu.VMEM((8 * rows, width), BF),
            pltpu.VMEM((8 * tall, width), BF),
            pltpu.SemaphoreType.DMA((16,)),
        ],
        compiler_params=PARAMS,
        cost_estimate=pl.CostEstimate(flops=0, bytes_accessed=8 * 2**20, transcendentals=0),
        name="select_factors",
    )(place, *parts_a, *parts_b)


def project_kernel(blocks, own_ref, mine_ref, other_ref, acts_ref, grad_ref, chosen_ref, out_ref):
    for n in range(blocks):
        own = own_ref[n] == 1
        rows = pl.ds(n * BLOCK, BLOCK)
        factor_a = jnp.where(own, mine_ref[n], other_ref[n])
        factor_b = jnp.where(own, mine_ref[blocks + n], other_ref[blocks + n])
        chosen_ref[n] = factor_a
        contract = (((1,), (1,)), ((), ()))
        out_ref[n] = lax.dot_general(
            factor_b, grad_ref[rows, :], contract, preferred_element_type=F32
        ).astype(BF)
        out_ref[blocks + n] = lax.dot_general(
            factor_a, acts_ref[rows, :], contract, preferred_element_type=F32
        ).astype(BF)


def project(own, mine, other, acts, grad):
    blocks, (rank, width) = mine.shape[0] // 2, mine.shape[1:]
    return pl.pallas_call(
        functools.partial(project_kernel, blocks),
        out_shape=(
            jax.ShapeDtypeStruct((blocks, rank, width), BF),
            jax.ShapeDtypeStruct((2 * blocks, rank, BLOCK), BF),
        ),
        in_specs=[SMEM()] + [VMEM()] * 4,
        out_specs=(VMEM(),) * 2,
        compiler_params=PARAMS,
        cost_estimate=pl.CostEstimate(flops=0, bytes_accessed=8 * 2**20, transcendentals=0),
        name="project_ranks",
    )(own, mine, other, acts, grad)


def plane_sum(x):
    for axis in ("y", "x"):
        terms = [x] + [plane_hop(x, step, axis) for step in (1, 3, 2)]
        x = sum(term.astype(F32) for term in terms).astype(BF)
    return x


def contribute_kernel(blocks, ranks_ref, acts_ref, grad_ref, a_ref, b_ref):
    for n in range(blocks):
        rows = pl.ds(n * BLOCK, BLOCK)
        a_ref[n] = (
            SCALE * jnp.dot(ranks_ref[n], acts_ref[rows, :], preferred_element_type=F32)
        ).astype(BF)
        b_ref[n] = (
            SCALE * jnp.dot(ranks_ref[blocks + n], grad_ref[rows, :], preferred_element_type=F32)
        ).astype(BF)


def contribute(ranks, acts, grad):
    blocks, rank, width = ranks.shape[0] // 2, ranks.shape[1], acts.shape[1]
    shape = jax.ShapeDtypeStruct((blocks, rank, width), BF)
    return pl.pallas_call(
        functools.partial(contribute_kernel, blocks),
        out_shape=(shape, shape),
        in_specs=[VMEM()] * 3,
        out_specs=(VMEM(),) * 2,
        compiler_params=PARAMS,
        cost_estimate=pl.CostEstimate(flops=0, bytes_accessed=8 * 2**20, transcendentals=0),
        name="factor_contributions",
    )(ranks, acts, grad)


def total_kernel(needs, *refs):
    place, used, refs = refs[0], refs[1], refs[2:]
    a_refs, b_refs = refs[:7], refs[7:14]
    mine_ref, other_ref, hold_a, hold_b, sems = refs[14:]
    copies = fetch(a_refs, hold_a, sems, 0) + fetch(b_refs, hold_b, sems, 7)
    for copy in copies:
        copy.wait()

    def one(need, hold):
        def term(source):
            at = need * 8 + source
            return hold[place[at]].astype(F32) * used[at].astype(F32)

        value = term(0)
        for source in range(1, 7):
            value += term(source)
        return value

    @pl.loop(0, needs)
    def _(need):
        mine_ref[need] = one(need, hold_a)
        mine_ref[needs + need] = one(need, hold_b)
        other_ref[need] = one(needs + need, hold_a)
        other_ref[needs + need] = one(needs + need, hold_b)


def total(place, used, parts_a, parts_b, needs):
    blocks, (rank, width) = 7 * parts_a[0].shape[0], parts_a[0].shape[1:]
    shape = jax.ShapeDtypeStruct((2 * needs, rank, width), F32)
    return pl.pallas_call(
        functools.partial(total_kernel, needs),
        out_shape=(shape, shape),
        in_specs=[SMEM()] * 2 + [ANY()] * 14,
        out_specs=(VMEM(),) * 2,
        scratch_shapes=[
            pltpu.VMEM((blocks, rank, width), BF),
            pltpu.VMEM((blocks, rank, width), BF),
            pltpu.SemaphoreType.DMA((14,)),
        ],
        compiler_params=PARAMS,
        cost_estimate=pl.CostEstimate(flops=0, bytes_accessed=16 * 2**20, transcendentals=0),
        name="gradient_totals",
    )(place, used, *parts_a, *parts_b)


def far_term(place, used, far_ref, need, first):
    at = need * 8 + 7
    return far_ref[place[at] - first].astype(F32) * used[at].astype(F32)


def share_kernel(needs, first, place, used, far_a, far_b, near_ref, out_ref):
    @pl.loop(0, needs)
    def _(need):
        for k, far in enumerate((far_a, far_b)):
            at = k * needs + need
            out_ref[at] = (
                near_ref[at] + far_term(place, used, far, needs + need, first)
            ).astype(BF)


def share(place, used, far_a, far_b, near):
    return pl.pallas_call(
        functools.partial(share_kernel, near.shape[0] // 2, 7 * far_a.shape[0]),
        out_shape=jax.ShapeDtypeStruct(near.shape, BF),
        in_specs=[SMEM()] * 2 + [VMEM()] * 3,
        out_specs=VMEM(),
        compiler_params=PARAMS,
        cost_estimate=pl.CostEstimate(flops=0, bytes_accessed=4 * 2**20, transcendentals=0),
        name="gradient_share",
    )(place, used, far_a, far_b, near)


def update_kernel(
    slots, rolls, first, place, used, own_ref, a_ref, b_ref, mine_roll, other_roll,
    far_a, far_b, mine_ref, other_ref, new_a, new_b, roll_a, roll_b,
):
    needs = slots + rolls

    def fresh(factor, at, far):
        gradient = (
            mine_ref[at]
            + far_term(place, used, far, at % needs, first)
            + other_ref[at].astype(F32)
        )
        return (factor.astype(F32) - LEARN_RATE * gradient).astype(BF)

    for n in range(slots):
        new_a[n] = fresh(a_ref[n], n, far_a)
        new_b[n] = fresh(b_ref[n], needs + n, far_b)
    for n in range(rolls):
        own = own_ref[n] == 1
        roll_a[n] = fresh(jnp.where(own, mine_roll[n], other_roll[n]), slots + n, far_a)
        roll_b[n] = fresh(
            jnp.where(own, mine_roll[rolls + n], other_roll[rolls + n]), needs + slots + n, far_b
        )


def update(place, used, own, factor_a, factor_b, mine_roll, other_roll, far_a, far_b, mine, other):
    slots, rank, width = factor_a.shape
    rolls = mine_roll.shape[0] // 2
    shape = lambda n: jax.ShapeDtypeStruct((n, rank, width), BF)
    return pl.pallas_call(
        functools.partial(update_kernel, slots, rolls, 7 * far_a.shape[0]),
        out_shape=(shape(slots), shape(slots), shape(rolls), shape(rolls)),
        in_specs=[SMEM()] * 3 + [VMEM()] * 8,
        out_specs=(VMEM(),) * 4,
        compiler_params=PARAMS,
        cost_estimate=pl.CostEstimate(flops=0, bytes_accessed=8 * 2**20, transcendentals=0),
        name="update_factors",
    )(place, used, own, factor_a, factor_b, mine_roll, other_roll, far_a, far_b, mine, other)


def frozen_kernel(grad_ref, weight_ref, out_ref):
    out_ref[...] = lax.dot_general(
        grad_ref[...], weight_ref[...], (((1,), (1,)), ((), ())), preferred_element_type=F32
    ).astype(BF)


def frozen(grad, weight):
    (rows, depth), columns = grad.shape, weight.shape[0]
    tile = 1024
    return pl.pallas_call(
        frozen_kernel,
        grid=(columns // tile,),
        out_shape=jax.ShapeDtypeStruct((rows, columns), BF),
        in_specs=[
            pl.BlockSpec((rows, depth), lambda j: (0, 0)),
            pl.BlockSpec((tile, depth), lambda j: (j, 0)),
        ],
        out_specs=pl.BlockSpec((rows, tile), lambda j: (0, j)),
        compiler_params=PARAMS,
        cost_estimate=pl.CostEstimate(
            flops=2 * rows * depth * columns, bytes_accessed=24 * 2**20, transcendentals=0
        ),
        name="frozen_partial",
    )(grad, weight)


def finish_kernel(blocks, ranks_ref, chosen_ref, base_ref, out_ref):
    for n in range(blocks):
        rows = pl.ds(n * BLOCK, BLOCK)
        term = lax.dot_general(
            ranks_ref[n], chosen_ref[n], (((0,), (0,)), ((), ())), preferred_element_type=F32
        )
        out_ref[rows, :] = (base_ref[rows, :].astype(F32) + SCALE * term).astype(BF)


def finish(ranks, chosen, base):
    blocks = chosen.shape[0]
    return pl.pallas_call(
        functools.partial(finish_kernel, blocks),
        out_shape=jax.ShapeDtypeStruct(base.shape, BF),
        in_specs=[VMEM()] * 3,
        out_specs=VMEM(),
        compiler_params=PARAMS,
        cost_estimate=pl.CostEstimate(flops=0, bytes_accessed=4 * 2**20, transcendentals=0),
        name="input_gradient",
    )(ranks, chosen, base)


def per_device(
    input_acts, out_grad, base_weight, factor_a, factor_b, block_adapter, adapter_slot, rollout_map
):
    blocks = block_adapter.shape[0]
    slots = factor_a.shape[0]
    rolls = rollout_map.size
    groups = lax.axis_size("dp")
    chips = groups // CORES
    me = lax.axis_index("dp")
    chip, core = me // CORES, me % CORES

    wanted = slot_lookup(jnp.concatenate([block_adapter, rollout_map.reshape(-1)]), adapter_slot)
    other_wanted = core_swap(wanted)
    other = me ^ 1

    def places(slot_ids):
        owner = slot_ids // slots
        here = owner % CORES == core
        distance = (owner // CORES - chip + chips) % chips
        return jnp.where(here, distance * slots + slot_ids % slots, 0), here.astype(jnp.int32)

    mine_place, mine_own = places(wanted)
    other_place, _ = places(other_wanted)

    partial_value = frozen(out_grad, base_weight)
    base = lax.psum_scatter(partial_value, "tensor", scatter_dimension=1, tiled=True)

    width = factor_a.shape[2]
    ids = jnp.pad(wanted[None].astype(BF), ((0, 15), (0, width - blocks - rolls)))
    parts_a, parts_b = ring_gather(
        factor_a.reshape(-1, width), jnp.concatenate([factor_b.reshape(-1, width), ids])
    )
    mine_sel, other_sel, mine_roll, other_roll, ring_ids = select(
        jnp.concatenate([mine_place, other_place]), parts_a, parts_b, blocks, rolls, slots
    )
    got_sel = core_swap(other_sel)
    got_roll = core_swap(other_roll)
    chosen_a, rank_parts = project(mine_own[:blocks], mine_sel, got_sel, input_acts, out_grad)
    ranks = plane_sum(rank_parts)

    order = [0, 1, 2, 3, 5, 6, 7, 4]
    ring = ring_ids[:, 0, :blocks].astype(jnp.int32)
    ring = jnp.stack([ring[k] for k in order])
    own_slots = jnp.arange(slots, dtype=jnp.int32)
    need = jnp.concatenate(
        [me * slots + own_slots, wanted[blocks:], other * slots + own_slots, other_wanted[blocks:]]
    )
    match = (need[:, None, None] == ring[None]).astype(jnp.int32)
    used = jnp.sum(match, axis=2)
    at_block = jnp.sum(match * jnp.arange(blocks, dtype=jnp.int32)[None, None], axis=2)
    source = jnp.arange(chips, dtype=jnp.int32)[None, :] * blocks + at_block
    source, used = source.reshape(-1), used.reshape(-1)

    part_a, part_b = contribute(ranks, input_acts, out_grad)
    parts_a, parts_b = ring_gather(part_a, part_b)
    near = order[:7]
    mine_total, other_total = total(
        source, used, [parts_a[k] for k in near], [parts_b[k] for k in near], slots + rolls
    )
    got_total = core_swap(share(source, used, parts_a[4], parts_b[4], other_total))
    new_a, new_b, roll_a, roll_b = update(
        source, used, mine_own[blocks:], factor_a, factor_b, mine_roll, got_roll,
        parts_a[4], parts_b[4], mine_total, got_total,
    )
    return finish(ranks, chosen_a, base), new_a, new_b, roll_a, roll_b


def solution(mesh):
    return jax.shard_map(
        per_device,
        mesh=mesh,
        in_specs=(
            P("dp", "tensor"),
            P("dp", "tensor"),
            P(None, "tensor"),
            P("dp", None, "tensor"),
            P("dp", None, "tensor"),
            P("dp"),
            P(),
            P("dp", None),
        ),
        out_specs=(
            P("dp", "tensor"),
            P("dp", None, "tensor"),
            P("dp", None, "tensor"),
            P("dp", None, "tensor"),
            P("dp", None, "tensor"),
        ),
        check_vma=False,
    )
```

profile of v0, /device:TPU:1, one launch (start us, length us, event | category | flops | bytes accessed | tf_op | source)
XLA Modules:
  0.0 154.5 jit_solution(13950709791972448407)
XLA Ops:
  8.4 3.4 %copy-done.6 = bf16[8192,512]{1,0:T(8,128)(2,1)S(1)} copy-done((bf16[8192,512]{1,0:T(8,128)(2,1)S(1)}, bf16[8192,512]{1,0:T(8,128)(2,1)}, u32[]{:S(2)}) %copy-start.6) | copy-done | bytes 8388632
  11.8 10.8 %frozen_partial.1 = bf16[896,8192]{1,0:T(8,128)(2,1)} custom-call(bf16[896,512]{1,0:T(8,128)(2,1)S(1)} %copy-done.1, bf16[8192,512]{1,0:T(8,128)(2,1)S(1)} %copy-done.6), custom_call_target="tpu_custom_call" | custom-call | flops 7516192768 | bytes 25165824 | tf_op jit(solution)/shard_map/frozen_partial/pallas_call | solution.py:321
  23.6 6.5 %collective-permute-start.8 = (bf16[144,512]{1,0:T(8,128)(2,1)S(1)}, bf16[144,512]{1,0:T(8,128)(2,1)S(1)}, u32[]{:S(2)}, u32[]{:S(2)}) collective-permute-start(bf16[144,512]{1,0:T(8,128)(2,1)S(1)} %fusion.1.refs_9_), channel_id=1, source_target_pairs={{0,224},{16,240},{32,0},{48,16},{64,32},{80,48},{96,64},{112,80},{... | collective-permute-start | bytes 442376 | tf_op jit(solution)/shard_map/ppermute | solution.py:36
  30.1 2.5 %collective-permute-done.8.refs_10_ = bf16[144,512]{1,0:T(8,128)(2,1)S(1)} collective-permute-done((bf16[144,512]{1,0:T(8,128)(2,1)S(1)}, bf16[144,512]{1,0:T(8,128)(2,1)S(1)}, u32[]{:S(2)}, u32[]{:S(2)}) %collective-permute-start.8) | collective-permute-done | bytes 147488 | tf_op jit(solution)/shard_map/ppermute | solution.py:36
  32.6 3.4 %collective-permute-start.9 = (bf16[144,512]{1,0:T(8,128)(2,1)S(1)}, bf16[144,512]{1,0:T(8,128)(2,1)S(1)}, u32[]{:S(2)}, u32[]{:S(2)}) collective-permute-start(bf16[144,512]{1,0:T(8,128)(2,1)S(1)} %collective-permute-done.8.refs_10_), channel_id=1, source_target_pairs={{0,224},{16,240},{32,0},{48,16},{64,32},{80,48},{96,64},{112,80},{... | collective-permute-start | bytes 442376 | tf_op jit(solution)/shard_map/ppermute | solution.py:36
  38.5 2.7 %collective-permute-start.10 = (bf16[144,512]{1,0:T(8,128)(2,1)S(1)}, bf16[144,512]{1,0:T(8,128)(2,1)S(1)}, u32[]{:S(2)}, u32[]{:S(2)}) collective-permute-start(bf16[144,512]{1,0:T(8,128)(2,1)S(1)} %collective-permute-done.9.refs_11_), channel_id=1, source_target_pairs={{0,224},{16,240},{32,0},{48,16},{64,32},{80,48},{96,64},{112,80},{... | collective-permute-start | bytes 442376 | tf_op jit(solution)/shard_map/ppermute | solution.py:36
  41.2 2.6 %collective-permute-start.2 = (bf16[128,512]{1,0:T(8,128)(2,1)S(1)}, bf16[128,512]{1,0:T(8,128)(2,1)S(1)}, u32[]{:S(2)}, u32[]{:S(2)}) collective-permute-start(bf16[128,512]{1,0:T(8,128)(2,1)S(1)} %collective-permute-done.1.refs_2_), channel_id=1, source_target_pairs={{0,224},{16,240},{32,0},{48,16},{64,32},{80,48},{96,64},{112,80},{... | collective-permute-start | bytes 393224 | tf_op jit(solution)/shard_map/ppermute | solution.py:36
  43.8 3.4 %collective-permute-start = (s32[15]{0:T(128)S(1)}, s32[15]{0:T(128)S(1)}, u32[]{:S(2)}, u32[]{:S(2)}) collective-permute-start(s32[15]{0:T(128)S(1)} %select_reduce_fusion), channel_id=1, source_target_pairs={{0,16},{16,0},{32,48},{48,32},{64,80},{80,64},{96,112},{112,96},{1... | collective-permute-start | bytes 188 | tf_op jit(solution)/shard_map/ppermute | solution.py:41
  47.3 3.0 %collective-permute-start.3 = (bf16[128,512]{1,0:T(8,128)(2,1)S(1)}, bf16[128,512]{1,0:T(8,128)(2,1)S(1)}, u32[]{:S(2)}, u32[]{:S(2)}) collective-permute-start(bf16[128,512]{1,0:T(8,128)(2,1)S(1)} %collective-permute-done.2.refs_3_), channel_id=1, source_target_pairs={{0,224},{16,240},{32,0},{48,16},{64,32},{80,48},{96,64},{112,80},{... | collective-permute-start | bytes 393224 | tf_op jit(solution)/shard_map/ppermute | solution.py:36
  50.3 2.8 %collective-permute-start.11 = (bf16[144,512]{1,0:T(8,128)(2,1)S(1)}, bf16[144,512]{1,0:T(8,128)(2,1)S(1)}, u32[]{:S(2)}, u32[]{:S(2)}) collective-permute-start(bf16[144,512]{1,0:T(8,128)(2,1)S(1)} %collective-permute-done.10.refs_12_), channel_id=1, source_target_pairs={{0,224},{16,240},{32,0},{48,16},{64,32},{80,48},{96,64},{112,80},{... | collective-permute-start | bytes 442376 | tf_op jit(solution)/shard_map/ppermute | solution.py:36
  53.3 2.5 %collective-permute-done.14.refs_14_ = bf16[144,512]{1,0:T(8,128)(2,1)S(1)} collective-permute-done((bf16[144,512]{1,0:T(8,128)(2,1)S(1)}, bf16[144,512]{1,0:T(8,128)(2,1)S(1)}, u32[]{:S(2)}, u32[]{:S(2)}) %collective-permute-start.14) | collective-permute-done | bytes 147488 | tf_op jit(solution)/shard_map/ppermute | solution.py:36
  57.2 4.0 %select_factors.1 = (bf16[14,32,512]{2,1,0:T(8,128)(2,1)S(1)}, bf16[14,32,512]{2,1,0:T(8,128)(2,1)S(1)}, bf16[16,32,512]{2,1,0:T(8,128)(2,1)S(1)}, bf16[16,32,51...) custom-call(s32[30]{0:T(128)S(1)} %pad_add_fusion.2.refs_0_, bf16[128,512]{1,0:T(8,128)(2,1)S(1)} %bitcast.14, ...), custom_call_target="tpu_custom_call" | custom-call | bytes 8388608 | tf_op jit(solution)/shard_map/select_factors/pallas_call | solution.py:117
  61.2 4.1 %collective-permute-start.15 = (bf16[14,32,512]{2,1,0:T(8,128)(2,1)S(1)}, bf16[14,32,512]{2,1,0:T(8,128)(2,1)S(1)}, u32[]{:S(2)}, u32[]{:S(2)}) collective-permute-start(bf16[14,32,512]{2,1,0:T(8,128)(2,1)S(1)} %get-tuple-element.21), channel_id=1, source_target_pairs={{0,16},{16,0},{32,48},{48,32},{64,80},{80,64},{96,112},{112,96},{1... | collective-permute-start | bytes 1376264 | tf_op jit(solution)/shard_map/ppermute | solution.py:41
  67.9 3.0 %collective-permute-start.18 = (bf16[14,32,128]{2,1,0:T(8,128)(2,1)S(1)}, bf16[14,32,128]{2,1,0:T(8,128)(2,1)S(1)}, u32[]{:S(2)}, u32[]{:S(2)}) collective-permute-start(bf16[14,32,128]{2,1,0:T(8,128)(2,1)S(1)} %get-tuple-element.22), channel_id=1, source_target_pairs={{0,2},{1,3},{2,0},{3,1},{4,6},{5,7},{6,4},{7,5},{8,10},{9,11},{10,... | collective-permute-start | bytes 344072 | tf_op jit(solution)/shard_map/ppermute | solution.py:50
  72.4 4.4 %collective-permute-done.18 = bf16[14,32,128]{2,1,0:T(8,128)(2,1)S(1)} collective-permute-done((bf16[14,32,128]{2,1,0:T(8,128)(2,1)S(1)}, bf16[14,32,128]{2,1,0:T(8,128)(2,1)S(1)}, u32[]{:S(2)}, u32[]{:S(2)}) %collective-permute-start.18) | collective-permute-done | bytes 114720 | tf_op jit(solution)/shard_map/ppermute | solution.py:50
  76.8 5.2 %collective-permute-done.17 = bf16[14,32,128]{2,1,0:T(8,128)(2,1)S(1)} collective-permute-done((bf16[14,32,128]{2,1,0:T(8,128)(2,1)S(1)}, bf16[14,32,128]{2,1,0:T(8,128)(2,1)S(1)}, u32[]{:S(2)}, u32[]{:S(2)}) %collective-permute-start.17) | collective-permute-done | bytes 114720 | tf_op jit(solution)/shard_map/ppermute | solution.py:50
  82.1 2.6 %collective-permute-start.21 = (bf16[14,32,128]{2,1,0:T(8,128)(2,1)S(1)}, bf16[14,32,128]{2,1,0:T(8,128)(2,1)S(1)}, u32[]{:S(2)}, u32[]{:S(2)}) collective-permute-start(bf16[14,32,128]{2,1,0:T(8,128)(2,1)S(1)} %add_convert_fusion.1), channel_id=1, source_target_pairs={{0,8},{1,9},{2,10},{3,11},{4,12},{5,13},{6,14},{7,15},{8,0},{9,1},... | collective-permute-start | bytes 344072 | tf_op jit(solution)/shard_map/ppermute | solution.py:50
  86.2 4.5 %collective-permute-done.21 = bf16[14,32,128]{2,1,0:T(8,128)(2,1)S(1)} collective-permute-done((bf16[14,32,128]{2,1,0:T(8,128)(2,1)S(1)}, bf16[14,32,128]{2,1,0:T(8,128)(2,1)S(1)}, u32[]{:S(2)}, u32[]{:S(2)}) %collective-permute-start.21) | collective-permute-done | bytes 114720 | tf_op jit(solution)/shard_map/ppermute | solution.py:50
  90.7 4.7 %collective-permute-done.20 = bf16[14,32,128]{2,1,0:T(8,128)(2,1)S(1)} collective-permute-done((bf16[14,32,128]{2,1,0:T(8,128)(2,1)S(1)}, bf16[14,32,128]{2,1,0:T(8,128)(2,1)S(1)}, u32[]{:S(2)}, u32[]{:S(2)}) %collective-permute-start.20) | collective-permute-done | bytes 114720 | tf_op jit(solution)/shard_map/ppermute | solution.py:50
  95.9 2.7 %collective-permute-start.27 = (bf16[7,32,512]{2,1,0:T(8,128)(2,1)S(1)}, bf16[7,32,512]{2,1,0:T(8,128)(2,1)S(1)}, u32[]{:S(2)}, u32[]{:S(2)}) collective-permute-start(bf16[7,32,512]{2,1,0:T(8,128)(2,1)S(1)} %get-tuple-element.28.refs_9_), channel_id=1, source_target_pairs={{0,224},{16,240},{32,0},{48,16},{64,32},{80,48},{96,64},{112,80},{... | collective-permute-start | bytes 688136 | tf_op jit(solution)/shard_map/ppermute | solution.py:36
  100.2 2.2 %collective-permute-done.23.refs_8_ = bf16[7,32,512]{2,1,0:T(8,128)(2,1)S(1)} collective-permute-done((bf16[7,32,512]{2,1,0:T(8,128)(2,1)S(1)}, bf16[7,32,512]{2,1,0:T(8,128)(2,1)S(1)}, u32[]{:S(2)}, u32[]{:S(2)}) %collective-permute-start.23) | collective-permute-done | bytes 229408 | tf_op jit(solution)/shard_map/ppermute | solution.py:36
  102.4 2.7 %collective-permute-start.28 = (bf16[7,32,512]{2,1,0:T(8,128)(2,1)S(1)}, bf16[7,32,512]{2,1,0:T(8,128)(2,1)S(1)}, u32[]{:S(2)}, u32[]{:S(2)}) collective-permute-start(bf16[7,32,512]{2,1,0:T(8,128)(2,1)S(1)} %collective-permute-done.27.refs_10_), channel_id=1, source_target_pairs={{0,224},{16,240},{32,0},{48,16},{64,32},{80,48},{96,64},{112,80},{... | collective-permute-start | bytes 688136 | tf_op jit(solution)/shard_map/ppermute | solution.py:36
  106.5 2.9 %collective-permute-start.32 = (bf16[7,32,512]{2,1,0:T(8,128)(2,1)S(1)}, bf16[7,32,512]{2,1,0:T(8,128)(2,1)}, u32[]{:S(2)}, u32[]{:S(2)}) collective-permute-start(bf16[7,32,512]{2,1,0:T(8,128)(2,1)S(1)} %collective-permute-done.31.refs_3_), channel_id=1, source_target_pairs={{0,224},{16,240},{32,0},{48,16},{64,32},{80,48},{96,64},{112,80},{... | collective-permute-start | bytes 688136 | tf_op jit(solution)/shard_map/ppermute | solution.py:36
  109.4 3.2 %collective-permute-done.24.refs_7_ = bf16[7,32,512]{2,1,0:T(8,128)(2,1)S(1)} collective-permute-done((bf16[7,32,512]{2,1,0:T(8,128)(2,1)S(1)}, bf16[7,32,512]{2,1,0:T(8,128)(2,1)S(1)}, u32[]{:S(2)}, u32[]{:S(2)}) %collective-permute-start.24) | collective-permute-done | bytes 229408 | tf_op jit(solution)/shard_map/ppermute | solution.py:36
  112.7 2.7 %collective-permute-start.29 = (bf16[7,32,512]{2,1,0:T(8,128)(2,1)S(1)}, bf16[7,32,512]{2,1,0:T(8,128)(2,1)}, u32[]{:S(2)}, u32[]{:S(2)}) collective-permute-start(bf16[7,32,512]{2,1,0:T(8,128)(2,1)S(1)} %collective-permute-done.28.refs_11_), channel_id=1, source_target_pairs={{0,224},{16,240},{32,0},{48,16},{64,32},{80,48},{96,64},{112,80},{... | collective-permute-start | bytes 688136 | tf_op jit(solution)/shard_map/ppermute | solution.py:36
  116.3 2.8 %collective-permute-start.33 = (bf16[7,32,512]{2,1,0:T(8,128)(2,1)}, bf16[7,32,512]{2,1,0:T(8,128)(2,1)}, u32[]{:S(2)}, u32[]{:S(2)}) collective-permute-start(bf16[7,32,512]{2,1,0:T(8,128)(2,1)} %collective-permute-done.32.refs_4_), channel_id=1, source_target_pairs={{0,224},{16,240},{32,0},{48,16},{64,32},{80,48},{96,64},{112,80},{... | collective-permute-start | bytes 688136 | tf_op jit(solution)/shard_map/ppermute | solution.py:36
  121.2 3.1 %collective-permute-start.30 = (bf16[7,32,512]{2,1,0:T(8,128)(2,1)}, bf16[7,32,512]{2,1,0:T(8,128)(2,1)S(1)}, u32[]{:S(2)}, u32[]{:S(2)}) collective-permute-start(bf16[7,32,512]{2,1,0:T(8,128)(2,1)} %collective-permute-done.29.refs_12_), channel_id=1, source_target_pairs={{0,224},{16,240},{32,0},{48,16},{64,32},{80,48},{96,64},{112,80},{... | collective-permute-start | bytes 688136 | tf_op jit(solution)/shard_map/ppermute | solution.py:36
  126.1 1.8 %collective-permute-done.36.refs_13_ = bf16[7,32,512]{2,1,0:T(8,128)(2,1)} collective-permute-done((bf16[7,32,512]{2,1,0:T(8,128)(2,1)}, bf16[7,32,512]{2,1,0:T(8,128)(2,1)}, u32[]{:S(2)}, u32[]{:S(2)}) %collective-permute-start.36) | collective-permute-done | bytes 229408 | tf_op jit(solution)/shard_map/ppermute | solution.py:36
  127.9 6.1 %gradient_totals.1 = (f32[24,32,512]{2,1,0:T(8,128)S(1)}, f32[24,32,512]{2,1,0:T(8,128)S(1)}) custom-call(s32[192]{0:T(256)S(1)} %add.116.refs_0_.place, s32[192]{0:T(256)S(1)} %reshape.51.refs_1_.used, bf16[7,32,512]{2,1,0:T(8,128)(2,1)S(1)} %get-tuple-element.27.refs_2_, bf16[7,32,512]{2,1,0:T(8,128)(2,1)S(1)} %collective-permute-done.31.refs_3_, ...), custom_call_target="tpu_custom_call" | custom-call | bytes 16777216 | tf_op jit(solution)/shard_map/gradient_totals/pallas_call | solution.py:229
  134.9 5.5 %collective-permute-start.37 = (bf16[24,32,512]{2,1,0:T(8,128)(2,1)S(1)}, bf16[24,32,512]{2,1,0:T(8,128)(2,1)S(1)}, u32[]{:S(2)}, u32[]{:S(2)}) collective-permute-start(bf16[24,32,512]{2,1,0:T(8,128)(2,1)S(1)} %gradient_share.1), channel_id=1, source_target_pairs={{0,16},{16,0},{32,48},{48,32},{64,80},{80,64},{96,112},{112,96},{1... | collective-permute-start | bytes 2359304 | tf_op jit(solution)/shard_map/ppermute | solution.py:41
  140.6 2.7 %collective-permute-done.22.other_roll = bf16[16,32,512]{2,1,0:T(8,128)(2,1)S(1)} collective-permute-done((bf16[16,32,512]{2,1,0:T(8,128)(2,1)}, bf16[16,32,512]{2,1,0:T(8,128)(2,1)S(1)}, u32[]{:S(2)}, u32[]{:S(2)}) %collective-permute-start.22) | collective-permute-done | bytes 524320 | tf_op jit(solution)/shard_map/ppermute | solution.py:41
  143.3 1.8 %update_factors.1 = (bf16[4,32,512]{2,1,0:T(8,128)(2,1)}, bf16[4,32,512]{2,1,0:T(8,128)(2,1)}, bf16[8,32,512]{2,1,0:T(8,128)(2,1)}, bf16[8,32,512]{2,1,0:T(8,128)(2,1)}) custom-call(s32[192]{0:T(256)S(1)} %add.116.refs_0_.place, s32[192]{0:T(256)S(1)} %reshape.51.refs_1_.used, s32[8]{0:T(128)S(1)} %slice.50.own_ref, bf16[4,32,512]{2,1,0:T(8,128)(2,1)S(1)} %copy-done.4, ...), custom_call_target="tpu_custom_call" | custom-call | bytes 8388608 | tf_op jit(solution)/shard_map/update_factors/pallas_call | solution.py:301
  (105 shorter events, 23.9 us)
Async XLA Ops:
  7.2 138.0 %reduce-scatter.2.cloned.1.call-start = ((), (), s32[]{:S(2)}) async-start(), calls=%async_computation.1 | async-start | bytes 15597568 | tf_op jit(solution)/shard_map/reduce_scatter | solution.py:385
  23.6 9.0 %collective-permute-start.8 = (bf16[144,512]{1,0:T(8,128)(2,1)S(1)}, bf16[144,512]{1,0:T(8,128)(2,1)S(1)}, u32[]{:S(2)}, u32[]{:S(2)}) collective-permute-start(bf16[144,512]{1,0:T(8,128)(2,1)S(1)} %fusion.1.refs_9_), channel_id=1, source_target_pairs={{0,224},{16,240},{32,0},{48,16},{64,32},{80,48},{96,64},{112,80},{... | collective-permute-start | bytes 442376 | tf_op jit(solution)/shard_map/ppermute | solution.py:36
  30.1 8.4 %collective-permute-start.12 = (bf16[144,512]{1,0:T(8,128)(2,1)S(1)}, bf16[144,512]{1,0:T(8,128)(2,1)S(1)}, u32[]{:S(2)}, u32[]{:S(2)}) collective-permute-start(bf16[144,512]{1,0:T(8,128)(2,1)S(1)} %fusion.1.refs_9_), channel_id=1, source_target_pairs={{0,32},{16,48},{32,64},{48,80},{64,96},{80,112},{96,128},{112,144}... | collective-permute-start | bytes 442376 | tf_op jit(solution)/shard_map/ppermute | solution.py:36
  36.0 7.8 %collective-permute-start.5 = (bf16[128,512]{1,0:T(8,128)(2,1)S(1)}, bf16[128,512]{1,0:T(8,128)(2,1)S(1)}, u32[]{:S(2)}, u32[]{:S(2)}) collective-permute-start(bf16[128,512]{1,0:T(8,128)(2,1)S(1)} %collective-permute-done.4.refs_8_), channel_id=1, source_target_pairs={{0,32},{16,48},{32,64},{48,80},{64,96},{80,112},{96,128},{112,144}... | collective-permute-start | bytes 393224 | tf_op jit(solution)/shard_map/ppermute | solution.py:36
  38.5 11.7 %collective-permute-start.13 = (bf16[144,512]{1,0:T(8,128)(2,1)S(1)}, bf16[144,512]{1,0:T(8,128)(2,1)S(1)}, u32[]{:S(2)}, u32[]{:S(2)}) collective-permute-start(bf16[144,512]{1,0:T(8,128)(2,1)S(1)} %collective-permute-done.12.refs_16_), channel_id=1, source_target_pairs={{0,32},{16,48},{32,64},{48,80},{64,96},{80,112},{96,128},{112,144}... | collective-permute-start | bytes 442376 | tf_op jit(solution)/shard_map/ppermute | solution.py:36
  38.5 11.8 %collective-permute-start.10 = (bf16[144,512]{1,0:T(8,128)(2,1)S(1)}, bf16[144,512]{1,0:T(8,128)(2,1)S(1)}, u32[]{:S(2)}, u32[]{:S(2)}) collective-permute-start(bf16[144,512]{1,0:T(8,128)(2,1)S(1)} %collective-permute-done.9.refs_11_), channel_id=1, source_target_pairs={{0,224},{16,240},{32,0},{48,16},{64,32},{80,48},{96,64},{112,80},{... | collective-permute-start | bytes 442376 | tf_op jit(solution)/shard_map/ppermute | solution.py:36
  41.2 6.1 %collective-permute-start.2 = (bf16[128,512]{1,0:T(8,128)(2,1)S(1)}, bf16[128,512]{1,0:T(8,128)(2,1)S(1)}, u32[]{:S(2)}, u32[]{:S(2)}) collective-permute-start(bf16[128,512]{1,0:T(8,128)(2,1)S(1)} %collective-permute-done.1.refs_2_), channel_id=1, source_target_pairs={{0,224},{16,240},{32,0},{48,16},{64,32},{80,48},{96,64},{112,80},{... | collective-permute-start | bytes 393224 | tf_op jit(solution)/shard_map/ppermute | solution.py:36
  43.8 6.4 %collective-permute-start.6 = (bf16[128,512]{1,0:T(8,128)(2,1)S(1)}, bf16[128,512]{1,0:T(8,128)(2,1)S(1)}, u32[]{:S(2)}, u32[]{:S(2)}) collective-permute-start(bf16[128,512]{1,0:T(8,128)(2,1)S(1)} %collective-permute-done.5.refs_7_), channel_id=1, source_target_pairs={{0,32},{16,48},{32,64},{48,80},{64,96},{80,112},{96,128},{112,144}... | collective-permute-start | bytes 393224 | tf_op jit(solution)/shard_map/ppermute | solution.py:36
  43.8 9.4 %collective-permute-start = (s32[15]{0:T(128)S(1)}, s32[15]{0:T(128)S(1)}, u32[]{:S(2)}, u32[]{:S(2)}) collective-permute-start(s32[15]{0:T(128)S(1)} %select_reduce_fusion), channel_id=1, source_target_pairs={{0,16},{16,0},{32,48},{48,32},{64,80},{80,64},{96,112},{112,96},{1... | collective-permute-start | bytes 188 | tf_op jit(solution)/shard_map/ppermute | solution.py:41
  50.2 7.0 %collective-permute-start.7 = (bf16[128,512]{1,0:T(8,128)(2,1)S(1)}, bf16[128,512]{1,0:T(8,128)(2,1)S(1)}, u32[]{:S(2)}, u32[]{:S(2)}) collective-permute-start(bf16[128,512]{1,0:T(8,128)(2,1)S(1)} %collective-permute-done.6.refs_6_), channel_id=1, source_target_pairs={{0,32},{16,48},{32,64},{48,80},{64,96},{80,112},{96,128},{112,144}... | collective-permute-start | bytes 393224 | tf_op jit(solution)/shard_map/ppermute | solution.py:36
  50.3 6.9 %collective-permute-start.11 = (bf16[144,512]{1,0:T(8,128)(2,1)S(1)}, bf16[144,512]{1,0:T(8,128)(2,1)S(1)}, u32[]{:S(2)}, u32[]{:S(2)}) collective-permute-start(bf16[144,512]{1,0:T(8,128)(2,1)S(1)} %collective-permute-done.10.refs_12_), channel_id=1, source_target_pairs={{0,224},{16,240},{32,0},{48,16},{64,32},{80,48},{96,64},{112,80},{... | collective-permute-start | bytes 442376 | tf_op jit(solution)/shard_map/ppermute | solution.py:36
  67.9 8.9 %collective-permute-start.18 = (bf16[14,32,128]{2,1,0:T(8,128)(2,1)S(1)}, bf16[14,32,128]{2,1,0:T(8,128)(2,1)S(1)}, u32[]{:S(2)}, u32[]{:S(2)}) collective-permute-start(bf16[14,32,128]{2,1,0:T(8,128)(2,1)S(1)} %get-tuple-element.22), channel_id=1, source_target_pairs={{0,2},{1,3},{2,0},{3,1},{4,6},{5,7},{6,4},{7,5},{8,10},{9,11},{10,... | collective-permute-start | bytes 344072 | tf_op jit(solution)/shard_map/ppermute | solution.py:50
  70.9 11.2 %collective-permute-start.17 = (bf16[14,32,128]{2,1,0:T(8,128)(2,1)S(1)}, bf16[14,32,128]{2,1,0:T(8,128)(2,1)S(1)}, u32[]{:S(2)}, u32[]{:S(2)}) collective-permute-start(bf16[14,32,128]{2,1,0:T(8,128)(2,1)S(1)} %get-tuple-element.22), channel_id=1, source_target_pairs={{0,3},{1,0},{2,1},{3,2},{4,7},{5,4},{6,5},{7,6},{8,11},{9,8},{10,9... | collective-permute-start | bytes 344072 | tf_op jit(solution)/shard_map/ppermute | solution.py:50
  71.7 10.4 %collective-permute-start.16 = (bf16[14,32,128]{2,1,0:T(8,128)(2,1)S(1)}, bf16[14,32,128]{2,1,0:T(8,128)(2,1)S(1)}, u32[]{:S(2)}, u32[]{:S(2)}) collective-permute-start(bf16[14,32,128]{2,1,0:T(8,128)(2,1)S(1)} %get-tuple-element.22), channel_id=1, source_target_pairs={{0,1},{1,2},{2,3},{3,0},{4,5},{5,6},{6,7},{7,4},{8,9},{9,10},{10,1... | collective-permute-start | bytes 344072 | tf_op jit(solution)/shard_map/ppermute | solution.py:50
  82.1 8.5 %collective-permute-start.21 = (bf16[14,32,128]{2,1,0:T(8,128)(2,1)S(1)}, bf16[14,32,128]{2,1,0:T(8,128)(2,1)S(1)}, u32[]{:S(2)}, u32[]{:S(2)}) collective-permute-start(bf16[14,32,128]{2,1,0:T(8,128)(2,1)S(1)} %add_convert_fusion.1), channel_id=1, source_target_pairs={{0,8},{1,9},{2,10},{3,11},{4,12},{5,13},{6,14},{7,15},{8,0},{9,1},... | collective-permute-start | bytes 344072 | tf_op jit(solution)/shard_map/ppermute | solution.py:50
  84.8 10.6 %collective-permute-start.20 = (bf16[14,32,128]{2,1,0:T(8,128)(2,1)S(1)}, bf16[14,32,128]{2,1,0:T(8,128)(2,1)S(1)}, u32[]{:S(2)}, u32[]{:S(2)}) collective-permute-start(bf16[14,32,128]{2,1,0:T(8,128)(2,1)S(1)} %add_convert_fusion.1), channel_id=1, source_target_pairs={{0,12},{1,13},{2,14},{3,15},{4,0},{5,1},{6,2},{7,3},{8,4},{9,5},{1... | collective-permute-start | bytes 344072 | tf_op jit(solution)/shard_map/ppermute | solution.py:50
  85.6 9.8 %collective-permute-start.19 = (bf16[14,32,128]{2,1,0:T(8,128)(2,1)S(1)}, bf16[14,32,128]{2,1,0:T(8,128)(2,1)S(1)}, u32[]{:S(2)}, u32[]{:S(2)}) collective-permute-start(bf16[14,32,128]{2,1,0:T(8,128)(2,1)S(1)} %add_convert_fusion.1), channel_id=1, source_target_pairs={{0,4},{1,5},{2,6},{3,7},{4,8},{5,9},{6,10},{7,11},{8,12},{9,13},{1... | collective-permute-start | bytes 344072 | tf_op jit(solution)/shard_map/ppermute | solution.py:50
  95.8 6.6 %collective-permute-start.23 = (bf16[7,32,512]{2,1,0:T(8,128)(2,1)S(1)}, bf16[7,32,512]{2,1,0:T(8,128)(2,1)S(1)}, u32[]{:S(2)}, u32[]{:S(2)}) collective-permute-start(bf16[7,32,512]{2,1,0:T(8,128)(2,1)S(1)} %get-tuple-element.27.refs_2_), channel_id=1, source_target_pairs={{0,32},{16,48},{32,64},{48,80},{64,96},{80,112},{96,128},{112,144}... | collective-permute-start | bytes 688136 | tf_op jit(solution)/shard_map/ppermute | solution.py:36
  95.9 6.5 %collective-permute-start.27 = (bf16[7,32,512]{2,1,0:T(8,128)(2,1)S(1)}, bf16[7,32,512]{2,1,0:T(8,128)(2,1)S(1)}, u32[]{:S(2)}, u32[]{:S(2)}) collective-permute-start(bf16[7,32,512]{2,1,0:T(8,128)(2,1)S(1)} %get-tuple-element.28.refs_9_), channel_id=1, source_target_pairs={{0,224},{16,240},{32,0},{48,16},{64,32},{80,48},{96,64},{112,80},{... | collective-permute-start | bytes 688136 | tf_op jit(solution)/shard_map/ppermute | solution.py:36
  98.7 7.7 %collective-permute-start.31 = (bf16[7,32,512]{2,1,0:T(8,128)(2,1)S(1)}, bf16[7,32,512]{2,1,0:T(8,128)(2,1)S(1)}, u32[]{:S(2)}, u32[]{:S(2)}) collective-permute-start(bf16[7,32,512]{2,1,0:T(8,128)(2,1)S(1)} %get-tuple-element.27.refs_2_), channel_id=1, source_target_pairs={{0,224},{16,240},{32,0},{48,16},{64,32},{80,48},{96,64},{112,80},{... | collective-permute-start | bytes 688136 | tf_op jit(solution)/shard_map/ppermute | solution.py:36
  99.6 9.8 %collective-permute-start.34 = (bf16[7,32,512]{2,1,0:T(8,128)(2,1)S(1)}, bf16[7,32,512]{2,1,0:T(8,128)(2,1)S(1)}, u32[]{:S(2)}, u32[]{:S(2)}) collective-permute-start(bf16[7,32,512]{2,1,0:T(8,128)(2,1)S(1)} %get-tuple-element.28.refs_9_), channel_id=1, source_target_pairs={{0,32},{16,48},{32,64},{48,80},{64,96},{80,112},{96,128},{112,144}... | collective-permute-start | bytes 688136 | tf_op jit(solution)/shard_map/ppermute | solution.py:36
  102.4 10.3 %collective-permute-start.24 = (bf16[7,32,512]{2,1,0:T(8,128)(2,1)S(1)}, bf16[7,32,512]{2,1,0:T(8,128)(2,1)S(1)}, u32[]{:S(2)}, u32[]{:S(2)}) collective-permute-start(bf16[7,32,512]{2,1,0:T(8,128)(2,1)S(1)} %collective-permute-done.23.refs_8_), channel_id=1, source_target_pairs={{0,32},{16,48},{32,64},{48,80},{64,96},{80,112},{96,128},{112,144}... | collective-permute-start | bytes 688136 | tf_op jit(solution)/shard_map/ppermute | solution.py:36
  102.4 10.3 %collective-permute-start.28 = (bf16[7,32,512]{2,1,0:T(8,128)(2,1)S(1)}, bf16[7,32,512]{2,1,0:T(8,128)(2,1)S(1)}, u32[]{:S(2)}, u32[]{:S(2)}) collective-permute-start(bf16[7,32,512]{2,1,0:T(8,128)(2,1)S(1)} %collective-permute-done.27.refs_10_), channel_id=1, source_target_pairs={{0,224},{16,240},{32,0},{48,16},{64,32},{80,48},{96,64},{112,80},{... | collective-permute-start | bytes 688136 | tf_op jit(solution)/shard_map/ppermute | solution.py:36
  106.5 9.8 %collective-permute-start.32 = (bf16[7,32,512]{2,1,0:T(8,128)(2,1)S(1)}, bf16[7,32,512]{2,1,0:T(8,128)(2,1)}, u32[]{:S(2)}, u32[]{:S(2)}) collective-permute-start(bf16[7,32,512]{2,1,0:T(8,128)(2,1)S(1)} %collective-permute-done.31.refs_3_), channel_id=1, source_target_pairs={{0,224},{16,240},{32,0},{48,16},{64,32},{80,48},{96,64},{112,80},{... | collective-permute-start | bytes 688136 | tf_op jit(solution)/shard_map/ppermute | solution.py:36
  109.4 9.7 %collective-permute-start.35 = (bf16[7,32,512]{2,1,0:T(8,128)(2,1)S(1)}, bf16[7,32,512]{2,1,0:T(8,128)(2,1)}, u32[]{:S(2)}, u32[]{:S(2)}) collective-permute-start(bf16[7,32,512]{2,1,0:T(8,128)(2,1)S(1)} %collective-permute-done.34.refs_15_), channel_id=1, source_target_pairs={{0,32},{16,48},{32,64},{48,80},{64,96},{80,112},{96,128},{112,144}... | collective-permute-start | bytes 688136 | tf_op jit(solution)/shard_map/ppermute | solution.py:36
  112.7 6.9 %collective-permute-start.25 = (bf16[7,32,512]{2,1,0:T(8,128)(2,1)S(1)}, bf16[7,32,512]{2,1,0:T(8,128)(2,1)}, u32[]{:S(2)}, u32[]{:S(2)}) collective-permute-start(bf16[7,32,512]{2,1,0:T(8,128)(2,1)S(1)} %collective-permute-done.24.refs_7_), channel_id=1, source_target_pairs={{0,32},{16,48},{32,64},{48,80},{64,96},{80,112},{96,128},{112,144}... | collective-permute-start | bytes 688136 | tf_op jit(solution)/shard_map/ppermute | solution.py:36
  112.7 8.6 %collective-permute-start.29 = (bf16[7,32,512]{2,1,0:T(8,128)(2,1)S(1)}, bf16[7,32,512]{2,1,0:T(8,128)(2,1)}, u32[]{:S(2)}, u32[]{:S(2)}) collective-permute-start(bf16[7,32,512]{2,1,0:T(8,128)(2,1)S(1)} %collective-permute-done.28.refs_11_), channel_id=1, source_target_pairs={{0,224},{16,240},{32,0},{48,16},{64,32},{80,48},{96,64},{112,80},{... | collective-permute-start | bytes 688136 | tf_op jit(solution)/shard_map/ppermute | solution.py:36
  116.3 9.8 %collective-permute-start.33 = (bf16[7,32,512]{2,1,0:T(8,128)(2,1)}, bf16[7,32,512]{2,1,0:T(8,128)(2,1)}, u32[]{:S(2)}, u32[]{:S(2)}) collective-permute-start(bf16[7,32,512]{2,1,0:T(8,128)(2,1)} %collective-permute-done.32.refs_4_), channel_id=1, source_target_pairs={{0,224},{16,240},{32,0},{48,16},{64,32},{80,48},{96,64},{112,80},{... | collective-permute-start | bytes 688136 | tf_op jit(solution)/shard_map/ppermute | solution.py:36
  119.1 8.8 %collective-permute-start.36 = (bf16[7,32,512]{2,1,0:T(8,128)(2,1)}, bf16[7,32,512]{2,1,0:T(8,128)(2,1)}, u32[]{:S(2)}, u32[]{:S(2)}) collective-permute-start(bf16[7,32,512]{2,1,0:T(8,128)(2,1)} %collective-permute-done.35.refs_14_), channel_id=1, source_target_pairs={{0,32},{16,48},{32,64},{48,80},{64,96},{80,112},{96,128},{112,144}... | collective-permute-start | bytes 688136 | tf_op jit(solution)/shard_map/ppermute | solution.py:36
  119.5 14.5 %collective-permute-start.26 = (bf16[7,32,512]{2,1,0:T(8,128)(2,1)}, bf16[7,32,512]{2,1,0:T(8,128)(2,1)S(1)}, u32[]{:S(2)}, u32[]{:S(2)}) collective-permute-start(bf16[7,32,512]{2,1,0:T(8,128)(2,1)} %collective-permute-done.25.refs_6_), channel_id=1, source_target_pairs={{0,32},{16,48},{32,64},{48,80},{64,96},{80,112},{96,128},{112,144}... | collective-permute-start | bytes 688136 | tf_op jit(solution)/shard_map/ppermute | solution.py:36
  121.2 12.8 %collective-permute-start.30 = (bf16[7,32,512]{2,1,0:T(8,128)(2,1)}, bf16[7,32,512]{2,1,0:T(8,128)(2,1)S(1)}, u32[]{:S(2)}, u32[]{:S(2)}) collective-permute-start(bf16[7,32,512]{2,1,0:T(8,128)(2,1)} %collective-permute-done.29.refs_12_), channel_id=1, source_target_pairs={{0,224},{16,240},{32,0},{48,16},{64,32},{80,48},{96,64},{112,80},{... | collective-permute-start | bytes 688136 | tf_op jit(solution)/shard_map/ppermute | solution.py:36
  134.9 8.4 %collective-permute-start.37 = (bf16[24,32,512]{2,1,0:T(8,128)(2,1)S(1)}, bf16[24,32,512]{2,1,0:T(8,128)(2,1)S(1)}, u32[]{:S(2)}, u32[]{:S(2)}) collective-permute-start(bf16[24,32,512]{2,1,0:T(8,128)(2,1)S(1)} %gradient_share.1), channel_id=1, source_target_pairs={{0,16},{16,0},{32,48},{48,32},{64,80},{80,64},{96,112},{112,96},{1... | collective-permute-start | bytes 2359304 | tf_op jit(solution)/shard_map/ppermute | solution.py:41
  (18 other events, 176.2 us)
Sparse Core Ops, SparseCore 0:
  22.8 118.8 reduce-scatter.1
where the time goes:
time: 155 us; the launch traced here: 154 us
  starting transfers between devices  62.7 us (40%)
  waiting for transfers between devices  43.3 us (28%)
  Pallas kernels  26.5 us (17%)
  between operations  14.3 us (9%)
  local copies, waits for them, and re-layouts  6.98 us (5%)
    ppermute x28, starting transfers between devices, z_hop(): return lax.ppermute(x, 'dp', perm)  41 us
    ppermute x28, waiting for transfers between devices, z_hop(): return lax.ppermute(x, 'dp', perm)  20.3 us
    ppermute x6, waiting for transfers between devices, plane_hop(): return lax.ppermute(x, 'tensor', perm)  18.8 us
    ppermute x4, starting transfers between devices, core_swap(): return lax.ppermute(x, 'dp', [(d, d ^ 1) for d in range(n)])  13.1 us
    pallas_call x1, Pallas kernels, frozen(): pl.pallas_call(frozen_kernel, grid=(columns // tile,), out_shape=jax.Shap...  10.8 us
    ppermute x6, starting transfers between devices, plane_hop(): return lax.ppermute(x, 'tensor', perm)  8.52 us
    unnamed x23, local copies, waits for them, and re-layouts  6.35 us
    pallas_call x1, Pallas kernels, total(): pl.pallas_call(functools.partial(total_kernel, needs), out_shape=(shape,...  6.11 us
  transfers between devices with their start and end apart: 39, of which 18 were waited for; matrix products, arithmetic and copies ran while one was open for 1% of the time, Pallas kernels for 9%

commit v1 on v0

--- a/solution.py
+++ b/solution.py
@@ -14,6 +14,8 @@
 CORES = 2
 SIDE = 4
 LEARN_RATE = 0.25
+TILE = 2048
+BASE_VMEM = 58 * 2**20
 SCALE = 1.0 / math.sqrt(INPUT_FEATURES * ADAPTER_RANK)
 
 BF = jnp.bfloat16
@@ -77,51 +79,58 @@
     return copies
 
 
-def select_kernel(blocks, rolls, slots, rank, *refs):
+def pick_kernel(rank, rows, within_mine, within_other, *refs):
+    a_refs, b_refs = refs[:8], refs[8:16]
+    mine_ref, other_ref, ids_ref = refs[16:]
+    for k in range(8):
+        for ref, within in ((mine_ref, within_mine), (other_ref, within_other)):
+            at = pl.ds(pl.multiple_of(within[k] * rank, rank), rank)
+            ref[k] = a_refs[k][at, :]
+            ref[8 + k] = b_refs[k][at, :]
+        ids_ref[k] = b_refs[k][rows:, : ids_ref.shape[2]]
+
+
+def pick(within_mine, within_other, parts_a, parts_b, rank):
+    rows, width = parts_a[0].shape
+    tall = parts_b[0].shape[0]
+    shape = jax.ShapeDtypeStruct((16, rank, width), BF)
+    return pl.pallas_call(
+        functools.partial(pick_kernel, rank, rows),
+        out_shape=(shape, shape, jax.ShapeDtypeStruct((8, tall - rows, 128), BF)),
+        in_specs=[SMEM()] * 2 + [VMEM()] * 16,
+        out_specs=(VMEM(),) * 3,
+        compiler_params=PARAMS,
+        cost_estimate=pl.CostEstimate(flops=0, bytes_accessed=6 * 2**20, transcendentals=0),
+        name="pick_factors",
+    )(within_mine, within_other, *parts_a, *parts_b)
+
+
+def rolls_kernel(rolls, slots, rank, *refs):
     place, refs = refs[0], refs[1:]
     a_refs, b_refs = refs[:8], refs[8:16]
-    mine_ref, other_ref, mine_roll, other_roll, ids_ref, hold_a, hold_b, sems = refs[16:]
+    mine_ref, other_ref, hold_a, hold_b, sems = refs[16:]
     copies = fetch(a_refs, hold_a, sems, 0) + fetch(b_refs, hold_b, sems, 8)
     for copy in copies:
         copy.wait()
-    need = blocks + rolls
     tail = b_refs[0].shape[0] - slots * rank
-
-    def from_a(at):
-        return hold_a[pl.ds(pl.multiple_of(place[at] * rank, rank), rank), :]
-
-    def from_b(at):
-        row = place[at] * rank + place[at] // slots * tail
-        return hold_b[pl.ds(pl.multiple_of(row, 16), rank), :]
-
-    for n in range(blocks):
-        mine_ref[n] = from_a(n)
-        mine_ref[blocks + n] = from_b(n)
-        other_ref[n] = from_a(need + n)
-        other_ref[blocks + n] = from_b(need + n)
-    for n in range(rolls):
-        mine_roll[n] = from_a(blocks + n)
-        mine_roll[rolls + n] = from_b(blocks + n)
-        other_roll[n] = from_a(need + blocks + n)
-        other_roll[rolls + n] = from_b(need + blocks + n)
-    for k in range(8):
-        row = k * (slots * rank + tail) + slots * rank
-        ids_ref[k] = hold_b[row : row + tail, : ids_ref.shape[2]]
-
-
-def select(place, parts_a, parts_b, blocks, rolls, slots):
+    for ref, first in ((mine_ref, 0), (other_ref, rolls)):
+        for n in range(rolls):
+            at = place[first + n]
+            ref[n] = hold_a[pl.ds(pl.multiple_of(at * rank, rank), rank), :]
+            row = at * rank + at // slots * tail
+            ref[rolls + n] = hold_b[pl.ds(pl.multiple_of(row, 16), rank), :]
+
+
+def pick_rolls(place, parts_a, parts_b, rolls, slots):
     rows, width = parts_a[0].shape
     rank = rows // slots
     tall = parts_b[0].shape[0]
-    shape = lambda n: jax.ShapeDtypeStruct((n, rank, width), BF)
-    return pl.pallas_call(
-        functools.partial(select_kernel, blocks, rolls, slots, rank),
-        out_shape=(
-            shape(2 * blocks), shape(2 * blocks), shape(2 * rolls), shape(2 * rolls),
-            jax.ShapeDtypeStruct((8, tall - rows, 128), BF),
-        ),
+    shape = jax.ShapeDtypeStruct((2 * rolls, rank, width), BF)
+    return pl.pallas_call(
+        functools.partial(rolls_kernel, rolls, slots, rank),
+        out_shape=(shape, shape),
         in_specs=[SMEM()] + [ANY()] * 16,
-        out_specs=(VMEM(),) * 5,
+        out_specs=(VMEM(),) * 2,
         scratch_shapes=[
             pltpu.VMEM((8 * rows, width), BF),
             pltpu.VMEM((8 * tall, width), BF),
@@ -129,72 +138,103 @@
         ],
         compiler_params=PARAMS,
         cost_estimate=pl.CostEstimate(flops=0, bytes_accessed=8 * 2**20, transcendentals=0),
-        name="select_factors",
+        name="pick_rollouts",
     )(place, *parts_a, *parts_b)
 
 
-def project_kernel(blocks, own_ref, mine_ref, other_ref, acts_ref, grad_ref, chosen_ref, out_ref):
+def project_kernel(
+    blocks, own_ref, near_ref, here_ref, mine_ref, other_ref, acts_ref, grad_ref,
+    chosen_ref, *refs,
+):
+    out_refs, hold = refs[:SIDE], refs[SIDE]
     for n in range(blocks):
         own = own_ref[n] == 1
+        at = near_ref[n]
         rows = pl.ds(n * BLOCK, BLOCK)
-        factor_a = jnp.where(own, mine_ref[n], other_ref[n])
-        factor_b = jnp.where(own, mine_ref[blocks + n], other_ref[blocks + n])
+        factor_a = jnp.where(own, mine_ref[at], other_ref[at])
+        factor_b = jnp.where(own, mine_ref[8 + at], other_ref[8 + at])
         chosen_ref[n] = factor_a
         contract = (((1,), (1,)), ((), ()))
-        out_ref[n] = lax.dot_general(
+        hold[n] = lax.dot_general(
             factor_b, grad_ref[rows, :], contract, preferred_element_type=F32
         ).astype(BF)
-        out_ref[blocks + n] = lax.dot_general(
+        hold[blocks + n] = lax.dot_general(
             factor_a, acts_ref[rows, :], contract, preferred_element_type=F32
         ).astype(BF)
-
-
-def project(own, mine, other, acts, grad):
-    blocks, (rank, width) = mine.shape[0] // 2, mine.shape[1:]
+    quarter = hold.shape[0] // SIDE
+    for n in range(2 * blocks, hold.shape[0]):
+        hold[n] = jnp.zeros(hold.shape[1:], BF)
+    for step, out_ref in enumerate(out_refs):
+        first = lax.rem(here_ref[0] + step, SIDE) * quarter
+        for k in range(quarter):
+            out_ref[k] = hold[first + k]
+
+
+def project(own, near, here, mine, other, acts, grad):
+    blocks, (rank, width) = acts.shape[0] // BLOCK, mine.shape[1:]
+    quarter = -(-2 * blocks // SIDE)
     return pl.pallas_call(
         functools.partial(project_kernel, blocks),
-        out_shape=(
-            jax.ShapeDtypeStruct((blocks, rank, width), BF),
-            jax.ShapeDtypeStruct((2 * blocks, rank, BLOCK), BF),
-        ),
-        in_specs=[SMEM()] + [VMEM()] * 4,
-        out_specs=(VMEM(),) * 2,
+        out_shape=(jax.ShapeDtypeStruct((blocks, rank, width), BF),)
+        + (jax.ShapeDtypeStruct((quarter, rank, BLOCK), BF),) * SIDE,
+        in_specs=[SMEM()] * 3 + [VMEM()] * 4,
+        out_specs=(VMEM(),) * (1 + SIDE),
+        scratch_shapes=[pltpu.VMEM((SIDE * quarter, rank, BLOCK), BF)],
         compiler_params=PARAMS,
         cost_estimate=pl.CostEstimate(flops=0, bytes_accessed=8 * 2**20, transcendentals=0),
         name="project_ranks",
-    )(own, mine, other, acts, grad)
-
-
-def plane_sum(x):
-    for axis in ("y", "x"):
-        terms = [x] + [plane_hop(x, step, axis) for step in (1, 3, 2)]
-        x = sum(term.astype(F32) for term in terms).astype(BF)
-    return x
-
-
-def contribute_kernel(blocks, ranks_ref, acts_ref, grad_ref, a_ref, b_ref):
+    )(own, near, here, mine, other, acts, grad)
+
+
+def sum_kernel(terms, *refs):
+    out_ref = refs[-1]
+    out_ref[...] = sum(ref[...].astype(F32) for ref in refs[:terms]).astype(BF)
+
+
+def sum_after(token, terms):
+    return pl.pallas_call(
+        functools.partial(sum_kernel, len(terms)),
+        out_shape=jax.ShapeDtypeStruct(terms[0].shape, BF),
+        in_specs=[VMEM()] * len(terms) + [ANY()],
+        out_specs=VMEM(),
+        compiler_params=PARAMS,
+        cost_estimate=pl.CostEstimate(flops=0, bytes_accessed=2**20, transcendentals=0),
+        name="rank_sum",
+    )(*terms, token)
+
+
+def contribute_kernel(blocks, here_ref, *refs):
+    parts, (acts_ref, grad_ref, ranks_ref, a_ref, b_ref, hold) = refs[:SIDE], refs[SIDE:]
+    quarter = parts[0].shape[0]
+    for step, part in enumerate(parts):
+        first = lax.rem(here_ref[0] + SIDE - step, SIDE) * quarter
+        for k in range(quarter):
+            hold[first + k] = part[k]
     for n in range(blocks):
         rows = pl.ds(n * BLOCK, BLOCK)
+        ranks_ref[n] = hold[n]
         a_ref[n] = (
-            SCALE * jnp.dot(ranks_ref[n], acts_ref[rows, :], preferred_element_type=F32)
+            SCALE * jnp.dot(hold[n], acts_ref[rows, :], preferred_element_type=F32)
         ).astype(BF)
         b_ref[n] = (
-            SCALE * jnp.dot(ranks_ref[blocks + n], grad_ref[rows, :], preferred_element_type=F32)
+            SCALE * jnp.dot(hold[blocks + n], grad_ref[rows, :], preferred_element_type=F32)
         ).astype(BF)
 
 
-def contribute(ranks, acts, grad):
-    blocks, rank, width = ranks.shape[0] // 2, ranks.shape[1], acts.shape[1]
+def contribute(here, parts, acts, grad):
+    blocks, width = acts.shape[0] // BLOCK, acts.shape[1]
+    quarter, rank = parts[0].shape[:2]
     shape = jax.ShapeDtypeStruct((blocks, rank, width), BF)
     return pl.pallas_call(
         functools.partial(contribute_kernel, blocks),
-        out_shape=(shape, shape),
-        in_specs=[VMEM()] * 3,
-        out_specs=(VMEM(),) * 2,
+        out_shape=(jax.ShapeDtypeStruct((blocks, rank, BLOCK), BF), shape, shape),
+        in_specs=[SMEM()] + [VMEM()] * (2 + SIDE),
+        out_specs=(VMEM(),) * 3,
+        scratch_shapes=[pltpu.VMEM((SIDE * quarter, rank, BLOCK), BF)],
         compiler_params=PARAMS,
         cost_estimate=pl.CostEstimate(flops=0, bytes_accessed=8 * 2**20, transcendentals=0),
         name="factor_contributions",
-    )(ranks, acts, grad)
+    )(here, *parts, acts, grad)
 
 
 def total_kernel(needs, *refs):
@@ -309,29 +349,34 @@
     )(place, used, own, factor_a, factor_b, mine_roll, other_roll, far_a, far_b, mine, other)
 
 
-def frozen_kernel(grad_ref, weight_ref, out_ref):
-    out_ref[...] = lax.dot_general(
-        grad_ref[...], weight_ref[...], (((1,), (1,)), ((), ())), preferred_element_type=F32
-    ).astype(BF)
-
-
-def frozen(grad, weight):
+def product(grad, weight):
+    return lax.dot_general(grad, weight, (((1,), (1,)), ((), ())), preferred_element_type=F32)
+
+
+def products_kernel(grad_ref, weight_ref, out_ref):
+    value = product(grad_ref[...], weight_ref[...]).astype(BF)
+    width = out_ref.shape[2]
+    for k in range(out_ref.shape[0]):
+        out_ref[k] = value[:, k * width : (k + 1) * width]
+
+
+def products(grad, weight, blocks):
     (rows, depth), columns = grad.shape, weight.shape[0]
-    tile = 1024
-    return pl.pallas_call(
-        frozen_kernel,
+    width, tile = columns // blocks, TILE
+    return pl.pallas_call(
+        products_kernel,
         grid=(columns // tile,),
-        out_shape=jax.ShapeDtypeStruct((rows, columns), BF),
+        out_shape=jax.ShapeDtypeStruct((blocks, rows, width), BF),
         in_specs=[
             pl.BlockSpec((rows, depth), lambda j: (0, 0)),
             pl.BlockSpec((tile, depth), lambda j: (j, 0)),
         ],
-        out_specs=pl.BlockSpec((rows, tile), lambda j: (0, j)),
-        compiler_params=PARAMS,
+        out_specs=pl.BlockSpec((tile // width, rows, width), lambda j: (j, 0, 0)),
+        compiler_params=pltpu.CompilerParams(vmem_limit_bytes=BASE_VMEM),
         cost_estimate=pl.CostEstimate(
             flops=2 * rows * depth * columns, bytes_accessed=24 * 2**20, transcendentals=0
         ),
-        name="frozen_partial",
+        name="base_products",
     )(grad, weight)
 
 
@@ -341,14 +386,14 @@
         term = lax.dot_general(
             ranks_ref[n], chosen_ref[n], (((0,), (0,)), ((), ())), preferred_element_type=F32
         )
-        out_ref[rows, :] = (base_ref[rows, :].astype(F32) + SCALE * term).astype(BF)
+        out_ref[rows, :] = (base_ref[0, rows, :].astype(F32) + SCALE * term).astype(BF)
 
 
 def finish(ranks, chosen, base):
     blocks = chosen.shape[0]
     return pl.pallas_call(
         functools.partial(finish_kernel, blocks),
-        out_shape=jax.ShapeDtypeStruct(base.shape, BF),
+        out_shape=jax.ShapeDtypeStruct(base.shape[1:], BF),
         in_specs=[VMEM()] * 3,
         out_specs=VMEM(),
         compiler_params=PARAMS,
@@ -379,23 +424,51 @@
         return jnp.where(here, distance * slots + slot_ids % slots, 0), here.astype(jnp.int32)
 
     mine_place, mine_own = places(wanted)
-    other_place, _ = places(other_wanted)
-
-    partial_value = frozen(out_grad, base_weight)
-    base = lax.psum_scatter(partial_value, "tensor", scatter_dimension=1, tiled=True)
+    other_place, other_own = places(other_wanted)
+
+    def one_each(slot_ids, here):
+        distance = (slot_ids // slots // CORES - chip + chips) % chips
+        hit = (distance[None] == jnp.arange(chips, dtype=jnp.int32)[:, None]) & (here[None] == 1)
+        return jnp.sum(jnp.where(hit, slot_ids[None] % slots, 0), axis=1)
+
+    mine_within = one_each(wanted[:blocks], mine_own[:blocks])
+    other_within = one_each(other_wanted[:blocks], other_own[:blocks])
+    mine_near = (wanted[:blocks] // slots // CORES - chip + chips) % chips
+
+    partial_value = products(out_grad, base_weight, lax.axis_size("tensor"))
+    base = lax.psum_scatter(partial_value, "tensor", scatter_dimension=0, tiled=True)
 
     width = factor_a.shape[2]
     ids = jnp.pad(wanted[None].astype(BF), ((0, 15), (0, width - blocks - rolls)))
     parts_a, parts_b = ring_gather(
         factor_a.reshape(-1, width), jnp.concatenate([factor_b.reshape(-1, width), ids])
     )
-    mine_sel, other_sel, mine_roll, other_roll, ring_ids = select(
-        jnp.concatenate([mine_place, other_place]), parts_a, parts_b, blocks, rolls, slots
+    mine_sel, other_sel, ring_ids = pick(
+        mine_within, other_within, parts_a, parts_b, factor_a.shape[1]
     )
     got_sel = core_swap(other_sel)
+    here = (lax.axis_index("tensor") % SIDE).reshape(1)
+    chosen_a, *rank_parts = project(
+        mine_own[:blocks], mine_near, here, mine_sel, got_sel, input_acts, out_grad
+    )
+    mine_roll, other_roll = pick_rolls(
+        jnp.concatenate([mine_place[blocks:], other_place[blocks:]]),
+        parts_a, parts_b, rolls, slots,
+    )
     got_roll = core_swap(other_roll)
-    chosen_a, rank_parts = project(mine_own[:blocks], mine_sel, got_sel, input_acts, out_grad)
-    ranks = plane_sum(rank_parts)
+    quarter = sum_after(
+        mine_roll,
+        [rank_parts[0]] + [plane_hop(rank_parts[step], step, "y") for step in range(1, SIDE)],
+    )
+    quarter = sum(
+        term.astype(F32)
+        for term in [quarter] + [plane_hop(quarter, step, "x") for step in range(1, SIDE)]
+    ).astype(BF)
+    ranks, part_a, part_b = contribute(
+        here,
+        [quarter] + [plane_hop(quarter, step, "y") for step in range(1, SIDE)],
+        input_acts, out_grad,
+    )
 
     order = [0, 1, 2, 3, 5, 6, 7, 4]
     ring = ring_ids[:, 0, :blocks].astype(jnp.int32)
@@ -410,7 +483,6 @@
     source = jnp.arange(chips, dtype=jnp.int32)[None, :] * blocks + at_block
     source, used = source.reshape(-1), used.reshape(-1)
 
-    part_a, part_b = contribute(ranks, input_acts, out_grad)
     parts_a, parts_b = ring_gather(part_a, part_b)
     near = order[:7]
     mine_total, other_total = total(

time: 155 us -> 159 us (1.026)
  waiting for transfers between devices: 43.3 us -> 32.2 us
  local copies, waits for them, and re-layouts: 6.98 us -> 14.8 us
  Pallas kernels: 26.5 us -> 30.8 us
  starting transfers between devices: 62.7 us -> 65.6 us
    ppermute x6 -> x9, waiting for transfers between devices: 18.8 us -> 9.09 us  [plane_hop(): return lax.ppermute(x, 'tensor', perm)]
    unnamed x23 -> x69, local copies, waits for them, and re-layouts: 6.35 us -> 12.8 us
    pallas_call x3 -> x5, Pallas kernels: 15.1 us -> 18.6 us  [the longest x1 13.1 us: products(): pl.pallas_call(products_kernel, grid=(columns // tile,), out_shape=jax.Sh...]
    ppermute x6 -> x9, starting transfers between devices: 8.52 us -> 11.2 us  [plane_hop(): return lax.ppermute(x, 'tensor', perm)]
  transfers between devices with their start and end apart: 39 -> 42, of which waited for: 18 -> 19; matrix products, arithmetic and copies ran while one was open for 1% -> 2% of each run, Pallas kernels for 9% -> 10%
where the time goes in v1:
time: 159 us
  starting transfers between devices  65.6 us (41%)
  waiting for transfers between devices  32.2 us (20%)
  Pallas kernels  30.8 us (19%)
  local copies, waits for them, and re-layouts  14.8 us (9%)
  between operations  14.5 us (9%)
    ppermute x28, starting transfers between devices, z_hop(): return lax.ppermute(x, 'dp', perm)  42.3 us
    ppermute x28, waiting for transfers between devices, z_hop(): return lax.ppermute(x, 'dp', perm)  18.7 us
    pallas_call x1, Pallas kernels, products(): pl.pallas_call(products_kernel, grid=(columns // tile,), out_shape=jax.Sh...  13.1 us
    unnamed x69, local copies, waits for them, and re-layouts  12.8 us
    ppermute x4, starting transfers between devices, core_swap(): return lax.ppermute(x, 'dp', [(d, d ^ 1) for d in range(n)])  12 us
    ppermute x9, starting transfers between devices, plane_hop(): return lax.ppermute(x, 'tensor', perm)  11.2 us
    ppermute x9, waiting for transfers between devices, plane_hop(): return lax.ppermute(x, 'tensor', perm)  9.09 us
    pallas_call x1, Pallas kernels, total(): pl.pallas_call(functools.partial(total_kernel, needs), out_shape=(shape,...  6.38 us
  transfers between devices with their start and end apart: 42, of which 19 were waited for; matrix products, arithmetic and copies ran while one was open for 2% of the time, Pallas kernels for 10%

profile of v1, /device:TPU:1, one launch (start us, length us, event | category | flops | bytes accessed | tf_op | source)
XLA Modules:
  0.0 158.9 jit_solution(279276513591773627)
XLA Ops:
  7.2 13.1 %base_products.1 = bf16[16,896,512]{2,1,0:T(8,128)(2,1)} custom-call(bf16[896,512]{1,0:T(8,128)(2,1)} %grad_ref.3, bf16[8192,512]{1,0:T(8,128)(2,1)} %weight_ref.1), custom_call_target="tpu_custom_call" | custom-call | flops 7516192768 | bytes 25165824 | tf_op jit(solution)/shard_map/base_products/pallas_call | solution.py:366
  21.2 2.5 %collective-permute-start.4 = (bf16[128,512]{1,0:T(8,128)(2,1)S(1)}, bf16[128,512]{1,0:T(8,128)(2,1)S(1)}, u32[]{:S(2)}, u32[]{:S(2)}) collective-permute-start(bf16[128,512]{1,0:T(8,128)(2,1)S(1)} %bitcast.14), channel_id=1, source_target_pairs={{0,32},{16,48},{32,64},{48,80},{64,96},{80,112},{96,128},{112,144}... | collective-permute-start | bytes 393224 | tf_op jit(solution)/shard_map/ppermute | solution.py:38
  23.6 3.9 %collective-permute-start.1 = (bf16[128,512]{1,0:T(8,128)(2,1)S(1)}, bf16[128,512]{1,0:T(8,128)(2,1)S(1)}, u32[]{:S(2)}, u32[]{:S(2)}) collective-permute-start(bf16[128,512]{1,0:T(8,128)(2,1)S(1)} %bitcast.15), channel_id=1, source_target_pairs={{0,224},{16,240},{32,0},{48,16},{64,32},{80,48},{96,64},{112,80},{... | collective-permute-start | bytes 393224 | tf_op jit(solution)/shard_map/ppermute | solution.py:38
  29.0 2.7 %collective-permute-start.8 = (bf16[144,512]{1,0:T(8,128)(2,1)S(1)}, bf16[144,512]{1,0:T(8,128)(2,1)S(1)}, u32[]{:S(2)}, u32[]{:S(2)}) collective-permute-start(bf16[144,512]{1,0:T(8,128)(2,1)S(1)} %fusion.1.refs_8_.refs_9_), channel_id=1, source_target_pairs={{0,224},{16,240},{32,0},{48,16},{64,32},{80,48},{96,64},{112,80},{... | collective-permute-start | bytes 442376 | tf_op jit(solution)/shard_map/ppermute | solution.py:38
  32.1 2.6 %collective-permute-done.8.refs_9_.refs_10_ = bf16[144,512]{1,0:T(8,128)(2,1)S(1)} collective-permute-done((bf16[144,512]{1,0:T(8,128)(2,1)S(1)}, bf16[144,512]{1,0:T(8,128)(2,1)S(1)}, u32[]{:S(2)}, u32[]{:S(2)}) %collective-permute-start.8) | collective-permute-done | bytes 147488 | tf_op jit(solution)/shard_map/ppermute | solution.py:38
  34.6 3.4 %collective-permute-start.9 = (bf16[144,512]{1,0:T(8,128)(2,1)S(1)}, bf16[144,512]{1,0:T(8,128)(2,1)S(1)}, u32[]{:S(2)}, u32[]{:S(2)}) collective-permute-start(bf16[144,512]{1,0:T(8,128)(2,1)S(1)} %collective-permute-done.8.refs_9_.refs_10_), channel_id=1, source_target_pairs={{0,224},{16,240},{32,0},{48,16},{64,32},{80,48},{96,64},{112,80},{... | collective-permute-start | bytes 442376 | tf_op jit(solution)/shard_map/ppermute | solution.py:38
  40.1 3.5 %collective-permute-start.10 = (bf16[144,512]{1,0:T(8,128)(2,1)S(1)}, bf16[144,512]{1,0:T(8,128)(2,1)S(1)}, u32[]{:S(2)}, u32[]{:S(2)}) collective-permute-start(bf16[144,512]{1,0:T(8,128)(2,1)S(1)} %collective-permute-done.9.refs_10_.refs_11_), channel_id=1, source_target_pairs={{0,224},{16,240},{32,0},{48,16},{64,32},{80,48},{96,64},{112,80},{... | collective-permute-start | bytes 442376 | tf_op jit(solution)/shard_map/ppermute | solution.py:38
  43.7 2.7 %collective-permute-start.3 = (bf16[128,512]{1,0:T(8,128)(2,1)S(1)}, bf16[128,512]{1,0:T(8,128)(2,1)S(1)}, u32[]{:S(2)}, u32[]{:S(2)}) collective-permute-start(bf16[128,512]{1,0:T(8,128)(2,1)S(1)} %collective-permute-done.2.refs_2_.refs_3_), channel_id=1, source_target_pairs={{0,224},{16,240},{32,0},{48,16},{64,32},{80,48},{96,64},{112,80},{... | collective-permute-start | bytes 393224 | tf_op jit(solution)/shard_map/ppermute | solution.py:38
  46.7 2.9 %collective-permute-start.11 = (bf16[144,512]{1,0:T(8,128)(2,1)S(1)}, bf16[144,512]{1,0:T(8,128)(2,1)S(1)}, u32[]{:S(2)}, u32[]{:S(2)}) collective-permute-start(bf16[144,512]{1,0:T(8,128)(2,1)S(1)} %collective-permute-done.10.refs_11_.refs_12_), channel_id=1, source_target_pairs={{0,224},{16,240},{32,0},{48,16},{64,32},{80,48},{96,64},{112,80},{... | collective-permute-start | bytes 442376 | tf_op jit(solution)/shard_map/ppermute | solution.py:38
  49.8 2.2 %collective-permute-done.14.refs_13_.refs_14_ = bf16[144,512]{1,0:T(8,128)(2,1)S(1)} collective-permute-done((bf16[144,512]{1,0:T(8,128)(2,1)S(1)}, bf16[144,512]{1,0:T(8,128)(2,1)S(1)}, u32[]{:S(2)}, u32[]{:S(2)}) %collective-permute-start.14) | collective-permute-done | bytes 147488 | tf_op jit(solution)/shard_map/ppermute | solution.py:38
  56.3 3.4 %collective-permute-start.15 = (bf16[16,32,512]{2,1,0:T(8,128)(2,1)}, bf16[16,32,512]{2,1,0:T(8,128)(2,1)}, u32[]{:S(2)}, u32[]{:S(2)}) collective-permute-start(bf16[16,32,512]{2,1,0:T(8,128)(2,1)} %get-tuple-element.25), channel_id=1, source_target_pairs={{0,16},{16,0},{32,48},{48,32},{64,80},{80,64},{96,112},{112,96},{1... | collective-permute-start | bytes 1572872 | tf_op jit(solution)/shard_map/ppermute | solution.py:43
  59.8 1.7 %collective-permute-done.15.other_ref = bf16[16,32,512]{2,1,0:T(8,128)(2,1)} collective-permute-done((bf16[16,32,512]{2,1,0:T(8,128)(2,1)}, bf16[16,32,512]{2,1,0:T(8,128)(2,1)}, u32[]{:S(2)}, u32[]{:S(2)}) %collective-permute-start.15) | collective-permute-done | bytes 524320 | tf_op jit(solution)/shard_map/ppermute | solution.py:43
  62.6 1.8 %project_ranks.1 = (bf16[7,32,512]{2,1,0:T(8,128)(2,1)S(1)}, bf16[4,32,128]{2,1,0:T(8,128)(2,1)S(1)}, bf16[4,32,128]{2,1,0:T(8,128)(2,1)S(1)}, bf16[4,32,128]{2,1,0:T(8,128)(2,1)S(1)}, bf16[4,32,128]{2,1,0:T(8,128)(2,1)S(1)}) custom-call(s32[7]{0:T(128)S(1)} %bitcast.19, s32[7]{0:T(128)S(1)} %and_select_fusion.13.near_ref, s32[1]{0:T(128)} %bitcast.here_ref, ...), custom_call_target="tpu_custom_call" | custom-call | bytes 8388608 | tf_op jit(solution)/shard_map/project_ranks/pallas_call | solution.py:176
  65.7 2.6 %collective-permute-start.17 = (bf16[4,32,128]{2,1,0:T(8,128)(2,1)S(1)}, bf16[4,32,128]{2,1,0:T(8,128)(2,1)S(1)}, u32[]{:S(2)}, u32[]{:S(2)}) collective-permute-start(bf16[4,32,128]{2,1,0:T(8,128)(2,1)S(1)} %get-tuple-element.28), channel_id=1, source_target_pairs={{0,2},{1,3},{2,0},{3,1},{4,6},{5,7},{6,4},{7,5},{8,10},{9,11},{10,... | collective-permute-start | bytes 98312 | tf_op jit(solution)/shard_map/ppermute | solution.py:52
  76.8 3.7 %pick_rollouts.1 = (bf16[16,32,512]{2,1,0:T(8,128)(2,1)S(1)}, bf16[16,32,512]{2,1,0:T(8,128)(2,1)S(1)}) custom-call(s32[16]{0:T(128)S(1)} %pad_add_fusion.2.refs_0_, bf16[128,512]{1,0:T(8,128)(2,1)S(1)} %bitcast.17, bf16[128,512]{1,0:T(8,128)(2,1)S(1)} %copy-done.9, bf16[128,512]{1,0:T(8,128)(2,1)S(1)} %copy-done.13, bf16[128,512]{1,0:T(8,128)(2,1)S(1)} %copy-done.17, ...), custom_call_target="tpu_custom_call" | custom-call | bytes 8388608 | tf_op jit(solution)/shard_map/pick_rollouts/pallas_call | solution.py:129
  80.7 2.5 %collective-permute-start.21 = (bf16[4,32,128]{2,1,0:T(8,128)(2,1)S(1)}, bf16[4,32,128]{2,1,0:T(8,128)(2,1)S(1)}, u32[]{:S(2)}, u32[]{:S(2)}) collective-permute-start(bf16[4,32,128]{2,1,0:T(8,128)(2,1)S(1)} %rank_sum.1), channel_id=1, source_target_pairs={{0,12},{1,13},{2,14},{3,15},{4,0},{5,1},{6,2},{7,3},{8,4},{9,5},{1... | collective-permute-start | bytes 98312 | tf_op jit(solution)/shard_map/ppermute | solution.py:52
  84.8 3.1 %collective-permute-done.20 = bf16[4,32,128]{2,1,0:T(8,128)(2,1)S(1)} collective-permute-done((bf16[4,32,128]{2,1,0:T(8,128)(2,1)S(1)}, bf16[4,32,128]{2,1,0:T(8,128)(2,1)S(1)}, u32[]{:S(2)}, u32[]{:S(2)}) %collective-permute-start.20) | collective-permute-done | bytes 32800 | tf_op jit(solution)/shard_map/ppermute | solution.py:52
  89.2 1.8 %collective-permute-start.23 = (bf16[4,32,128]{2,1,0:T(8,128)(2,1)S(1)}, bf16[4,32,128]{2,1,0:T(8,128)(2,1)S(1)}, u32[]{:S(2)}, u32[]{:S(2)}) collective-permute-start(bf16[4,32,128]{2,1,0:T(8,128)(2,1)S(1)} %add_convert_fusion.refs_0_), channel_id=1, source_target_pairs={{0,2},{1,3},{2,0},{3,1},{4,6},{5,7},{6,4},{7,5},{8,10},{9,11},{10,... | collective-permute-start | bytes 98312 | tf_op jit(solution)/shard_map/ppermute | solution.py:52
  93.8 2.1 %collective-permute-done.22.refs_1_ = bf16[4,32,128]{2,1,0:T(8,128)(2,1)S(1)} collective-permute-done((bf16[4,32,128]{2,1,0:T(8,128)(2,1)S(1)}, bf16[4,32,128]{2,1,0:T(8,128)(2,1)S(1)}, u32[]{:S(2)}, u32[]{:S(2)}) %collective-permute-start.22) | collective-permute-done | bytes 32800 | tf_op jit(solution)/shard_map/ppermute | solution.py:52
  96.4 1.9 %collective-permute-start.26 = (bf16[7,32,512]{2,1,0:T(8,128)(2,1)S(1)}, bf16[7,32,512]{2,1,0:T(8,128)(2,1)S(1)}, u32[]{:S(2)}, u32[]{:S(2)}) collective-permute-start(bf16[7,32,512]{2,1,0:T(8,128)(2,1)S(1)} %get-tuple-element.35.refs_2_), channel_id=1, source_target_pairs={{0,32},{16,48},{32,64},{48,80},{64,96},{80,112},{96,128},{112,144}... | collective-permute-start | bytes 688136 | tf_op jit(solution)/shard_map/ppermute | solution.py:38
  98.3 1.9 %collective-permute-start.30 = (bf16[7,32,512]{2,1,0:T(8,128)(2,1)S(1)}, bf16[7,32,512]{2,1,0:T(8,128)(2,1)S(1)}, u32[]{:S(2)}, u32[]{:S(2)}) collective-permute-start(bf16[7,32,512]{2,1,0:T(8,128)(2,1)S(1)} %get-tuple-element.36.refs_9_), channel_id=1, source_target_pairs={{0,224},{16,240},{32,0},{48,16},{64,32},{80,48},{96,64},{112,80},{... | collective-permute-start | bytes 688136 | tf_op jit(solution)/shard_map/ppermute | solution.py:38
  103.8 2.4 %collective-permute-start.31 = (bf16[7,32,512]{2,1,0:T(8,128)(2,1)S(1)}, bf16[7,32,512]{2,1,0:T(8,128)(2,1)S(1)}, u32[]{:S(2)}, u32[]{:S(2)}) collective-permute-start(bf16[7,32,512]{2,1,0:T(8,128)(2,1)S(1)} %collective-permute-done.30.refs_10_), channel_id=1, source_target_pairs={{0,224},{16,240},{32,0},{48,16},{64,32},{80,48},{96,64},{112,80},{... | collective-permute-start | bytes 688136 | tf_op jit(solution)/shard_map/ppermute | solution.py:38
  107.6 2.4 %collective-permute-start.35 = (bf16[7,32,512]{2,1,0:T(8,128)(2,1)S(1)}, bf16[7,32,512]{2,1,0:T(8,128)(2,1)S(1)}, u32[]{:S(2)}, u32[]{:S(2)}) collective-permute-start(bf16[7,32,512]{2,1,0:T(8,128)(2,1)S(1)} %collective-permute-done.34.refs_3_), channel_id=1, source_target_pairs={{0,224},{16,240},{32,0},{48,16},{64,32},{80,48},{96,64},{112,80},{... | collective-permute-start | bytes 688136 | tf_op jit(solution)/shard_map/ppermute | solution.py:38
  110.5 3.1 %collective-permute-done.27.refs_7_ = bf16[7,32,512]{2,1,0:T(8,128)(2,1)S(1)} collective-permute-done((bf16[7,32,512]{2,1,0:T(8,128)(2,1)S(1)}, bf16[7,32,512]{2,1,0:T(8,128)(2,1)S(1)}, u32[]{:S(2)}, u32[]{:S(2)}) %collective-permute-start.27) | collective-permute-done | bytes 229408 | tf_op jit(solution)/shard_map/ppermute | solution.py:38
  117.5 2.5 %collective-permute-start.36 = (bf16[7,32,512]{2,1,0:T(8,128)(2,1)S(1)}, bf16[7,32,512]{2,1,0:T(8,128)(2,1)}, u32[]{:S(2)}, u32[]{:S(2)}) collective-permute-start(bf16[7,32,512]{2,1,0:T(8,128)(2,1)S(1)} %collective-permute-done.35.refs_4_), channel_id=1, source_target_pairs={{0,224},{16,240},{32,0},{48,16},{64,32},{80,48},{96,64},{112,80},{... | collective-permute-start | bytes 688136 | tf_op jit(solution)/shard_map/ppermute | solution.py:38
  120.0 2.5 %collective-permute-done.28.refs_6_ = bf16[7,32,512]{2,1,0:T(8,128)(2,1)} collective-permute-done((bf16[7,32,512]{2,1,0:T(8,128)(2,1)S(1)}, bf16[7,32,512]{2,1,0:T(8,128)(2,1)}, u32[]{:S(2)}, u32[]{:S(2)}) %collective-permute-start.28) | collective-permute-done | bytes 229408 | tf_op jit(solution)/shard_map/ppermute | solution.py:38
  123.7 1.5 collective-permute-start.33
  125.7 1.9 %collective-permute-done.36.refs_5_ = bf16[7,32,512]{2,1,0:T(8,128)(2,1)} collective-permute-done((bf16[7,32,512]{2,1,0:T(8,128)(2,1)S(1)}, bf16[7,32,512]{2,1,0:T(8,128)(2,1)}, u32[]{:S(2)}, u32[]{:S(2)}) %collective-permute-start.36) | collective-permute-done | bytes 229408 | tf_op jit(solution)/shard_map/ppermute | solution.py:38
  129.2 6.4 %gradient_totals.1 = (f32[24,32,512]{2,1,0:T(8,128)S(1)}, f32[24,32,512]{2,1,0:T(8,128)S(1)}) custom-call(s32[192]{0:T(256)S(1)} %add.149.refs_0_.place, s32[192]{0:T(256)S(1)} %reshape.75.refs_1_.used, bf16[7,32,512]{2,1,0:T(8,128)(2,1)S(1)} %get-tuple-element.35.refs_2_, bf16[7,32,512]{2,1,0:T(8,128)(2,1)S(1)} %collective-permute-done.34.refs_3_, ...), custom_call_target="tpu_custom_call" | custom-call | bytes 16777216 | tf_op jit(solution)/shard_map/gradient_totals/pallas_call | solution.py:269
  136.4 7.5 %collective-permute-start.40 = (bf16[24,32,512]{2,1,0:T(8,128)(2,1)S(1)}, bf16[24,32,512]{2,1,0:T(8,128)(2,1)S(1)}, u32[]{:S(2)}, u32[]{:S(2)}) collective-permute-start(bf16[24,32,512]{2,1,0:T(8,128)(2,1)S(1)} %gradient_share.1), channel_id=1, source_target_pairs={{0,16},{16,0},{32,48},{48,32},{64,80},{80,64},{96,112},{112,96},{1... | collective-permute-start | bytes 2359304 | tf_op jit(solution)/shard_map/ppermute | solution.py:43
  144.1 2.7 %collective-permute-done.25.other_roll = bf16[16,32,512]{2,1,0:T(8,128)(2,1)S(1)} collective-permute-done((bf16[16,32,512]{2,1,0:T(8,128)(2,1)}, bf16[16,32,512]{2,1,0:T(8,128)(2,1)S(1)}, u32[]{:S(2)}, u32[]{:S(2)}) %collective-permute-start.25) | collective-permute-done | bytes 524320 | tf_op jit(solution)/shard_map/ppermute | solution.py:43
  147.7 1.8 %update_factors.1 = (bf16[4,32,512]{2,1,0:T(8,128)(2,1)}, bf16[4,32,512]{2,1,0:T(8,128)(2,1)}, bf16[8,32,512]{2,1,0:T(8,128)(2,1)}, bf16[8,32,512]{2,1,0:T(8,128)(2,1)}) custom-call(s32[192]{0:T(256)S(1)} %add.149.refs_0_.place, s32[192]{0:T(256)S(1)} %reshape.75.refs_1_.used, s32[8]{0:T(128)S(1)} %slice.76.own_ref, bf16[4,32,512]{2,1,0:T(8,128)(2,1)S(1)} %copy-done.2, ...), custom_call_target="tpu_custom_call" | custom-call | bytes 8388608 | tf_op jit(solution)/shard_map/update_factors/pallas_call | solution.py:341
  (168 shorter events, 43.7 us)
Async XLA Ops:
  7.2 142.4 %reduce-scatter.4.cloned.1.call-start = ((), (), s32[]{:S(2)}) async-start(), calls=%async_computation.1 | async-start | bytes 15597568
  21.2 10.8 %collective-permute-start.4 = (bf16[128,512]{1,0:T(8,128)(2,1)S(1)}, bf16[128,512]{1,0:T(8,128)(2,1)S(1)}, u32[]{:S(2)}, u32[]{:S(2)}) collective-permute-start(bf16[128,512]{1,0:T(8,128)(2,1)S(1)} %bitcast.14), channel_id=1, source_target_pairs={{0,32},{16,48},{32,64},{48,80},{64,96},{80,112},{96,128},{112,144}... | collective-permute-start | bytes 393224 | tf_op jit(solution)/shard_map/ppermute | solution.py:38
  23.6 14.4 %collective-permute-start.1 = (bf16[128,512]{1,0:T(8,128)(2,1)S(1)}, bf16[128,512]{1,0:T(8,128)(2,1)S(1)}, u32[]{:S(2)}, u32[]{:S(2)}) collective-permute-start(bf16[128,512]{1,0:T(8,128)(2,1)S(1)} %bitcast.15), channel_id=1, source_target_pairs={{0,224},{16,240},{32,0},{48,16},{64,32},{80,48},{96,64},{112,80},{... | collective-permute-start | bytes 393224 | tf_op jit(solution)/shard_map/ppermute | solution.py:38
  29.0 9.2 %collective-permute-start.12 = (bf16[144,512]{1,0:T(8,128)(2,1)S(1)}, bf16[144,512]{1,0:T(8,128)(2,1)S(1)}, u32[]{:S(2)}, u32[]{:S(2)}) collective-permute-start(bf16[144,512]{1,0:T(8,128)(2,1)S(1)} %fusion.1.refs_8_.refs_9_), channel_id=1, source_target_pairs={{0,32},{16,48},{32,64},{48,80},{64,96},{80,112},{96,128},{112,144}... | collective-permute-start | bytes 442376 | tf_op jit(solution)/shard_map/ppermute | solution.py:38
  29.0 5.6 %collective-permute-start.8 = (bf16[144,512]{1,0:T(8,128)(2,1)S(1)}, bf16[144,512]{1,0:T(8,128)(2,1)S(1)}, u32[]{:S(2)}, u32[]{:S(2)}) collective-permute-start(bf16[144,512]{1,0:T(8,128)(2,1)S(1)} %fusion.1.refs_8_.refs_9_), channel_id=1, source_target_pairs={{0,224},{16,240},{32,0},{48,16},{64,32},{80,48},{96,64},{112,80},{... | collective-permute-start | bytes 442376 | tf_op jit(solution)/shard_map/ppermute | solution.py:38
  32.0 7.7 %collective-permute-start.5 = (bf16[128,512]{1,0:T(8,128)(2,1)S(1)}, bf16[128,512]{1,0:T(8,128)(2,1)S(1)}, u32[]{:S(2)}, u32[]{:S(2)}) collective-permute-start(bf16[128,512]{1,0:T(8,128)(2,1)S(1)} %collective-permute-done.4.refs_7_.refs_8_), channel_id=1, source_target_pairs={{0,32},{16,48},{32,64},{48,80},{64,96},{80,112},{96,128},{112,144}... | collective-permute-start | bytes 393224 | tf_op jit(solution)/shard_map/ppermute | solution.py:38
  38.1 5.6 %collective-permute-start.2 = (bf16[128,512]{1,0:T(8,128)(2,1)S(1)}, bf16[128,512]{1,0:T(8,128)(2,1)S(1)}, u32[]{:S(2)}, u32[]{:S(2)}) collective-permute-start(bf16[128,512]{1,0:T(8,128)(2,1)S(1)} %collective-permute-done.1.refs_1_.refs_2_), channel_id=1, source_target_pairs={{0,224},{16,240},{32,0},{48,16},{64,32},{80,48},{96,64},{112,80},{... | collective-permute-start | bytes 393224 | tf_op jit(solution)/shard_map/ppermute | solution.py:38
  38.2 8.2 %collective-permute-start.13 = (bf16[144,512]{1,0:T(8,128)(2,1)S(1)}, bf16[144,512]{1,0:T(8,128)(2,1)S(1)}, u32[]{:S(2)}, u32[]{:S(2)}) collective-permute-start(bf16[144,512]{1,0:T(8,128)(2,1)S(1)} %collective-permute-done.12.refs_15_.refs_16_), channel_id=1, source_target_pairs={{0,32},{16,48},{32,64},{48,80},{64,96},{80,112},{96,128},{112,144}... | collective-permute-start | bytes 442376 | tf_op jit(solution)/shard_map/ppermute | solution.py:38
  39.6 6.7 %collective-permute-start.6 = (bf16[128,512]{1,0:T(8,128)(2,1)S(1)}, bf16[128,512]{1,0:T(8,128)(2,1)S(1)}, u32[]{:S(2)}, u32[]{:S(2)}) collective-permute-start(bf16[128,512]{1,0:T(8,128)(2,1)S(1)} %collective-permute-done.5.refs_6_.refs_7_), channel_id=1, source_target_pairs={{0,32},{16,48},{32,64},{48,80},{64,96},{80,112},{96,128},{112,144}... | collective-permute-start | bytes 393224 | tf_op jit(solution)/shard_map/ppermute | solution.py:38
  40.1 6.5 %collective-permute-start.10 = (bf16[144,512]{1,0:T(8,128)(2,1)S(1)}, bf16[144,512]{1,0:T(8,128)(2,1)S(1)}, u32[]{:S(2)}, u32[]{:S(2)}) collective-permute-start(bf16[144,512]{1,0:T(8,128)(2,1)S(1)} %collective-permute-done.9.refs_10_.refs_11_), channel_id=1, source_target_pairs={{0,224},{16,240},{32,0},{48,16},{64,32},{80,48},{96,64},{112,80},{... | collective-permute-start | bytes 442376 | tf_op jit(solution)/shard_map/ppermute | solution.py:38
  43.7 6.1 %collective-permute-start.3 = (bf16[128,512]{1,0:T(8,128)(2,1)S(1)}, bf16[128,512]{1,0:T(8,128)(2,1)S(1)}, u32[]{:S(2)}, u32[]{:S(2)}) collective-permute-start(bf16[128,512]{1,0:T(8,128)(2,1)S(1)} %collective-permute-done.2.refs_2_.refs_3_), channel_id=1, source_target_pairs={{0,224},{16,240},{32,0},{48,16},{64,32},{80,48},{96,64},{112,80},{... | collective-permute-start | bytes 393224 | tf_op jit(solution)/shard_map/ppermute | solution.py:38
  46.4 5.6 %collective-permute-start.14 = (bf16[144,512]{1,0:T(8,128)(2,1)S(1)}, bf16[144,512]{1,0:T(8,128)(2,1)S(1)}, u32[]{:S(2)}, u32[]{:S(2)}) collective-permute-start(bf16[144,512]{1,0:T(8,128)(2,1)S(1)} %collective-permute-done.13.refs_14_.refs_15_), channel_id=1, source_target_pairs={{0,32},{16,48},{32,64},{48,80},{64,96},{80,112},{96,128},{112,144}... | collective-permute-start | bytes 442376 | tf_op jit(solution)/shard_map/ppermute | solution.py:38
  46.4 7.0 %collective-permute-start.7 = (bf16[128,512]{1,0:T(8,128)(2,1)S(1)}, bf16[128,512]{1,0:T(8,128)(2,1)S(1)}, u32[]{:S(2)}, u32[]{:S(2)}) collective-permute-start(bf16[128,512]{1,0:T(8,128)(2,1)S(1)} %collective-permute-done.6.refs_5_.refs_6_), channel_id=1, source_target_pairs={{0,32},{16,48},{32,64},{48,80},{64,96},{80,112},{96,128},{112,144}... | collective-permute-start | bytes 393224 | tf_op jit(solution)/shard_map/ppermute | solution.py:38
  46.7 6.7 %collective-permute-start.11 = (bf16[144,512]{1,0:T(8,128)(2,1)S(1)}, bf16[144,512]{1,0:T(8,128)(2,1)S(1)}, u32[]{:S(2)}, u32[]{:S(2)}) collective-permute-start(bf16[144,512]{1,0:T(8,128)(2,1)S(1)} %collective-permute-done.10.refs_11_.refs_12_), channel_id=1, source_target_pairs={{0,224},{16,240},{32,0},{48,16},{64,32},{80,48},{96,64},{112,80},{... | collective-permute-start | bytes 442376 | tf_op jit(solution)/shard_map/ppermute | solution.py:38
  64.4 16.2 %collective-permute-start.16 = (bf16[4,32,128]{2,1,0:T(8,128)(2,1)S(1)}, bf16[4,32,128]{2,1,0:T(8,128)(2,1)S(1)}, u32[]{:S(2)}, u32[]{:S(2)}) collective-permute-start(bf16[4,32,128]{2,1,0:T(8,128)(2,1)S(1)} %get-tuple-element.27), channel_id=1, source_target_pairs={{0,1},{1,2},{2,3},{3,0},{4,5},{5,6},{6,7},{7,4},{8,9},{9,10},{10,1... | collective-permute-start | bytes 98312 | tf_op jit(solution)/shard_map/ppermute | solution.py:52
  65.7 14.9 %collective-permute-start.17 = (bf16[4,32,128]{2,1,0:T(8,128)(2,1)S(1)}, bf16[4,32,128]{2,1,0:T(8,128)(2,1)S(1)}, u32[]{:S(2)}, u32[]{:S(2)}) collective-permute-start(bf16[4,32,128]{2,1,0:T(8,128)(2,1)S(1)} %get-tuple-element.28), channel_id=1, source_target_pairs={{0,2},{1,3},{2,0},{3,1},{4,6},{5,7},{6,4},{7,5},{8,10},{9,11},{10,... | collective-permute-start | bytes 98312 | tf_op jit(solution)/shard_map/ppermute | solution.py:52
  68.4 12.3 %collective-permute-start.18 = (bf16[4,32,128]{2,1,0:T(8,128)(2,1)S(1)}, bf16[4,32,128]{2,1,0:T(8,128)(2,1)S(1)}, u32[]{:S(2)}, u32[]{:S(2)}) collective-permute-start(bf16[4,32,128]{2,1,0:T(8,128)(2,1)S(1)} %get-tuple-element.29), channel_id=1, source_target_pairs={{0,3},{1,0},{2,1},{3,2},{4,7},{5,4},{6,5},{7,6},{8,11},{9,8},{10,9... | collective-permute-start | bytes 98312 | tf_op jit(solution)/shard_map/ppermute | solution.py:52
  96.4 7.1 %collective-permute-start.26 = (bf16[7,32,512]{2,1,0:T(8,128)(2,1)S(1)}, bf16[7,32,512]{2,1,0:T(8,128)(2,1)S(1)}, u32[]{:S(2)}, u32[]{:S(2)}) collective-permute-start(bf16[7,32,512]{2,1,0:T(8,128)(2,1)S(1)} %get-tuple-element.35.refs_2_), channel_id=1, source_target_pairs={{0,32},{16,48},{32,64},{48,80},{64,96},{80,112},{96,128},{112,144}... | collective-permute-start | bytes 688136 | tf_op jit(solution)/shard_map/ppermute | solution.py:38
  98.3 5.5 %collective-permute-start.30 = (bf16[7,32,512]{2,1,0:T(8,128)(2,1)S(1)}, bf16[7,32,512]{2,1,0:T(8,128)(2,1)S(1)}, u32[]{:S(2)}, u32[]{:S(2)}) collective-permute-start(bf16[7,32,512]{2,1,0:T(8,128)(2,1)S(1)} %get-tuple-element.36.refs_9_), channel_id=1, source_target_pairs={{0,224},{16,240},{32,0},{48,16},{64,32},{80,48},{96,64},{112,80},{... | collective-permute-start | bytes 688136 | tf_op jit(solution)/shard_map/ppermute | solution.py:38
  101.6 6.0 %collective-permute-start.34 = (bf16[7,32,512]{2,1,0:T(8,128)(2,1)S(1)}, bf16[7,32,512]{2,1,0:T(8,128)(2,1)S(1)}, u32[]{:S(2)}, u32[]{:S(2)}) collective-permute-start(bf16[7,32,512]{2,1,0:T(8,128)(2,1)S(1)} %get-tuple-element.35.refs_2_), channel_id=1, source_target_pairs={{0,224},{16,240},{32,0},{48,16},{64,32},{80,48},{96,64},{112,80},{... | collective-permute-start | bytes 688136 | tf_op jit(solution)/shard_map/ppermute | solution.py:38
  102.9 7.2 %collective-permute-start.37 = (bf16[7,32,512]{2,1,0:T(8,128)(2,1)S(1)}, bf16[7,32,512]{2,1,0:T(8,128)(2,1)S(1)}, u32[]{:S(2)}, u32[]{:S(2)}) collective-permute-start(bf16[7,32,512]{2,1,0:T(8,128)(2,1)S(1)} %get-tuple-element.36.refs_9_), channel_id=1, source_target_pairs={{0,32},{16,48},{32,64},{48,80},{64,96},{80,112},{96,128},{112,144}... | collective-permute-start | bytes 688136 | tf_op jit(solution)/shard_map/ppermute | solution.py:38
  103.5 10.1 %collective-permute-start.27 = (bf16[7,32,512]{2,1,0:T(8,128)(2,1)S(1)}, bf16[7,32,512]{2,1,0:T(8,128)(2,1)S(1)}, u32[]{:S(2)}, u32[]{:S(2)}) collective-permute-start(bf16[7,32,512]{2,1,0:T(8,128)(2,1)S(1)} %collective-permute-done.26.refs_8_), channel_id=1, source_target_pairs={{0,32},{16,48},{32,64},{48,80},{64,96},{80,112},{96,128},{112,144}... | collective-permute-start | bytes 688136 | tf_op jit(solution)/shard_map/ppermute | solution.py:38
  103.8 11.1 %collective-permute-start.31 = (bf16[7,32,512]{2,1,0:T(8,128)(2,1)S(1)}, bf16[7,32,512]{2,1,0:T(8,128)(2,1)S(1)}, u32[]{:S(2)}, u32[]{:S(2)}) collective-permute-start(bf16[7,32,512]{2,1,0:T(8,128)(2,1)S(1)} %collective-permute-done.30.refs_10_), channel_id=1, source_target_pairs={{0,224},{16,240},{32,0},{48,16},{64,32},{80,48},{96,64},{112,80},{... | collective-permute-start | bytes 688136 | tf_op jit(solution)/shard_map/ppermute | solution.py:38
  107.6 9.9 %collective-permute-start.35 = (bf16[7,32,512]{2,1,0:T(8,128)(2,1)S(1)}, bf16[7,32,512]{2,1,0:T(8,128)(2,1)S(1)}, u32[]{:S(2)}, u32[]{:S(2)}) collective-permute-start(bf16[7,32,512]{2,1,0:T(8,128)(2,1)S(1)} %collective-permute-done.34.refs_3_), channel_id=1, source_target_pairs={{0,224},{16,240},{32,0},{48,16},{64,32},{80,48},{96,64},{112,80},{... | collective-permute-start | bytes 688136 | tf_op jit(solution)/shard_map/ppermute | solution.py:38
  110.2 9.9 %collective-permute-start.38 = (bf16[7,32,512]{2,1,0:T(8,128)(2,1)S(1)}, bf16[7,32,512]{2,1,0:T(8,128)(2,1)}, u32[]{:S(2)}, u32[]{:S(2)}) collective-permute-start(bf16[7,32,512]{2,1,0:T(8,128)(2,1)S(1)} %collective-permute-done.37.refs_15_), channel_id=1, source_target_pairs={{0,32},{16,48},{32,64},{48,80},{64,96},{80,112},{96,128},{112,144}... | collective-permute-start | bytes 688136 | tf_op jit(solution)/shard_map/ppermute | solution.py:38
  113.5 9.0 %collective-permute-start.28 = (bf16[7,32,512]{2,1,0:T(8,128)(2,1)S(1)}, bf16[7,32,512]{2,1,0:T(8,128)(2,1)}, u32[]{:S(2)}, u32[]{:S(2)}) collective-permute-start(bf16[7,32,512]{2,1,0:T(8,128)(2,1)S(1)} %collective-permute-done.27.refs_7_), channel_id=1, source_target_pairs={{0,32},{16,48},{32,64},{48,80},{64,96},{80,112},{96,128},{112,144}... | collective-permute-start | bytes 688136 | tf_op jit(solution)/shard_map/ppermute | solution.py:38
  114.9 8.8 %collective-permute-start.32 = (bf16[7,32,512]{2,1,0:T(8,128)(2,1)S(1)}, bf16[7,32,512]{2,1,0:T(8,128)(2,1)}, u32[]{:S(2)}, u32[]{:S(2)}) collective-permute-start(bf16[7,32,512]{2,1,0:T(8,128)(2,1)S(1)} %collective-permute-done.31.refs_11_), channel_id=1, source_target_pairs={{0,224},{16,240},{32,0},{48,16},{64,32},{80,48},{96,64},{112,80},{... | collective-permute-start | bytes 688136 | tf_op jit(solution)/shard_map/ppermute | solution.py:38
  117.5 10.1 %collective-permute-start.36 = (bf16[7,32,512]{2,1,0:T(8,128)(2,1)S(1)}, bf16[7,32,512]{2,1,0:T(8,128)(2,1)}, u32[]{:S(2)}, u32[]{:S(2)}) collective-permute-start(bf16[7,32,512]{2,1,0:T(8,128)(2,1)S(1)} %collective-permute-done.35.refs_4_), channel_id=1, source_target_pairs={{0,224},{16,240},{32,0},{48,16},{64,32},{80,48},{96,64},{112,80},{... | collective-permute-start | bytes 688136 | tf_op jit(solution)/shard_map/ppermute | solution.py:38
  120.0 9.1 %collective-permute-start.39 = (bf16[7,32,512]{2,1,0:T(8,128)(2,1)}, bf16[7,32,512]{2,1,0:T(8,128)(2,1)}, u32[]{:S(2)}, u32[]{:S(2)}) collective-permute-start(bf16[7,32,512]{2,1,0:T(8,128)(2,1)} %collective-permute-done.38.refs_14_), channel_id=1, source_target_pairs={{0,32},{16,48},{32,64},{48,80},{64,96},{80,112},{96,128},{112,144}... | collective-permute-start | bytes 688136 | tf_op jit(solution)/shard_map/ppermute | solution.py:38
  122.5 13.0 %collective-permute-start.29 = (bf16[7,32,512]{2,1,0:T(8,128)(2,1)}, bf16[7,32,512]{2,1,0:T(8,128)(2,1)S(1)}, u32[]{:S(2)}, u32[]{:S(2)}) collective-permute-start(bf16[7,32,512]{2,1,0:T(8,128)(2,1)} %collective-permute-done.28.refs_6_), channel_id=1, source_target_pairs={{0,32},{16,48},{32,64},{48,80},{64,96},{80,112},{96,128},{112,144}... | collective-permute-start | bytes 688136 | tf_op jit(solution)/shard_map/ppermute | solution.py:38
  123.7 11.9 %collective-permute-start.33 = (bf16[7,32,512]{2,1,0:T(8,128)(2,1)}, bf16[7,32,512]{2,1,0:T(8,128)(2,1)S(1)}, u32[]{:S(2)}, u32[]{:S(2)}) collective-permute-start(bf16[7,32,512]{2,1,0:T(8,128)(2,1)} %collective-permute-done.32.refs_12_), channel_id=1, source_target_pairs={{0,224},{16,240},{32,0},{48,16},{64,32},{80,48},{96,64},{112,80},{... | collective-permute-start | bytes 688136 | tf_op jit(solution)/shard_map/ppermute | solution.py:38
  136.4 10.4 %collective-permute-start.40 = (bf16[24,32,512]{2,1,0:T(8,128)(2,1)S(1)}, bf16[24,32,512]{2,1,0:T(8,128)(2,1)S(1)}, u32[]{:S(2)}, u32[]{:S(2)}) collective-permute-start(bf16[24,32,512]{2,1,0:T(8,128)(2,1)S(1)} %gradient_share.1), channel_id=1, source_target_pairs={{0,16},{16,0},{32,48},{48,32},{64,80},{80,64},{96,112},{112,96},{1... | collective-permute-start | bytes 2359304 | tf_op jit(solution)/shard_map/ppermute | solution.py:43
  (44 other events, 582.4 us)
Sparse Core Ops, SparseCore 0:
  20.5 112.9 reduce-scatter.3

commit v2 on v1

--- a/solution.py
+++ b/solution.py
@@ -68,78 +68,42 @@
     return [[parts[place] for place in range(8)] for parts in found]
 
 
-def fetch(sources, target, sems, first):
-    copies, row = [], 0
-    for k, ref in enumerate(sources):
-        rows = ref.shape[0]
-        copies.append(pltpu.make_async_copy(ref, target.at[pl.ds(row, rows)], sems.at[first + k]))
-        row += rows
-    for copy in copies:
-        copy.start()
-    return copies
-
-
-def pick_kernel(rank, rows, within_mine, within_other, *refs):
+def pick_kernel(rank, slots, rolls, within_mine, within_other, place, *refs):
     a_refs, b_refs = refs[:8], refs[8:16]
-    mine_ref, other_ref, ids_ref = refs[16:]
+    mine_ref, other_ref, mine_roll, other_roll, ids_ref, hold_a, hold_b = refs[16:]
+    rows = slots * rank
     for k in range(8):
         for ref, within in ((mine_ref, within_mine), (other_ref, within_other)):
             at = pl.ds(pl.multiple_of(within[k] * rank, rank), rank)
             ref[k] = a_refs[k][at, :]
             ref[8 + k] = b_refs[k][at, :]
         ids_ref[k] = b_refs[k][rows:, : ids_ref.shape[2]]
-
-
-def pick(within_mine, within_other, parts_a, parts_b, rank):
+        hold_a[k * rows : (k + 1) * rows, :] = a_refs[k][...]
+        hold_b[k * rows : (k + 1) * rows, :] = b_refs[k][:rows, :]
+    for ref, first in ((mine_roll, 0), (other_roll, rolls)):
+        for n in range(rolls):
+            at = pl.ds(pl.multiple_of(place[first + n] * rank, rank), rank)
+            ref[n] = hold_a[at, :]
+            ref[rolls + n] = hold_b[at, :]
+
+
+def pick(within_mine, within_other, place, parts_a, parts_b, rank):
     rows, width = parts_a[0].shape
-    tall = parts_b[0].shape[0]
-    shape = jax.ShapeDtypeStruct((16, rank, width), BF)
-    return pl.pallas_call(
-        functools.partial(pick_kernel, rank, rows),
-        out_shape=(shape, shape, jax.ShapeDtypeStruct((8, tall - rows, 128), BF)),
-        in_specs=[SMEM()] * 2 + [VMEM()] * 16,
-        out_specs=(VMEM(),) * 3,
+    tall, rolls = parts_b[0].shape[0], place.shape[0] // 2
+    shape = lambda n: jax.ShapeDtypeStruct((n, rank, width), BF)
+    return pl.pallas_call(
+        functools.partial(pick_kernel, rank, rows // rank, rolls),
+        out_shape=(
+            shape(16), shape(16), shape(2 * rolls), shape(2 * rolls),
+            jax.ShapeDtypeStruct((8, tall - rows, 128), BF),
+        ),
+        in_specs=[SMEM()] * 3 + [VMEM()] * 16,
+        out_specs=(VMEM(),) * 5,
+        scratch_shapes=[pltpu.VMEM((8 * rows, width), BF)] * 2,
         compiler_params=PARAMS,
         cost_estimate=pl.CostEstimate(flops=0, bytes_accessed=6 * 2**20, transcendentals=0),
         name="pick_factors",
-    )(within_mine, within_other, *parts_a, *parts_b)
-
-
-def rolls_kernel(rolls, slots, rank, *refs):
-    place, refs = refs[0], refs[1:]
-    a_refs, b_refs = refs[:8], refs[8:16]
-    mine_ref, other_ref, hold_a, hold_b, sems = refs[16:]
-    copies = fetch(a_refs, hold_a, sems, 0) + fetch(b_refs, hold_b, sems, 8)
-    for copy in copies:
-        copy.wait()
-    tail = b_refs[0].shape[0] - slots * rank
-    for ref, first in ((mine_ref, 0), (other_ref, rolls)):
-        for n in range(rolls):
-            at = place[first + n]
-            ref[n] = hold_a[pl.ds(pl.multiple_of(at * rank, rank), rank), :]
-            row = at * rank + at // slots * tail
-            ref[rolls + n] = hold_b[pl.ds(pl.multiple_of(row, 16), rank), :]
-
-
-def pick_rolls(place, parts_a, parts_b, rolls, slots):
-    rows, width = parts_a[0].shape
-    rank = rows // slots
-    tall = parts_b[0].shape[0]
-    shape = jax.ShapeDtypeStruct((2 * rolls, rank, width), BF)
-    return pl.pallas_call(
-        functools.partial(rolls_kernel, rolls, slots, rank),
-        out_shape=(shape, shape),
-        in_specs=[SMEM()] + [ANY()] * 16,
-        out_specs=(VMEM(),) * 2,
-        scratch_shapes=[
-            pltpu.VMEM((8 * rows, width), BF),
-            pltpu.VMEM((8 * tall, width), BF),
-            pltpu.SemaphoreType.DMA((16,)),
-        ],
-        compiler_params=PARAMS,
-        cost_estimate=pl.CostEstimate(flops=0, bytes_accessed=8 * 2**20, transcendentals=0),
-        name="pick_rollouts",
-    )(place, *parts_a, *parts_b)
+    )(within_mine, within_other, place, *parts_a, *parts_b)
 
 
 def project_kernel(
@@ -186,23 +150,6 @@
     )(own, near, here, mine, other, acts, grad)
 
 
-def sum_kernel(terms, *refs):
-    out_ref = refs[-1]
-    out_ref[...] = sum(ref[...].astype(F32) for ref in refs[:terms]).astype(BF)
-
-
-def sum_after(token, terms):
-    return pl.pallas_call(
-        functools.partial(sum_kernel, len(terms)),
-        out_shape=jax.ShapeDtypeStruct(terms[0].shape, BF),
-        in_specs=[VMEM()] * len(terms) + [ANY()],
-        out_specs=VMEM(),
-        compiler_params=PARAMS,
-        cost_estimate=pl.CostEstimate(flops=0, bytes_accessed=2**20, transcendentals=0),
-        name="rank_sum",
-    )(*terms, token)
-
-
 def contribute_kernel(blocks, here_ref, *refs):
     parts, (acts_ref, grad_ref, ranks_ref, a_ref, b_ref, hold) = refs[:SIDE], refs[SIDE:]
     quarter = parts[0].shape[0]
@@ -237,69 +184,56 @@
     )(here, *parts, acts, grad)
 
 
-def total_kernel(needs, *refs):
-    place, used, refs = refs[0], refs[1], refs[2:]
-    a_refs, b_refs = refs[:7], refs[7:14]
-    mine_ref, other_ref, hold_a, hold_b, sems = refs[14:]
-    copies = fetch(a_refs, hold_a, sems, 0) + fetch(b_refs, hold_b, sems, 7)
-    for copy in copies:
-        copy.wait()
-
-    def one(need, hold):
-        def term(source):
+def total_kernel(needs, place, used, *refs):
+    a_refs, b_refs, (mine_ref, other_ref) = refs[:7], refs[7:14], refs[14:]
+
+    def one(need, parts):
+        value = None
+        for source, part in enumerate(parts):
             at = need * 8 + source
-            return hold[place[at]].astype(F32) * used[at].astype(F32)
-
-        value = term(0)
-        for source in range(1, 7):
-            value += term(source)
+            term = part[place[at]].astype(F32) * used[at].astype(F32)
+            value = term if value is None else value + term
         return value
 
     @pl.loop(0, needs)
     def _(need):
-        mine_ref[need] = one(need, hold_a)
-        mine_ref[needs + need] = one(need, hold_b)
-        other_ref[need] = one(needs + need, hold_a)
-        other_ref[needs + need] = one(needs + need, hold_b)
+        mine_ref[need] = one(need, a_refs)
+        mine_ref[needs + need] = one(need, b_refs)
+        other_ref[need] = one(needs + need, a_refs)
+        other_ref[needs + need] = one(needs + need, b_refs)
 
 
 def total(place, used, parts_a, parts_b, needs):
-    blocks, (rank, width) = 7 * parts_a[0].shape[0], parts_a[0].shape[1:]
-    shape = jax.ShapeDtypeStruct((2 * needs, rank, width), F32)
+    shape = jax.ShapeDtypeStruct((2 * needs,) + parts_a[0].shape[1:], F32)
     return pl.pallas_call(
         functools.partial(total_kernel, needs),
         out_shape=(shape, shape),
-        in_specs=[SMEM()] * 2 + [ANY()] * 14,
+        in_specs=[SMEM()] * 2 + [VMEM()] * 14,
         out_specs=(VMEM(),) * 2,
-        scratch_shapes=[
-            pltpu.VMEM((blocks, rank, width), BF),
-            pltpu.VMEM((blocks, rank, width), BF),
-            pltpu.SemaphoreType.DMA((14,)),
-        ],
         compiler_params=PARAMS,
         cost_estimate=pl.CostEstimate(flops=0, bytes_accessed=16 * 2**20, transcendentals=0),
         name="gradient_totals",
     )(place, used, *parts_a, *parts_b)
 
 
-def far_term(place, used, far_ref, need, first):
+def far_term(place, used, far_ref, need):
     at = need * 8 + 7
-    return far_ref[place[at] - first].astype(F32) * used[at].astype(F32)
-
-
-def share_kernel(needs, first, place, used, far_a, far_b, near_ref, out_ref):
+    return far_ref[place[at]].astype(F32) * used[at].astype(F32)
+
+
+def share_kernel(needs, place, used, far_a, far_b, near_ref, out_ref):
     @pl.loop(0, needs)
     def _(need):
         for k, far in enumerate((far_a, far_b)):
             at = k * needs + need
             out_ref[at] = (
-                near_ref[at] + far_term(place, used, far, needs + need, first)
+                near_ref[at] + far_term(place, used, far, needs + need)
             ).astype(BF)
 
 
 def share(place, used, far_a, far_b, near):
     return pl.pallas_call(
-        functools.partial(share_kernel, near.shape[0] // 2, 7 * far_a.shape[0]),
+        functools.partial(share_kernel, near.shape[0] // 2),
         out_shape=jax.ShapeDtypeStruct(near.shape, BF),
         in_specs=[SMEM()] * 2 + [VMEM()] * 3,
         out_specs=VMEM(),
@@ -310,7 +244,7 @@
 
 
 def update_kernel(
-    slots, rolls, first, place, used, own_ref, a_ref, b_ref, mine_roll, other_roll,
+    slots, rolls, place, used, own_ref, a_ref, b_ref, mine_roll, other_roll,
     far_a, far_b, mine_ref, other_ref, new_a, new_b, roll_a, roll_b,
 ):
     needs = slots + rolls
@@ -318,7 +252,7 @@
     def fresh(factor, at, far):
         gradient = (
             mine_ref[at]
-            + far_term(place, used, far, at % needs, first)
+            + far_term(place, used, far, at % needs)
             + other_ref[at].astype(F32)
         )
         return (factor.astype(F32) - LEARN_RATE * gradient).astype(BF)
@@ -339,7 +273,7 @@
     rolls = mine_roll.shape[0] // 2
     shape = lambda n: jax.ShapeDtypeStruct((n, rank, width), BF)
     return pl.pallas_call(
-        functools.partial(update_kernel, slots, rolls, 7 * far_a.shape[0]),
+        functools.partial(update_kernel, slots, rolls),
         out_shape=(shape(slots), shape(slots), shape(rolls), shape(rolls)),
         in_specs=[SMEM()] * 3 + [VMEM()] * 8,
         out_specs=(VMEM(),) * 4,
@@ -443,27 +377,22 @@
     parts_a, parts_b = ring_gather(
         factor_a.reshape(-1, width), jnp.concatenate([factor_b.reshape(-1, width), ids])
     )
-    mine_sel, other_sel, ring_ids = pick(
-        mine_within, other_within, parts_a, parts_b, factor_a.shape[1]
+    mine_sel, other_sel, mine_roll, other_roll, ring_ids = pick(
+        mine_within, other_within,
+        jnp.concatenate([mine_place[blocks:], other_place[blocks:]]),
+        parts_a, parts_b, factor_a.shape[1],
     )
     got_sel = core_swap(other_sel)
     here = (lax.axis_index("tensor") % SIDE).reshape(1)
     chosen_a, *rank_parts = project(
         mine_own[:blocks], mine_near, here, mine_sel, got_sel, input_acts, out_grad
     )
-    mine_roll, other_roll = pick_rolls(
-        jnp.concatenate([mine_place[blocks:], other_place[blocks:]]),
-        parts_a, parts_b, rolls, slots,
-    )
     got_roll = core_swap(other_roll)
-    quarter = sum_after(
-        mine_roll,
-        [rank_parts[0]] + [plane_hop(rank_parts[step], step, "y") for step in range(1, SIDE)],
-    )
-    quarter = sum(
-        term.astype(F32)
-        for term in [quarter] + [plane_hop(quarter, step, "x") for step in range(1, SIDE)]
-    ).astype(BF)
+    quarter = rank_parts[0]
+    for axis, terms in (("y", rank_parts), ("x", None)):
+        terms = terms or [quarter] * SIDE
+        came = [plane_hop(terms[step], step, axis) for step in range(1, SIDE)]
+        quarter = sum(term.astype(F32) for term in [quarter, *came]).astype(BF)
     ranks, part_a, part_b = contribute(
         here,
         [quarter] + [plane_hop(quarter, step, "y") for step in range(1, SIDE)],
@@ -480,8 +409,7 @@
     match = (need[:, None, None] == ring[None]).astype(jnp.int32)
     used = jnp.sum(match, axis=2)
     at_block = jnp.sum(match * jnp.arange(blocks, dtype=jnp.int32)[None, None], axis=2)
-    source = jnp.arange(chips, dtype=jnp.int32)[None, :] * blocks + at_block
-    source, used = source.reshape(-1), used.reshape(-1)
+    source, used = at_block.reshape(-1), used.reshape(-1)
 
     parts_a, parts_b = ring_gather(part_a, part_b)
     near = order[:7]

time: 159 us -> 145 us (0.912)
  local copies, waits for them, and re-layouts: 14.8 us -> 4.42 us
  Pallas kernels: 30.8 us -> 24.1 us
  waiting for transfers between devices: 32.2 us -> 38.4 us
  starting transfers between devices: 65.6 us -> 62.7 us
    unnamed x69 -> x23, local copies, waits for them, and re-layouts: 12.8 us -> 3.66 us
    pallas_call x5 -> x3, Pallas kernels: 7.87 us -> 4.32 us  [the longest x1 1.84 us: update(): pl.pallas_call(functools.partial(update_kernel, slots, rolls), out_shape=...]
    ppermute x28, waiting for transfers between devices: 18.7 us -> 21.7 us  [z_hop(): return lax.ppermute(x, 'dp', perm)]
    ppermute x9, waiting for transfers between devices: 9.09 us -> 12.1 us  [plane_hop(): return lax.ppermute(x, 'tensor', perm)]
    ppermute x28, starting transfers between devices: 42.3 us -> 39.5 us  [z_hop(): return lax.ppermute(x, 'dp', perm)]
    pallas_call x1, Pallas kernels: 6.38 us -> 3.69 us  [total(): pl.pallas_call(functools.partial(total_kernel, needs), out_shape=(shape,...]
  transfers between devices with their start and end apart: 42 -> 42, of which waited for: 19 -> 23; matrix products, arithmetic and copies ran while one was open for 2% -> 1% of each run, Pallas kernels for 10% -> 7%
where the time goes in v2:
time: 145 us
  starting transfers between devices  62.7 us (43%)
  waiting for transfers between devices  38.4 us (26%)
  Pallas kernels  24.1 us (17%)
  between operations  14.2 us (10%)
  local copies, waits for them, and re-layouts  4.42 us (3%)
    ppermute x28, starting transfers between devices, z_hop(): return lax.ppermute(x, 'dp', perm)  39.5 us
    ppermute x28, waiting for transfers between devices, z_hop(): return lax.ppermute(x, 'dp', perm)  21.7 us
    pallas_call x1, Pallas kernels, products(): pl.pallas_call(products_kernel, grid=(columns // tile,), out_shape=jax.Sh...  13.1 us
    ppermute x9, waiting for transfers between devices, plane_hop(): return lax.ppermute(x, 'tensor', perm)  12.1 us
    ppermute x9, starting transfers between devices, plane_hop(): return lax.ppermute(x, 'tensor', perm)  11.9 us
    ppermute x4, starting transfers between devices, core_swap(): return lax.ppermute(x, 'dp', [(d, d ^ 1) for d in range(n)])  11.2 us
    ppermute x4, waiting for transfers between devices, core_swap(): return lax.ppermute(x, 'dp', [(d, d ^ 1) for d in range(n)])  4.45 us
    pallas_call x1, Pallas kernels, total(): pl.pallas_call(functools.partial(total_kernel, needs), out_shape=(shape,...  3.69 us
  transfers between devices with their start and end apart: 42, of which 23 were waited for; matrix products, arithmetic and copies ran while one was open for 1% of the time, Pallas kernels for 7%

profile of v2, /device:TPU:1, one launch (start us, length us, event | category | flops | bytes accessed | tf_op | source)
XLA Modules:
  0.0 144.8 jit_solution(10844604035462922346)
XLA Ops:
  7.2 13.1 %base_products.1 = bf16[16,896,512]{2,1,0:T(8,128)(2,1)} custom-call(bf16[896,512]{1,0:T(8,128)(2,1)} %grad_ref.3, bf16[8192,512]{1,0:T(8,128)(2,1)} %weight_ref.1), custom_call_target="tpu_custom_call" | custom-call | flops 7516192768 | bytes 25165824 | tf_op jit(solution)/shard_map/base_products/pallas_call | solution.py:300
  21.2 2.5 %collective-permute-start.4 = (bf16[128,512]{1,0:T(8,128)(2,1)S(1)}, bf16[128,512]{1,0:T(8,128)(2,1)S(1)}, u32[]{:S(2)}, u32[]{:S(2)}) collective-permute-start(bf16[128,512]{1,0:T(8,128)(2,1)S(1)} %bitcast.14), channel_id=1, source_target_pairs={{0,32},{16,48},{32,64},{48,80},{64,96},{80,112},{96,128},{112,144}... | collective-permute-start | bytes 393224 | tf_op jit(solution)/shard_map/ppermute | solution.py:38
  23.7 3.9 %collective-permute-start.1 = (bf16[128,512]{1,0:T(8,128)(2,1)S(1)}, bf16[128,512]{1,0:T(8,128)(2,1)S(1)}, u32[]{:S(2)}, u32[]{:S(2)}) collective-permute-start(bf16[128,512]{1,0:T(8,128)(2,1)S(1)} %bitcast.15), channel_id=1, source_target_pairs={{0,224},{16,240},{32,0},{48,16},{64,32},{80,48},{96,64},{112,80},{... | collective-permute-start | bytes 393224 | tf_op jit(solution)/shard_map/ppermute | solution.py:38
  29.1 2.7 %collective-permute-start.8 = (bf16[144,512]{1,0:T(8,128)(2,1)S(1)}, bf16[144,512]{1,0:T(8,128)(2,1)S(1)}, u32[]{:S(2)}, u32[]{:S(2)}) collective-permute-start(bf16[144,512]{1,0:T(8,128)(2,1)S(1)} %fusion.1.refs_8_), channel_id=1, source_target_pairs={{0,224},{16,240},{32,0},{48,16},{64,32},{80,48},{96,64},{112,80},{... | collective-permute-start | bytes 442376 | tf_op jit(solution)/shard_map/ppermute | solution.py:38
  32.3 2.4 %collective-permute-done.8.refs_9_ = bf16[144,512]{1,0:T(8,128)(2,1)S(1)} collective-permute-done((bf16[144,512]{1,0:T(8,128)(2,1)S(1)}, bf16[144,512]{1,0:T(8,128)(2,1)S(1)}, u32[]{:S(2)}, u32[]{:S(2)}) %collective-permute-start.8) | collective-permute-done | bytes 147488 | tf_op jit(solution)/shard_map/ppermute | solution.py:38
  34.7 3.4 %collective-permute-start.9 = (bf16[144,512]{1,0:T(8,128)(2,1)S(1)}, bf16[144,512]{1,0:T(8,128)(2,1)S(1)}, u32[]{:S(2)}, u32[]{:S(2)}) collective-permute-start(bf16[144,512]{1,0:T(8,128)(2,1)S(1)} %collective-permute-done.8.refs_9_), channel_id=1, source_target_pairs={{0,224},{16,240},{32,0},{48,16},{64,32},{80,48},{96,64},{112,80},{... | collective-permute-start | bytes 442376 | tf_op jit(solution)/shard_map/ppermute | solution.py:38
  40.2 3.5 %collective-permute-start.10 = (bf16[144,512]{1,0:T(8,128)(2,1)S(1)}, bf16[144,512]{1,0:T(8,128)(2,1)S(1)}, u32[]{:S(2)}, u32[]{:S(2)}) collective-permute-start(bf16[144,512]{1,0:T(8,128)(2,1)S(1)} %collective-permute-done.9.refs_10_), channel_id=1, source_target_pairs={{0,224},{16,240},{32,0},{48,16},{64,32},{80,48},{96,64},{112,80},{... | collective-permute-start | bytes 442376 | tf_op jit(solution)/shard_map/ppermute | solution.py:38
  43.7 2.7 %collective-permute-start.3 = (bf16[128,512]{1,0:T(8,128)(2,1)S(1)}, bf16[128,512]{1,0:T(8,128)(2,1)S(1)}, u32[]{:S(2)}, u32[]{:S(2)}) collective-permute-start(bf16[128,512]{1,0:T(8,128)(2,1)S(1)} %collective-permute-done.2.refs_2_), channel_id=1, source_target_pairs={{0,224},{16,240},{32,0},{48,16},{64,32},{80,48},{96,64},{112,80},{... | collective-permute-start | bytes 393224 | tf_op jit(solution)/shard_map/ppermute | solution.py:38
  46.7 3.0 %collective-permute-start.11 = (bf16[144,512]{1,0:T(8,128)(2,1)S(1)}, bf16[144,512]{1,0:T(8,128)(2,1)S(1)}, u32[]{:S(2)}, u32[]{:S(2)}) collective-permute-start(bf16[144,512]{1,0:T(8,128)(2,1)S(1)} %collective-permute-done.10.refs_11_), channel_id=1, source_target_pairs={{0,224},{16,240},{32,0},{48,16},{64,32},{80,48},{96,64},{112,80},{... | collective-permute-start | bytes 442376 | tf_op jit(solution)/shard_map/ppermute | solution.py:38
  49.9 2.2 %collective-permute-done.14.refs_13_ = bf16[144,512]{1,0:T(8,128)(2,1)S(1)} collective-permute-done((bf16[144,512]{1,0:T(8,128)(2,1)S(1)}, bf16[144,512]{1,0:T(8,128)(2,1)S(1)}, u32[]{:S(2)}, u32[]{:S(2)}) %collective-permute-start.14) | collective-permute-done | bytes 147488 | tf_op jit(solution)/shard_map/ppermute | solution.py:38
  53.4 1.6 %pick_factors.1 = (bf16[16,32,512]{2,1,0:T(8,128)(2,1)S(1)}, bf16[16,32,512]{2,1,0:T(8,128)(2,1)}, bf16[16,32,512]{2,1,0:T(8,128)(2,1)S(1)}, bf16[16,32,512]{2,1,0:T(8,128)(2,1)S(1)}, bf16[8,16,128]{2,1,0:T(8,128)(2,1)S(1)}) custom-call(s32[8]{0:T(128)S(1)} %select_reduce_fusion.2.within_mine, s32[8]{0:T(128)S(1)} %select_reduce_fusion.1.within_other, ...), custom_call_target="tpu_custom_call" | custom-call | bytes 6291456 | tf_op jit(solution)/shard_map/pick_factors/pallas_call | solution.py:94
  56.7 3.3 %collective-permute-start.15 = (bf16[16,32,512]{2,1,0:T(8,128)(2,1)}, bf16[16,32,512]{2,1,0:T(8,128)(2,1)S(1)}, u32[]{:S(2)}, u32[]{:S(2)}) collective-permute-start(bf16[16,32,512]{2,1,0:T(8,128)(2,1)} %get-tuple-element.25), channel_id=1, source_target_pairs={{0,16},{16,0},{32,48},{48,32},{64,80},{80,64},{96,112},{112,96},{1... | collective-permute-start | bytes 1572872 | tf_op jit(solution)/shard_map/ppermute | solution.py:43
  60.0 1.7 %collective-permute-done.15.other_ref = bf16[16,32,512]{2,1,0:T(8,128)(2,1)S(1)} collective-permute-done((bf16[16,32,512]{2,1,0:T(8,128)(2,1)}, bf16[16,32,512]{2,1,0:T(8,128)(2,1)S(1)}, u32[]{:S(2)}, u32[]{:S(2)}) %collective-permute-start.15) | collective-permute-done | bytes 524320 | tf_op jit(solution)/shard_map/ppermute | solution.py:43
  64.4 2.6 %collective-permute-start.17 = (bf16[4,32,128]{2,1,0:T(8,128)(2,1)S(1)}, bf16[4,32,128]{2,1,0:T(8,128)(2,1)S(1)}, u32[]{:S(2)}, u32[]{:S(2)}) collective-permute-start(bf16[4,32,128]{2,1,0:T(8,128)(2,1)S(1)} %get-tuple-element.28), channel_id=1, source_target_pairs={{0,2},{1,3},{2,0},{3,1},{4,6},{5,7},{6,4},{7,5},{8,10},{9,11},{10,... | collective-permute-start | bytes 98312 | tf_op jit(solution)/shard_map/ppermute | solution.py:52
  68.1 2.9 %collective-permute-done.17 = bf16[4,32,128]{2,1,0:T(8,128)(2,1)S(1)} collective-permute-done((bf16[4,32,128]{2,1,0:T(8,128)(2,1)S(1)}, bf16[4,32,128]{2,1,0:T(8,128)(2,1)S(1)}, u32[]{:S(2)}, u32[]{:S(2)}) %collective-permute-start.17) | collective-permute-done | bytes 32800 | tf_op jit(solution)/shard_map/ppermute | solution.py:52
  71.0 2.6 %collective-permute-start.21 = (bf16[4,32,128]{2,1,0:T(8,128)(2,1)S(1)}, bf16[4,32,128]{2,1,0:T(8,128)(2,1)S(1)}, u32[]{:S(2)}, u32[]{:S(2)}) collective-permute-start(bf16[4,32,128]{2,1,0:T(8,128)(2,1)S(1)} %add_convert_fusion.1), channel_id=1, source_target_pairs={{0,12},{1,13},{2,14},{3,15},{4,0},{5,1},{6,2},{7,3},{8,4},{9,5},{1... | collective-permute-start | bytes 98312 | tf_op jit(solution)/shard_map/ppermute | solution.py:52
  74.9 3.5 %collective-permute-done.20 = bf16[4,32,128]{2,1,0:T(8,128)(2,1)S(1)} collective-permute-done((bf16[4,32,128]{2,1,0:T(8,128)(2,1)S(1)}, bf16[4,32,128]{2,1,0:T(8,128)(2,1)S(1)}, u32[]{:S(2)}, u32[]{:S(2)}) %collective-permute-start.20) | collective-permute-done | bytes 32800 | tf_op jit(solution)/shard_map/ppermute | solution.py:52
  79.3 2.5 %collective-permute-start.24 = (bf16[4,32,128]{2,1,0:T(8,128)(2,1)S(1)}, bf16[4,32,128]{2,1,0:T(8,128)(2,1)S(1)}, u32[]{:S(2)}, u32[]{:S(2)}) collective-permute-start(bf16[4,32,128]{2,1,0:T(8,128)(2,1)S(1)} %add_convert_fusion.refs_0_), channel_id=1, source_target_pairs={{0,3},{1,0},{2,1},{3,2},{4,7},{5,4},{6,5},{7,6},{8,11},{9,8},{10,9... | collective-permute-start | bytes 98312 | tf_op jit(solution)/shard_map/ppermute | solution.py:52
  83.4 3.2 %collective-permute-done.23.refs_2_ = bf16[4,32,128]{2,1,0:T(8,128)(2,1)S(1)} collective-permute-done((bf16[4,32,128]{2,1,0:T(8,128)(2,1)S(1)}, bf16[4,32,128]{2,1,0:T(8,128)(2,1)S(1)}, u32[]{:S(2)}, u32[]{:S(2)}) %collective-permute-start.23) | collective-permute-done | bytes 32800 | tf_op jit(solution)/shard_map/ppermute | solution.py:52
  88.9 1.5 %collective-permute-start.30 = (bf16[7,32,512]{2,1,0:T(8,128)(2,1)S(1)}, bf16[7,32,512]{2,1,0:T(8,128)(2,1)S(1)}, u32[]{:S(2)}, u32[]{:S(2)}) collective-permute-start(bf16[7,32,512]{2,1,0:T(8,128)(2,1)S(1)} %get-tuple-element.36.refs_7_), channel_id=1, source_target_pairs={{0,224},{16,240},{32,0},{48,16},{64,32},{80,48},{96,64},{112,80},{... | collective-permute-start | bytes 688136 | tf_op jit(solution)/shard_map/ppermute | solution.py:38
  91.9 2.3 %collective-permute-done.26.refs_6_ = bf16[7,32,512]{2,1,0:T(8,128)(2,1)S(1)} collective-permute-done((bf16[7,32,512]{2,1,0:T(8,128)(2,1)S(1)}, bf16[7,32,512]{2,1,0:T(8,128)(2,1)S(1)}, u32[]{:S(2)}, u32[]{:S(2)}) %collective-permute-start.26) | collective-permute-done | bytes 229408 | tf_op jit(solution)/shard_map/ppermute | solution.py:38
  94.5 2.4 %collective-permute-start.31 = (bf16[7,32,512]{2,1,0:T(8,128)(2,1)S(1)}, bf16[7,32,512]{2,1,0:T(8,128)(2,1)S(1)}, u32[]{:S(2)}, u32[]{:S(2)}) collective-permute-start(bf16[7,32,512]{2,1,0:T(8,128)(2,1)S(1)} %collective-permute-done.30.refs_8_), channel_id=1, source_target_pairs={{0,224},{16,240},{32,0},{48,16},{64,32},{80,48},{96,64},{112,80},{... | collective-permute-start | bytes 688136 | tf_op jit(solution)/shard_map/ppermute | solution.py:38
  97.0 2.4 %collective-permute-start.35 = (bf16[7,32,512]{2,1,0:T(8,128)(2,1)S(1)}, bf16[7,32,512]{2,1,0:T(8,128)(2,1)}, u32[]{:S(2)}, u32[]{:S(2)}) collective-permute-start(bf16[7,32,512]{2,1,0:T(8,128)(2,1)S(1)} %collective-permute-done.34.refs_1_), channel_id=1, source_target_pairs={{0,224},{16,240},{32,0},{48,16},{64,32},{80,48},{96,64},{112,80},{... | collective-permute-start | bytes 688136 | tf_op jit(solution)/shard_map/ppermute | solution.py:38
  100.3 4.5 %collective-permute-done.27.refs_5_ = bf16[7,32,512]{2,1,0:T(8,128)(2,1)S(1)} collective-permute-done((bf16[7,32,512]{2,1,0:T(8,128)(2,1)S(1)}, bf16[7,32,512]{2,1,0:T(8,128)(2,1)S(1)}, u32[]{:S(2)}, u32[]{:S(2)}) %collective-permute-start.27) | collective-permute-done | bytes 229408 | tf_op jit(solution)/shard_map/ppermute | solution.py:38
  104.8 2.7 %collective-permute-start.32 = (bf16[7,32,512]{2,1,0:T(8,128)(2,1)S(1)}, bf16[7,32,512]{2,1,0:T(8,128)(2,1)}, u32[]{:S(2)}, u32[]{:S(2)}) collective-permute-start(bf16[7,32,512]{2,1,0:T(8,128)(2,1)S(1)} %collective-permute-done.31.refs_9_), channel_id=1, source_target_pairs={{0,224},{16,240},{32,0},{48,16},{64,32},{80,48},{96,64},{112,80},{... | collective-permute-start | bytes 688136 | tf_op jit(solution)/shard_map/ppermute | solution.py:38
  107.8 1.4 collective-permute-start.36
  109.7 3.6 %collective-permute-done.28.refs_4_ = bf16[7,32,512]{2,1,0:T(8,128)(2,1)} collective-permute-done((bf16[7,32,512]{2,1,0:T(8,128)(2,1)S(1)}, bf16[7,32,512]{2,1,0:T(8,128)(2,1)}, u32[]{:S(2)}, u32[]{:S(2)}) %collective-permute-start.28) | collective-permute-done | bytes 229408 | tf_op jit(solution)/shard_map/ppermute | solution.py:38
  113.4 2.7 %collective-permute-start.33 = (bf16[7,32,512]{2,1,0:T(8,128)(2,1)}, bf16[7,32,512]{2,1,0:T(8,128)(2,1)S(1)}, u32[]{:S(2)}, u32[]{:S(2)}) collective-permute-start(bf16[7,32,512]{2,1,0:T(8,128)(2,1)} %collective-permute-done.32.refs_10_), channel_id=1, source_target_pairs={{0,224},{16,240},{32,0},{48,16},{64,32},{80,48},{96,64},{112,80},{... | collective-permute-start | bytes 688136 | tf_op jit(solution)/shard_map/ppermute | solution.py:38
  118.9 3.7 %gradient_totals.1 = (f32[24,32,512]{2,1,0:T(8,128)S(1)}, f32[24,32,512]{2,1,0:T(8,128)S(1)}) custom-call(s32[192]{0:T(256)S(1)} %reshape.69.place, s32[192]{0:T(256)S(1)} %reshape.70.used, bf16[7,32,512]{2,1,0:T(8,128)(2,1)S(1)} %get-tuple-element.35.refs_0_, bf16[7,32,512]{2,1,0:T(8,128)(2,1)S(1)} %collective-permute-done.34.refs_1_, ...), custom_call_target="tpu_custom_call" | custom-call | bytes 16777216 | tf_op jit(solution)/shard_map/gradient_totals/pallas_call | solution.py:208
  123.9 6.8 %collective-permute-start.40 = (bf16[24,32,512]{2,1,0:T(8,128)(2,1)S(1)}, bf16[24,32,512]{2,1,0:T(8,128)(2,1)S(1)}, u32[]{:S(2)}, u32[]{:S(2)}) collective-permute-start(bf16[24,32,512]{2,1,0:T(8,128)(2,1)S(1)} %gradient_share.1), channel_id=1, source_target_pairs={{0,16},{16,0},{32,48},{48,32},{64,80},{80,64},{96,112},{112,96},{1... | collective-permute-start | bytes 2359304 | tf_op jit(solution)/shard_map/ppermute | solution.py:43
  130.9 2.7 %collective-permute-done.25.other_roll = bf16[16,32,512]{2,1,0:T(8,128)(2,1)S(1)} collective-permute-done((bf16[16,32,512]{2,1,0:T(8,128)(2,1)}, bf16[16,32,512]{2,1,0:T(8,128)(2,1)S(1)}, u32[]{:S(2)}, u32[]{:S(2)}) %collective-permute-start.25) | collective-permute-done | bytes 524320 | tf_op jit(solution)/shard_map/ppermute | solution.py:43
  133.6 1.8 %update_factors.1 = (bf16[4,32,512]{2,1,0:T(8,128)(2,1)}, bf16[4,32,512]{2,1,0:T(8,128)(2,1)}, bf16[8,32,512]{2,1,0:T(8,128)(2,1)}, bf16[8,32,512]{2,1,0:T(8,128)(2,1)}) custom-call(s32[192]{0:T(256)S(1)} %reshape.69.place, s32[192]{0:T(256)S(1)} %reshape.70.used, s32[8]{0:T(128)S(1)} %slice.76.own_ref, bf16[4,32,512]{2,1,0:T(8,128)(2,1)S(1)} %copy-done.3, ...), custom_call_target="tpu_custom_call" | custom-call | bytes 8388608 | tf_op jit(solution)/shard_map/update_factors/pallas_call | solution.py:275
  (119 shorter events, 28.8 us)
Async XLA Ops:
  7.2 128.3 %reduce-scatter.4.cloned.1.call-start = ((), (), s32[]{:S(2)}) async-start(), calls=%async_computation.1 | async-start | bytes 15597568
  21.2 10.9 %collective-permute-start.4 = (bf16[128,512]{1,0:T(8,128)(2,1)S(1)}, bf16[128,512]{1,0:T(8,128)(2,1)S(1)}, u32[]{:S(2)}, u32[]{:S(2)}) collective-permute-start(bf16[128,512]{1,0:T(8,128)(2,1)S(1)} %bitcast.14), channel_id=1, source_target_pairs={{0,32},{16,48},{32,64},{48,80},{64,96},{80,112},{96,128},{112,144}... | collective-permute-start | bytes 393224 | tf_op jit(solution)/shard_map/ppermute | solution.py:38
  23.7 14.4 %collective-permute-start.1 = (bf16[128,512]{1,0:T(8,128)(2,1)S(1)}, bf16[128,512]{1,0:T(8,128)(2,1)S(1)}, u32[]{:S(2)}, u32[]{:S(2)}) collective-permute-start(bf16[128,512]{1,0:T(8,128)(2,1)S(1)} %bitcast.15), channel_id=1, source_target_pairs={{0,224},{16,240},{32,0},{48,16},{64,32},{80,48},{96,64},{112,80},{... | collective-permute-start | bytes 393224 | tf_op jit(solution)/shard_map/ppermute | solution.py:38
  29.0 9.2 %collective-permute-start.12 = (bf16[144,512]{1,0:T(8,128)(2,1)S(1)}, bf16[144,512]{1,0:T(8,128)(2,1)S(1)}, u32[]{:S(2)}, u32[]{:S(2)}) collective-permute-start(bf16[144,512]{1,0:T(8,128)(2,1)S(1)} %fusion.1.refs_8_), channel_id=1, source_target_pairs={{0,32},{16,48},{32,64},{48,80},{64,96},{80,112},{96,128},{112,144}... | collective-permute-start | bytes 442376 | tf_op jit(solution)/shard_map/ppermute | solution.py:38
  29.1 5.6 %collective-permute-start.8 = (bf16[144,512]{1,0:T(8,128)(2,1)S(1)}, bf16[144,512]{1,0:T(8,128)(2,1)S(1)}, u32[]{:S(2)}, u32[]{:S(2)}) collective-permute-start(bf16[144,512]{1,0:T(8,128)(2,1)S(1)} %fusion.1.refs_8_), channel_id=1, source_target_pairs={{0,224},{16,240},{32,0},{48,16},{64,32},{80,48},{96,64},{112,80},{... | collective-permute-start | bytes 442376 | tf_op jit(solution)/shard_map/ppermute | solution.py:38
  32.2 7.4 %collective-permute-start.5 = (bf16[128,512]{1,0:T(8,128)(2,1)S(1)}, bf16[128,512]{1,0:T(8,128)(2,1)S(1)}, u32[]{:S(2)}, u32[]{:S(2)}) collective-permute-start(bf16[128,512]{1,0:T(8,128)(2,1)S(1)} %collective-permute-done.4.refs_7_), channel_id=1, source_target_pairs={{0,32},{16,48},{32,64},{48,80},{64,96},{80,112},{96,128},{112,144}... | collective-permute-start | bytes 393224 | tf_op jit(solution)/shard_map/ppermute | solution.py:38
  34.7 5.5 %collective-permute-start.9 = (bf16[144,512]{1,0:T(8,128)(2,1)S(1)}, bf16[144,512]{1,0:T(8,128)(2,1)S(1)}, u32[]{:S(2)}, u32[]{:S(2)}) collective-permute-start(bf16[144,512]{1,0:T(8,128)(2,1)S(1)} %collective-permute-done.8.refs_9_), channel_id=1, source_target_pairs={{0,224},{16,240},{32,0},{48,16},{64,32},{80,48},{96,64},{112,80},{... | collective-permute-start | bytes 442376 | tf_op jit(solution)/shard_map/ppermute | solution.py:38
  38.1 5.6 %collective-permute-start.2 = (bf16[128,512]{1,0:T(8,128)(2,1)S(1)}, bf16[128,512]{1,0:T(8,128)(2,1)S(1)}, u32[]{:S(2)}, u32[]{:S(2)}) collective-permute-start(bf16[128,512]{1,0:T(8,128)(2,1)S(1)} %collective-permute-done.1.refs_1_), channel_id=1, source_target_pairs={{0,224},{16,240},{32,0},{48,16},{64,32},{80,48},{96,64},{112,80},{... | collective-permute-start | bytes 393224 | tf_op jit(solution)/shard_map/ppermute | solution.py:38
  38.2 8.2 %collective-permute-start.13 = (bf16[144,512]{1,0:T(8,128)(2,1)S(1)}, bf16[144,512]{1,0:T(8,128)(2,1)S(1)}, u32[]{:S(2)}, u32[]{:S(2)}) collective-permute-start(bf16[144,512]{1,0:T(8,128)(2,1)S(1)} %collective-permute-done.12.refs_15_), channel_id=1, source_target_pairs={{0,32},{16,48},{32,64},{48,80},{64,96},{80,112},{96,128},{112,144}... | collective-permute-start | bytes 442376 | tf_op jit(solution)/shard_map/ppermute | solution.py:38
  39.6 6.9 %collective-permute-start.6 = (bf16[128,512]{1,0:T(8,128)(2,1)S(1)}, bf16[128,512]{1,0:T(8,128)(2,1)S(1)}, u32[]{:S(2)}, u32[]{:S(2)}) collective-permute-start(bf16[128,512]{1,0:T(8,128)(2,1)S(1)} %collective-permute-done.5.refs_6_), channel_id=1, source_target_pairs={{0,32},{16,48},{32,64},{48,80},{64,96},{80,112},{96,128},{112,144}... | collective-permute-start | bytes 393224 | tf_op jit(solution)/shard_map/ppermute | solution.py:38
  40.2 6.5 %collective-permute-start.10 = (bf16[144,512]{1,0:T(8,128)(2,1)S(1)}, bf16[144,512]{1,0:T(8,128)(2,1)S(1)}, u32[]{:S(2)}, u32[]{:S(2)}) collective-permute-start(bf16[144,512]{1,0:T(8,128)(2,1)S(1)} %collective-permute-done.9.refs_10_), channel_id=1, source_target_pairs={{0,224},{16,240},{32,0},{48,16},{64,32},{80,48},{96,64},{112,80},{... | collective-permute-start | bytes 442376 | tf_op jit(solution)/shard_map/ppermute | solution.py:38
  43.7 6.2 %collective-permute-start.3 = (bf16[128,512]{1,0:T(8,128)(2,1)S(1)}, bf16[128,512]{1,0:T(8,128)(2,1)S(1)}, u32[]{:S(2)}, u32[]{:S(2)}) collective-permute-start(bf16[128,512]{1,0:T(8,128)(2,1)S(1)} %collective-permute-done.2.refs_2_), channel_id=1, source_target_pairs={{0,224},{16,240},{32,0},{48,16},{64,32},{80,48},{96,64},{112,80},{... | collective-permute-start | bytes 393224 | tf_op jit(solution)/shard_map/ppermute | solution.py:38
  46.4 5.6 %collective-permute-start.14 = (bf16[144,512]{1,0:T(8,128)(2,1)S(1)}, bf16[144,512]{1,0:T(8,128)(2,1)S(1)}, u32[]{:S(2)}, u32[]{:S(2)}) collective-permute-start(bf16[144,512]{1,0:T(8,128)(2,1)S(1)} %collective-permute-done.13.refs_14_), channel_id=1, source_target_pairs={{0,32},{16,48},{32,64},{48,80},{64,96},{80,112},{96,128},{112,144}... | collective-permute-start | bytes 442376 | tf_op jit(solution)/shard_map/ppermute | solution.py:38
  46.4 7.0 %collective-permute-start.7 = (bf16[128,512]{1,0:T(8,128)(2,1)S(1)}, bf16[128,512]{1,0:T(8,128)(2,1)S(1)}, u32[]{:S(2)}, u32[]{:S(2)}) collective-permute-start(bf16[128,512]{1,0:T(8,128)(2,1)S(1)} %collective-permute-done.6.refs_5_), channel_id=1, source_target_pairs={{0,32},{16,48},{32,64},{48,80},{64,96},{80,112},{96,128},{112,144}... | collective-permute-start | bytes 393224 | tf_op jit(solution)/shard_map/ppermute | solution.py:38
  46.7 6.7 %collective-permute-start.11 = (bf16[144,512]{1,0:T(8,128)(2,1)S(1)}, bf16[144,512]{1,0:T(8,128)(2,1)S(1)}, u32[]{:S(2)}, u32[]{:S(2)}) collective-permute-start(bf16[144,512]{1,0:T(8,128)(2,1)S(1)} %collective-permute-done.10.refs_11_), channel_id=1, source_target_pairs={{0,224},{16,240},{32,0},{48,16},{64,32},{80,48},{96,64},{112,80},{... | collective-permute-start | bytes 442376 | tf_op jit(solution)/shard_map/ppermute | solution.py:38
  64.4 6.6 %collective-permute-start.17 = (bf16[4,32,128]{2,1,0:T(8,128)(2,1)S(1)}, bf16[4,32,128]{2,1,0:T(8,128)(2,1)S(1)}, u32[]{:S(2)}, u32[]{:S(2)}) collective-permute-start(bf16[4,32,128]{2,1,0:T(8,128)(2,1)S(1)} %get-tuple-element.28), channel_id=1, source_target_pairs={{0,2},{1,3},{2,0},{3,1},{4,6},{5,7},{6,4},{7,5},{8,10},{9,11},{10,... | collective-permute-start | bytes 98312 | tf_op jit(solution)/shard_map/ppermute | solution.py:52
  81.8 5.3 %collective-permute-start.22 = (bf16[4,32,128]{2,1,0:T(8,128)(2,1)S(1)}, bf16[4,32,128]{2,1,0:T(8,128)(2,1)S(1)}, u32[]{:S(2)}, u32[]{:S(2)}) collective-permute-start(bf16[4,32,128]{2,1,0:T(8,128)(2,1)S(1)} %add_convert_fusion.refs_0_), channel_id=1, source_target_pairs={{0,1},{1,2},{2,3},{3,0},{4,5},{5,6},{6,7},{7,4},{8,9},{9,10},{10,1... | collective-permute-start | bytes 98312 | tf_op jit(solution)/shard_map/ppermute | solution.py:52
  87.5 6.6 %collective-permute-start.26 = (bf16[7,32,512]{2,1,0:T(8,128)(2,1)S(1)}, bf16[7,32,512]{2,1,0:T(8,128)(2,1)S(1)}, u32[]{:S(2)}, u32[]{:S(2)}) collective-permute-start(bf16[7,32,512]{2,1,0:T(8,128)(2,1)S(1)} %get-tuple-element.35.refs_0_), channel_id=1, source_target_pairs={{0,32},{16,48},{32,64},{48,80},{64,96},{80,112},{96,128},{112,144}... | collective-permute-start | bytes 688136 | tf_op jit(solution)/shard_map/ppermute | solution.py:38
  88.9 5.6 %collective-permute-start.30 = (bf16[7,32,512]{2,1,0:T(8,128)(2,1)S(1)}, bf16[7,32,512]{2,1,0:T(8,128)(2,1)S(1)}, u32[]{:S(2)}, u32[]{:S(2)}) collective-permute-start(bf16[7,32,512]{2,1,0:T(8,128)(2,1)S(1)} %get-tuple-element.36.refs_7_), channel_id=1, source_target_pairs={{0,224},{16,240},{32,0},{48,16},{64,32},{80,48},{96,64},{112,80},{... | collective-permute-start | bytes 688136 | tf_op jit(solution)/shard_map/ppermute | solution.py:38
  90.4 6.6 %collective-permute-start.34 = (bf16[7,32,512]{2,1,0:T(8,128)(2,1)S(1)}, bf16[7,32,512]{2,1,0:T(8,128)(2,1)S(1)}, u32[]{:S(2)}, u32[]{:S(2)}) collective-permute-start(bf16[7,32,512]{2,1,0:T(8,128)(2,1)S(1)} %get-tuple-element.35.refs_0_), channel_id=1, source_target_pairs={{0,224},{16,240},{32,0},{48,16},{64,32},{80,48},{96,64},{112,80},{... | collective-permute-start | bytes 688136 | tf_op jit(solution)/shard_map/ppermute | solution.py:38
  91.8 8.5 %collective-permute-start.37 = (bf16[7,32,512]{2,1,0:T(8,128)(2,1)S(1)}, bf16[7,32,512]{2,1,0:T(8,128)(2,1)S(1)}, u32[]{:S(2)}, u32[]{:S(2)}) collective-permute-start(bf16[7,32,512]{2,1,0:T(8,128)(2,1)S(1)} %get-tuple-element.36.refs_7_), channel_id=1, source_target_pairs={{0,32},{16,48},{32,64},{48,80},{64,96},{80,112},{96,128},{112,144}... | collective-permute-start | bytes 688136 | tf_op jit(solution)/shard_map/ppermute | solution.py:38
  94.1 10.7 %collective-permute-start.27 = (bf16[7,32,512]{2,1,0:T(8,128)(2,1)S(1)}, bf16[7,32,512]{2,1,0:T(8,128)(2,1)S(1)}, u32[]{:S(2)}, u32[]{:S(2)}) collective-permute-start(bf16[7,32,512]{2,1,0:T(8,128)(2,1)S(1)} %collective-permute-done.26.refs_6_), channel_id=1, source_target_pairs={{0,32},{16,48},{32,64},{48,80},{64,96},{80,112},{96,128},{112,144}... | collective-permute-start | bytes 688136 | tf_op jit(solution)/shard_map/ppermute | solution.py:38
  94.5 10.3 %collective-permute-start.31 = (bf16[7,32,512]{2,1,0:T(8,128)(2,1)S(1)}, bf16[7,32,512]{2,1,0:T(8,128)(2,1)S(1)}, u32[]{:S(2)}, u32[]{:S(2)}) collective-permute-start(bf16[7,32,512]{2,1,0:T(8,128)(2,1)S(1)} %collective-permute-done.30.refs_8_), channel_id=1, source_target_pairs={{0,224},{16,240},{32,0},{48,16},{64,32},{80,48},{96,64},{112,80},{... | collective-permute-start | bytes 688136 | tf_op jit(solution)/shard_map/ppermute | solution.py:38
  97.0 10.8 %collective-permute-start.35 = (bf16[7,32,512]{2,1,0:T(8,128)(2,1)S(1)}, bf16[7,32,512]{2,1,0:T(8,128)(2,1)}, u32[]{:S(2)}, u32[]{:S(2)}) collective-permute-start(bf16[7,32,512]{2,1,0:T(8,128)(2,1)S(1)} %collective-permute-done.34.refs_1_), channel_id=1, source_target_pairs={{0,224},{16,240},{32,0},{48,16},{64,32},{80,48},{96,64},{112,80},{... | collective-permute-start | bytes 688136 | tf_op jit(solution)/shard_map/ppermute | solution.py:38
  100.3 9.5 %collective-permute-start.38 = (bf16[7,32,512]{2,1,0:T(8,128)(2,1)S(1)}, bf16[7,32,512]{2,1,0:T(8,128)(2,1)}, u32[]{:S(2)}, u32[]{:S(2)}) collective-permute-start(bf16[7,32,512]{2,1,0:T(8,128)(2,1)S(1)} %collective-permute-done.37.refs_13_), channel_id=1, source_target_pairs={{0,32},{16,48},{32,64},{48,80},{64,96},{80,112},{96,128},{112,144}... | collective-permute-start | bytes 688136 | tf_op jit(solution)/shard_map/ppermute | solution.py:38
  104.8 8.5 %collective-permute-start.28 = (bf16[7,32,512]{2,1,0:T(8,128)(2,1)S(1)}, bf16[7,32,512]{2,1,0:T(8,128)(2,1)}, u32[]{:S(2)}, u32[]{:S(2)}) collective-permute-start(bf16[7,32,512]{2,1,0:T(8,128)(2,1)S(1)} %collective-permute-done.27.refs_5_), channel_id=1, source_target_pairs={{0,32},{16,48},{32,64},{48,80},{64,96},{80,112},{96,128},{112,144}... | collective-permute-start | bytes 688136 | tf_op jit(solution)/shard_map/ppermute | solution.py:38
  104.8 8.5 %collective-permute-start.32 = (bf16[7,32,512]{2,1,0:T(8,128)(2,1)S(1)}, bf16[7,32,512]{2,1,0:T(8,128)(2,1)}, u32[]{:S(2)}, u32[]{:S(2)}) collective-permute-start(bf16[7,32,512]{2,1,0:T(8,128)(2,1)S(1)} %collective-permute-done.31.refs_9_), channel_id=1, source_target_pairs={{0,224},{16,240},{32,0},{48,16},{64,32},{80,48},{96,64},{112,80},{... | collective-permute-start | bytes 688136 | tf_op jit(solution)/shard_map/ppermute | solution.py:38
  107.8 9.9 %collective-permute-start.36 = (bf16[7,32,512]{2,1,0:T(8,128)(2,1)}, bf16[7,32,512]{2,1,0:T(8,128)(2,1)}, u32[]{:S(2)}, u32[]{:S(2)}) collective-permute-start(bf16[7,32,512]{2,1,0:T(8,128)(2,1)} %collective-permute-done.35.refs_2_), channel_id=1, source_target_pairs={{0,224},{16,240},{32,0},{48,16},{64,32},{80,48},{96,64},{112,80},{... | collective-permute-start | bytes 688136 | tf_op jit(solution)/shard_map/ppermute | solution.py:38
  109.7 9.2 %collective-permute-start.39 = (bf16[7,32,512]{2,1,0:T(8,128)(2,1)}, bf16[7,32,512]{2,1,0:T(8,128)(2,1)}, u32[]{:S(2)}, u32[]{:S(2)}) collective-permute-start(bf16[7,32,512]{2,1,0:T(8,128)(2,1)} %collective-permute-done.38.refs_12_), channel_id=1, source_target_pairs={{0,32},{16,48},{32,64},{48,80},{64,96},{80,112},{96,128},{112,144}... | collective-permute-start | bytes 688136 | tf_op jit(solution)/shard_map/ppermute | solution.py:38
  113.4 9.7 %collective-permute-start.29 = (bf16[7,32,512]{2,1,0:T(8,128)(2,1)}, bf16[7,32,512]{2,1,0:T(8,128)(2,1)S(1)}, u32[]{:S(2)}, u32[]{:S(2)}) collective-permute-start(bf16[7,32,512]{2,1,0:T(8,128)(2,1)} %collective-permute-done.28.refs_4_), channel_id=1, source_target_pairs={{0,32},{16,48},{32,64},{48,80},{64,96},{80,112},{96,128},{112,144}... | collective-permute-start | bytes 688136 | tf_op jit(solution)/shard_map/ppermute | solution.py:38
  113.4 9.7 %collective-permute-start.33 = (bf16[7,32,512]{2,1,0:T(8,128)(2,1)}, bf16[7,32,512]{2,1,0:T(8,128)(2,1)S(1)}, u32[]{:S(2)}, u32[]{:S(2)}) collective-permute-start(bf16[7,32,512]{2,1,0:T(8,128)(2,1)} %collective-permute-done.32.refs_10_), channel_id=1, source_target_pairs={{0,224},{16,240},{32,0},{48,16},{64,32},{80,48},{96,64},{112,80},{... | collective-permute-start | bytes 688136 | tf_op jit(solution)/shard_map/ppermute | solution.py:38
  123.9 9.7 %collective-permute-start.40 = (bf16[24,32,512]{2,1,0:T(8,128)(2,1)S(1)}, bf16[24,32,512]{2,1,0:T(8,128)(2,1)S(1)}, u32[]{:S(2)}, u32[]{:S(2)}) collective-permute-start(bf16[24,32,512]{2,1,0:T(8,128)(2,1)S(1)} %gradient_share.1), channel_id=1, source_target_pairs={{0,16},{16,0},{32,48},{48,32},{64,80},{80,64},{96,112},{112,96},{1... | collective-permute-start | bytes 2359304 | tf_op jit(solution)/shard_map/ppermute | solution.py:43
  (21 other events, 231.5 us)
Sparse Core Ops, SparseCore 0:
  20.5 112.7 reduce-scatter.3

commit v3 on v2

--- a/solution.py
+++ b/solution.py
@@ -15,7 +15,7 @@
 SIDE = 4
 LEARN_RATE = 0.25
 TILE = 2048
-BASE_VMEM = 58 * 2**20
+BASE_VMEM = 54 * 2**20
 SCALE = 1.0 / math.sqrt(INPUT_FEATURES * ADAPTER_RANK)
 
 BF = jnp.bfloat16
@@ -185,7 +185,7 @@
 
 
 def total_kernel(needs, place, used, *refs):
-    a_refs, b_refs, (mine_ref, other_ref) = refs[:7], refs[7:14], refs[14:]
+    a_refs, b_refs, (_, mine_ref, other_ref) = refs[:7], refs[7:14], refs[14:]
 
     def one(need, parts):
         value = None
@@ -203,17 +203,17 @@
         other_ref[needs + need] = one(needs + need, b_refs)
 
 
-def total(place, used, parts_a, parts_b, needs):
+def total(place, used, parts_a, parts_b, token, needs):
     shape = jax.ShapeDtypeStruct((2 * needs,) + parts_a[0].shape[1:], F32)
     return pl.pallas_call(
         functools.partial(total_kernel, needs),
         out_shape=(shape, shape),
-        in_specs=[SMEM()] * 2 + [VMEM()] * 14,
+        in_specs=[SMEM()] * 2 + [VMEM()] * 15,
         out_specs=(VMEM(),) * 2,
         compiler_params=PARAMS,
         cost_estimate=pl.CostEstimate(flops=0, bytes_accessed=16 * 2**20, transcendentals=0),
         name="gradient_totals",
-    )(place, used, *parts_a, *parts_b)
+    )(place, used, *parts_a, *parts_b, token)
 
 
 def far_term(place, used, far_ref, need):
@@ -314,8 +314,8 @@
     )(grad, weight)
 
 
-def finish_kernel(blocks, ranks_ref, chosen_ref, base_ref, out_ref):
-    for n in range(blocks):
+def finish_kernel(ranks_ref, chosen_ref, base_ref, out_ref):
+    for n in range(ranks_ref.shape[0]):
         rows = pl.ds(n * BLOCK, BLOCK)
         term = lax.dot_general(
             ranks_ref[n], chosen_ref[n], (((0,), (0,)), ((), ())), preferred_element_type=F32
@@ -324,13 +324,18 @@
 
 
 def finish(ranks, chosen, base):
-    blocks = chosen.shape[0]
-    return pl.pallas_call(
-        functools.partial(finish_kernel, blocks),
+    blocks, rank, width = chosen.shape
+    return pl.pallas_call(
+        finish_kernel,
+        grid=(blocks,),
         out_shape=jax.ShapeDtypeStruct(base.shape[1:], BF),
-        in_specs=[VMEM()] * 3,
-        out_specs=VMEM(),
-        compiler_params=PARAMS,
+        in_specs=[
+            pl.BlockSpec((1, rank, BLOCK), lambda n: (n, 0, 0)),
+            pl.BlockSpec((1, rank, width), lambda n: (n, 0, 0)),
+            pl.BlockSpec((1, BLOCK, width), lambda n: (0, n, 0)),
+        ],
+        out_specs=pl.BlockSpec((BLOCK, width), lambda n: (n, 0)),
+        compiler_params=pltpu.CompilerParams(vmem_limit_bytes=BASE_VMEM),
         cost_estimate=pl.CostEstimate(flops=0, bytes_accessed=4 * 2**20, transcendentals=0),
         name="input_gradient",
     )(ranks, chosen, base)
@@ -414,7 +419,7 @@
     parts_a, parts_b = ring_gather(part_a, part_b)
     near = order[:7]
     mine_total, other_total = total(
-        source, used, [parts_a[k] for k in near], [parts_b[k] for k in near], slots + rolls
+        source, used, [parts_a[k] for k in near], [parts_b[k] for k in near], got_roll, slots + rolls
     )
     got_total = core_swap(share(source, used, parts_a[4], parts_b[4], other_total))
     new_a, new_b, roll_a, roll_b = update(

time: 145 us -> 151 us (1.041)
  waiting for transfers between devices: 38.4 us -> 33.8 us
  Pallas kernels: 24.1 us -> 28.2 us
  starting transfers between devices: 62.7 us -> 66 us
  local copies, waits for them, and re-layouts: 4.42 us -> 6.8 us
    pallas_call x1, Pallas kernels: 1.34 us -> 5.5 us  [finish(): pl.pallas_call(finish_kernel, grid=(blocks,), out_shape=jax.ShapeDtypeStr...]
    ppermute x4, starting transfers between devices: 11.2 us -> 14.6 us  [core_swap(): return lax.ppermute(x, 'dp', [(d, d ^ 1) for d in range(n)])]
    ppermute x28, waiting for transfers between devices: 21.7 us -> 18.5 us  [z_hop(): return lax.ppermute(x, 'dp', perm)]
    unnamed x23 -> x31, local copies, waits for them, and re-layouts: 3.66 us -> 6.03 us
  transfers between devices with their start and end apart: 42 -> 42, of which waited for: 23 -> 20; matrix products, arithmetic and copies ran while one was open for 1% -> 2% of each run, Pallas kernels for 7% -> 6%
where the time goes in v3:
time: 151 us
  starting transfers between devices  66 us (44%)
  waiting for transfers between devices  33.8 us (22%)
  Pallas kernels  28.2 us (19%)
  between operations  14.3 us (9%)
  local copies, waits for them, and re-layouts  6.8 us (5%)
  other arithmetic  1.66 us (1%)
    ppermute x28, starting transfers between devices, z_hop(): return lax.ppermute(x, 'dp', perm)  39.5 us
    ppermute x28, waiting for transfers between devices, z_hop(): return lax.ppermute(x, 'dp', perm)  18.5 us
    ppermute x4, starting transfers between devices, core_swap(): return lax.ppermute(x, 'dp', [(d, d ^ 1) for d in range(n)])  14.6 us
    pallas_call x1, Pallas kernels, products(): pl.pallas_call(products_kernel, grid=(columns // tile,), out_shape=jax.Sh...  13.1 us
    ppermute x9, starting transfers between devices, plane_hop(): return lax.ppermute(x, 'tensor', perm)  11.9 us
    ppermute x9, waiting for transfers between devices, plane_hop(): return lax.ppermute(x, 'tensor', perm)  11.7 us
    unnamed x31, local copies, waits for them, and re-layouts  6.03 us
    pallas_call x1, Pallas kernels, finish(): pl.pallas_call(finish_kernel, grid=(blocks,), out_shape=jax.ShapeDtypeStr...  5.5 us
  transfers between devices with their start and end apart: 42, of which 20 were waited for; matrix products, arithmetic and copies ran while one was open for 2% of the time, Pallas kernels for 6%

profile of v3, /device:TPU:1, one launch (start us, length us, event | category | flops | bytes accessed | tf_op | source)
XLA Modules:
  0.0 150.8 jit_solution(5185235198740603218)
XLA Ops:
  7.2 13.1 %base_products.1 = bf16[16,896,512]{2,1,0:T(8,128)(2,1)} custom-call(bf16[896,512]{1,0:T(8,128)(2,1)} %grad_ref.3, bf16[8192,512]{1,0:T(8,128)(2,1)} %weight_ref.1), custom_call_target="tpu_custom_call" | custom-call | flops 7516192768 | bytes 25165824 | tf_op jit(solution)/shard_map/base_products/pallas_call | solution.py:300
  21.2 2.5 %collective-permute-start.4 = (bf16[128,512]{1,0:T(8,128)(2,1)S(1)}, bf16[128,512]{1,0:T(8,128)(2,1)S(1)}, u32[]{:S(2)}, u32[]{:S(2)}) collective-permute-start(bf16[128,512]{1,0:T(8,128)(2,1)S(1)} %bitcast.14), channel_id=1, source_target_pairs={{0,32},{16,48},{32,64},{48,80},{64,96},{80,112},{96,128},{112,144}... | collective-permute-start | bytes 393224 | tf_op jit(solution)/shard_map/ppermute | solution.py:38
  23.7 3.9 %collective-permute-start.1 = (bf16[128,512]{1,0:T(8,128)(2,1)S(1)}, bf16[128,512]{1,0:T(8,128)(2,1)S(1)}, u32[]{:S(2)}, u32[]{:S(2)}) collective-permute-start(bf16[128,512]{1,0:T(8,128)(2,1)S(1)} %bitcast.15), channel_id=1, source_target_pairs={{0,224},{16,240},{32,0},{48,16},{64,32},{80,48},{96,64},{112,80},{... | collective-permute-start | bytes 393224 | tf_op jit(solution)/shard_map/ppermute | solution.py:38
  29.1 2.7 %collective-permute-start.8 = (bf16[144,512]{1,0:T(8,128)(2,1)S(1)}, bf16[144,512]{1,0:T(8,128)(2,1)S(1)}, u32[]{:S(2)}, u32[]{:S(2)}) collective-permute-start(bf16[144,512]{1,0:T(8,128)(2,1)S(1)} %fusion.1.refs_8_), channel_id=1, source_target_pairs={{0,224},{16,240},{32,0},{48,16},{64,32},{80,48},{96,64},{112,80},{... | collective-permute-start | bytes 442376 | tf_op jit(solution)/shard_map/ppermute | solution.py:38
  32.3 2.4 %collective-permute-done.8.refs_9_ = bf16[144,512]{1,0:T(8,128)(2,1)S(1)} collective-permute-done((bf16[144,512]{1,0:T(8,128)(2,1)S(1)}, bf16[144,512]{1,0:T(8,128)(2,1)S(1)}, u32[]{:S(2)}, u32[]{:S(2)}) %collective-permute-start.8) | collective-permute-done | bytes 147488 | tf_op jit(solution)/shard_map/ppermute | solution.py:38
  34.7 3.4 %collective-permute-start.9 = (bf16[144,512]{1,0:T(8,128)(2,1)S(1)}, bf16[144,512]{1,0:T(8,128)(2,1)S(1)}, u32[]{:S(2)}, u32[]{:S(2)}) collective-permute-start(bf16[144,512]{1,0:T(8,128)(2,1)S(1)} %collective-permute-done.8.refs_9_), channel_id=1, source_target_pairs={{0,224},{16,240},{32,0},{48,16},{64,32},{80,48},{96,64},{112,80},{... | collective-permute-start | bytes 442376 | tf_op jit(solution)/shard_map/ppermute | solution.py:38
  40.2 3.5 %collective-permute-start.10 = (bf16[144,512]{1,0:T(8,128)(2,1)S(1)}, bf16[144,512]{1,0:T(8,128)(2,1)S(1)}, u32[]{:S(2)}, u32[]{:S(2)}) collective-permute-start(bf16[144,512]{1,0:T(8,128)(2,1)S(1)} %collective-permute-done.9.refs_10_), channel_id=1, source_target_pairs={{0,224},{16,240},{32,0},{48,16},{64,32},{80,48},{96,64},{112,80},{... | collective-permute-start | bytes 442376 | tf_op jit(solution)/shard_map/ppermute | solution.py:38
  43.7 2.7 %collective-permute-start.3 = (bf16[128,512]{1,0:T(8,128)(2,1)S(1)}, bf16[128,512]{1,0:T(8,128)(2,1)S(1)}, u32[]{:S(2)}, u32[]{:S(2)}) collective-permute-start(bf16[128,512]{1,0:T(8,128)(2,1)S(1)} %collective-permute-done.2.refs_2_), channel_id=1, source_target_pairs={{0,224},{16,240},{32,0},{48,16},{64,32},{80,48},{96,64},{112,80},{... | collective-permute-start | bytes 393224 | tf_op jit(solution)/shard_map/ppermute | solution.py:38
  46.7 3.0 %collective-permute-start.11 = (bf16[144,512]{1,0:T(8,128)(2,1)S(1)}, bf16[144,512]{1,0:T(8,128)(2,1)S(1)}, u32[]{:S(2)}, u32[]{:S(2)}) collective-permute-start(bf16[144,512]{1,0:T(8,128)(2,1)S(1)} %collective-permute-done.10.refs_11_), channel_id=1, source_target_pairs={{0,224},{16,240},{32,0},{48,16},{64,32},{80,48},{96,64},{112,80},{... | collective-permute-start | bytes 442376 | tf_op jit(solution)/shard_map/ppermute | solution.py:38
  49.9 2.2 %collective-permute-done.14.refs_13_ = bf16[144,512]{1,0:T(8,128)(2,1)S(1)} collective-permute-done((bf16[144,512]{1,0:T(8,128)(2,1)S(1)}, bf16[144,512]{1,0:T(8,128)(2,1)S(1)}, u32[]{:S(2)}, u32[]{:S(2)}) %collective-permute-start.14) | collective-permute-done | bytes 147488 | tf_op jit(solution)/shard_map/ppermute | solution.py:38
  57.3 3.3 %collective-permute-start.15 = (bf16[16,32,512]{2,1,0:T(8,128)(2,1)}, bf16[16,32,512]{2,1,0:T(8,128)(2,1)S(1)}, u32[]{:S(2)}, u32[]{:S(2)}) collective-permute-start(bf16[16,32,512]{2,1,0:T(8,128)(2,1)} %get-tuple-element.25), channel_id=1, source_target_pairs={{0,16},{16,0},{32,48},{48,32},{64,80},{80,64},{96,112},{112,96},{1... | collective-permute-start | bytes 1572872 | tf_op jit(solution)/shard_map/ppermute | solution.py:43
  60.6 1.7 %collective-permute-done.15.other_ref = bf16[16,32,512]{2,1,0:T(8,128)(2,1)S(1)} collective-permute-done((bf16[16,32,512]{2,1,0:T(8,128)(2,1)}, bf16[16,32,512]{2,1,0:T(8,128)(2,1)S(1)}, u32[]{:S(2)}, u32[]{:S(2)}) %collective-permute-start.15) | collective-permute-done | bytes 524320 | tf_op jit(solution)/shard_map/ppermute | solution.py:43
  65.6 2.6 %collective-permute-start.17 = (bf16[4,32,128]{2,1,0:T(8,128)(2,1)S(1)}, bf16[4,32,128]{2,1,0:T(8,128)(2,1)S(1)}, u32[]{:S(2)}, u32[]{:S(2)}) collective-permute-start(bf16[4,32,128]{2,1,0:T(8,128)(2,1)S(1)} %get-tuple-element.28), channel_id=1, source_target_pairs={{0,2},{1,3},{2,0},{3,1},{4,6},{5,7},{6,4},{7,5},{8,10},{9,11},{10,... | collective-permute-start | bytes 98312 | tf_op jit(solution)/shard_map/ppermute | solution.py:52
  69.3 2.8 %collective-permute-done.17 = bf16[4,32,128]{2,1,0:T(8,128)(2,1)S(1)} collective-permute-done((bf16[4,32,128]{2,1,0:T(8,128)(2,1)S(1)}, bf16[4,32,128]{2,1,0:T(8,128)(2,1)S(1)}, u32[]{:S(2)}, u32[]{:S(2)}) %collective-permute-start.17) | collective-permute-done | bytes 32800 | tf_op jit(solution)/shard_map/ppermute | solution.py:52
  72.1 2.6 %collective-permute-start.21 = (bf16[4,32,128]{2,1,0:T(8,128)(2,1)S(1)}, bf16[4,32,128]{2,1,0:T(8,128)(2,1)S(1)}, u32[]{:S(2)}, u32[]{:S(2)}) collective-permute-start(bf16[4,32,128]{2,1,0:T(8,128)(2,1)S(1)} %add_convert_fusion.1), channel_id=1, source_target_pairs={{0,12},{1,13},{2,14},{3,15},{4,0},{5,1},{6,2},{7,3},{8,4},{9,5},{1... | collective-permute-start | bytes 98312 | tf_op jit(solution)/shard_map/ppermute | solution.py:52
  76.1 3.4 %collective-permute-done.20 = bf16[4,32,128]{2,1,0:T(8,128)(2,1)S(1)} collective-permute-done((bf16[4,32,128]{2,1,0:T(8,128)(2,1)S(1)}, bf16[4,32,128]{2,1,0:T(8,128)(2,1)S(1)}, u32[]{:S(2)}, u32[]{:S(2)}) %collective-permute-start.20) | collective-permute-done | bytes 32800 | tf_op jit(solution)/shard_map/ppermute | solution.py:52
  80.5 2.5 %collective-permute-start.24 = (bf16[4,32,128]{2,1,0:T(8,128)(2,1)S(1)}, bf16[4,32,128]{2,1,0:T(8,128)(2,1)S(1)}, u32[]{:S(2)}, u32[]{:S(2)}) collective-permute-start(bf16[4,32,128]{2,1,0:T(8,128)(2,1)S(1)} %add_convert_fusion.refs_0_), channel_id=1, source_target_pairs={{0,3},{1,0},{2,1},{3,2},{4,7},{5,4},{6,5},{7,6},{8,11},{9,8},{10,9... | collective-permute-start | bytes 98312 | tf_op jit(solution)/shard_map/ppermute | solution.py:52
  84.5 3.1 %collective-permute-done.23.refs_2_ = bf16[4,32,128]{2,1,0:T(8,128)(2,1)S(1)} collective-permute-done((bf16[4,32,128]{2,1,0:T(8,128)(2,1)S(1)}, bf16[4,32,128]{2,1,0:T(8,128)(2,1)S(1)}, u32[]{:S(2)}, u32[]{:S(2)}) %collective-permute-start.23) | collective-permute-done | bytes 32800 | tf_op jit(solution)/shard_map/ppermute | solution.py:52
  90.3 1.7 %collective-permute-start.30 = (bf16[7,32,512]{2,1,0:T(8,128)(2,1)S(1)}, bf16[7,32,512]{2,1,0:T(8,128)(2,1)S(1)}, u32[]{:S(2)}, u32[]{:S(2)}) collective-permute-start(bf16[7,32,512]{2,1,0:T(8,128)(2,1)S(1)} %get-tuple-element.36.refs_7_), channel_id=1, source_target_pairs={{0,224},{16,240},{32,0},{48,16},{64,32},{80,48},{96,64},{112,80},{... | collective-permute-start | bytes 688136 | tf_op jit(solution)/shard_map/ppermute | solution.py:38
  93.5 2.3 %collective-permute-done.26.refs_6_ = bf16[7,32,512]{2,1,0:T(8,128)(2,1)S(1)} collective-permute-done((bf16[7,32,512]{2,1,0:T(8,128)(2,1)S(1)}, bf16[7,32,512]{2,1,0:T(8,128)(2,1)S(1)}, u32[]{:S(2)}, u32[]{:S(2)}) %collective-permute-start.26) | collective-permute-done | bytes 229408 | tf_op jit(solution)/shard_map/ppermute | solution.py:38
  96.2 2.3 %collective-permute-start.31 = (bf16[7,32,512]{2,1,0:T(8,128)(2,1)S(1)}, bf16[7,32,512]{2,1,0:T(8,128)(2,1)S(1)}, u32[]{:S(2)}, u32[]{:S(2)}) collective-permute-start(bf16[7,32,512]{2,1,0:T(8,128)(2,1)S(1)} %collective-permute-done.30.refs_8_), channel_id=1, source_target_pairs={{0,224},{16,240},{32,0},{48,16},{64,32},{80,48},{96,64},{112,80},{... | collective-permute-start | bytes 688136 | tf_op jit(solution)/shard_map/ppermute | solution.py:38
  98.7 2.3 %collective-permute-start.35 = (bf16[7,32,512]{2,1,0:T(8,128)(2,1)S(1)}, bf16[7,32,512]{2,1,0:T(8,128)(2,1)}, u32[]{:S(2)}, u32[]{:S(2)}) collective-permute-start(bf16[7,32,512]{2,1,0:T(8,128)(2,1)S(1)} %collective-permute-done.34.refs_1_), channel_id=1, source_target_pairs={{0,224},{16,240},{32,0},{48,16},{64,32},{80,48},{96,64},{112,80},{... | collective-permute-start | bytes 688136 | tf_op jit(solution)/shard_map/ppermute | solution.py:38
  101.7 4.4 %collective-permute-done.27.refs_5_ = bf16[7,32,512]{2,1,0:T(8,128)(2,1)S(1)} collective-permute-done((bf16[7,32,512]{2,1,0:T(8,128)(2,1)S(1)}, bf16[7,32,512]{2,1,0:T(8,128)(2,1)S(1)}, u32[]{:S(2)}, u32[]{:S(2)}) %collective-permute-start.27) | collective-permute-done | bytes 229408 | tf_op jit(solution)/shard_map/ppermute | solution.py:38
  106.1 2.7 %collective-permute-start.32 = (bf16[7,32,512]{2,1,0:T(8,128)(2,1)S(1)}, bf16[7,32,512]{2,1,0:T(8,128)(2,1)}, u32[]{:S(2)}, u32[]{:S(2)}) collective-permute-start(bf16[7,32,512]{2,1,0:T(8,128)(2,1)S(1)} %collective-permute-done.31.refs_9_), channel_id=1, source_target_pairs={{0,224},{16,240},{32,0},{48,16},{64,32},{80,48},{96,64},{112,80},{... | collective-permute-start | bytes 688136 | tf_op jit(solution)/shard_map/ppermute | solution.py:38
  109.5 8.2 %collective-permute-start.25 = (bf16[16,32,512]{2,1,0:T(8,128)(2,1)}, bf16[16,32,512]{2,1,0:T(8,128)(2,1)S(1)}, u32[]{:S(2)}, u32[]{:S(2)}) collective-permute-start(bf16[16,32,512]{2,1,0:T(8,128)(2,1)} %copy-done.11), channel_id=1, source_target_pairs={{0,16},{16,0},{32,48},{48,32},{64,80},{80,64},{96,112},{112,96},{1... | collective-permute-start | bytes 1572872 | tf_op jit(solution)/shard_map/ppermute | solution.py:43
  120.1 2.6 %collective-permute-start.33 = (bf16[7,32,512]{2,1,0:T(8,128)(2,1)}, bf16[7,32,512]{2,1,0:T(8,128)(2,1)S(1)}, u32[]{:S(2)}, u32[]{:S(2)}) collective-permute-start(bf16[7,32,512]{2,1,0:T(8,128)(2,1)} %collective-permute-done.32.refs_10_), channel_id=1, source_target_pairs={{0,224},{16,240},{32,0},{48,16},{64,32},{80,48},{96,64},{112,80},{... | collective-permute-start | bytes 688136 | tf_op jit(solution)/shard_map/ppermute | solution.py:38
  123.2 2.9 %collective-permute-done.36.refs_3_ = bf16[7,32,512]{2,1,0:T(8,128)(2,1)} collective-permute-done((bf16[7,32,512]{2,1,0:T(8,128)(2,1)}, bf16[7,32,512]{2,1,0:T(8,128)(2,1)}, u32[]{:S(2)}, u32[]{:S(2)}) %collective-permute-start.36) | collective-permute-done | bytes 229408 | tf_op jit(solution)/shard_map/ppermute | solution.py:38
  127.8 3.6 %gradient_totals.1 = (f32[24,32,512]{2,1,0:T(8,128)S(1)}, f32[24,32,512]{2,1,0:T(8,128)S(1)}) custom-call(s32[192]{0:T(256)S(1)} %reshape.69.place, s32[192]{0:T(256)S(1)} %reshape.70.used, bf16[7,32,512]{2,1,0:T(8,128)(2,1)S(1)} %get-tuple-element.35.refs_0_, bf16[7,32,512]{2,1,0:T(8,128)(2,1)S(1)} %collective-permute-done.34.refs_1_, ...), custom_call_target="tpu_custom_call" | custom-call | bytes 16777216 | tf_op jit(solution)/shard_map/gradient_totals/pallas_call | solution.py:208
  132.6 2.0 %collective-permute-start.40 = (bf16[24,32,512]{2,1,0:T(8,128)(2,1)S(1)}, bf16[24,32,512]{2,1,0:T(8,128)(2,1)S(1)}, u32[]{:S(2)}, u32[]{:S(2)}) collective-permute-start(bf16[24,32,512]{2,1,0:T(8,128)(2,1)S(1)} %gradient_share.1), channel_id=1, source_target_pairs={{0,16},{16,0},{32,48},{48,32},{64,80},{80,64},{96,112},{112,96},{1... | collective-permute-start | bytes 2359304 | tf_op jit(solution)/shard_map/ppermute | solution.py:43
  134.7 1.8 %collective-permute-done.40.other_ref = bf16[24,32,512]{2,1,0:T(8,128)(2,1)S(1)} collective-permute-done((bf16[24,32,512]{2,1,0:T(8,128)(2,1)S(1)}, bf16[24,32,512]{2,1,0:T(8,128)(2,1)S(1)}, u32[]{:S(2)}, u32[]{:S(2)}) %collective-permute-start.40) | collective-permute-done | bytes 786464 | tf_op jit(solution)/shard_map/ppermute | solution.py:43
  136.6 1.8 %update_factors.1 = (bf16[4,32,512]{2,1,0:T(8,128)(2,1)}, bf16[4,32,512]{2,1,0:T(8,128)(2,1)}, bf16[8,32,512]{2,1,0:T(8,128)(2,1)}, bf16[8,32,512]{2,1,0:T(8,128)(2,1)}) custom-call(s32[192]{0:T(256)S(1)} %reshape.69.place, s32[192]{0:T(256)S(1)} %reshape.70.used, s32[8]{0:T(128)S(1)} %slice.76.own_ref, bf16[4,32,512]{2,1,0:T(8,128)(2,1)S(1)} %copy-done.2, ...), custom_call_target="tpu_custom_call" | custom-call | bytes 8388608 | tf_op jit(solution)/shard_map/update_factors/pallas_call | solution.py:275
  138.4 5.5 %input_gradient.1 = bf16[896,512]{1,0:T(8,128)(2,1)} custom-call(bf16[7,32,128]{2,1,0:T(8,128)(2,1)} %copy-done.9, bf16[7,32,512]{2,1,0:T(8,128)(2,1)} %copy-done.6, bf16[1,896,512]{2,1,0:T(8,128)(2,1)} %reduce-scatter.4.cloned.1.call-done.base_ref), custom_call_target="tpu_custom_call" | custom-call | bytes 4194304 | tf_op jit(solution)/shard_map/input_gradient/pallas_call | solution.py:328
  (127 shorter events, 31.0 us)
Async XLA Ops:
  7.2 131.3 %reduce-scatter.4.cloned.1.call-start = ((), (), s32[]{:S(2)}) async-start(), calls=%async_computation.1 | async-start | bytes 15597568
  21.2 10.9 %collective-permute-start.4 = (bf16[128,512]{1,0:T(8,128)(2,1)S(1)}, bf16[128,512]{1,0:T(8,128)(2,1)S(1)}, u32[]{:S(2)}, u32[]{:S(2)}) collective-permute-start(bf16[128,512]{1,0:T(8,128)(2,1)S(1)} %bitcast.14), channel_id=1, source_target_pairs={{0,32},{16,48},{32,64},{48,80},{64,96},{80,112},{96,128},{112,144}... | collective-permute-start | bytes 393224 | tf_op jit(solution)/shard_map/ppermute | solution.py:38
  23.7 14.4 %collective-permute-start.1 = (bf16[128,512]{1,0:T(8,128)(2,1)S(1)}, bf16[128,512]{1,0:T(8,128)(2,1)S(1)}, u32[]{:S(2)}, u32[]{:S(2)}) collective-permute-start(bf16[128,512]{1,0:T(8,128)(2,1)S(1)} %bitcast.15), channel_id=1, source_target_pairs={{0,224},{16,240},{32,0},{48,16},{64,32},{80,48},{96,64},{112,80},{... | collective-permute-start | bytes 393224 | tf_op jit(solution)/shard_map/ppermute | solution.py:38
  29.0 9.2 %collective-permute-start.12 = (bf16[144,512]{1,0:T(8,128)(2,1)S(1)}, bf16[144,512]{1,0:T(8,128)(2,1)S(1)}, u32[]{:S(2)}, u32[]{:S(2)}) collective-permute-start(bf16[144,512]{1,0:T(8,128)(2,1)S(1)} %fusion.1.refs_8_), channel_id=1, source_target_pairs={{0,32},{16,48},{32,64},{48,80},{64,96},{80,112},{96,128},{112,144}... | collective-permute-start | bytes 442376 | tf_op jit(solution)/shard_map/ppermute | solution.py:38
  29.1 5.6 %collective-permute-start.8 = (bf16[144,512]{1,0:T(8,128)(2,1)S(1)}, bf16[144,512]{1,0:T(8,128)(2,1)S(1)}, u32[]{:S(2)}, u32[]{:S(2)}) collective-permute-start(bf16[144,512]{1,0:T(8,128)(2,1)S(1)} %fusion.1.refs_8_), channel_id=1, source_target_pairs={{0,224},{16,240},{32,0},{48,16},{64,32},{80,48},{96,64},{112,80},{... | collective-permute-start | bytes 442376 | tf_op jit(solution)/shard_map/ppermute | solution.py:38
  32.2 7.4 %collective-permute-start.5 = (bf16[128,512]{1,0:T(8,128)(2,1)S(1)}, bf16[128,512]{1,0:T(8,128)(2,1)S(1)}, u32[]{:S(2)}, u32[]{:S(2)}) collective-permute-start(bf16[128,512]{1,0:T(8,128)(2,1)S(1)} %collective-permute-done.4.refs_7_), channel_id=1, source_target_pairs={{0,32},{16,48},{32,64},{48,80},{64,96},{80,112},{96,128},{112,144}... | collective-permute-start | bytes 393224 | tf_op jit(solution)/shard_map/ppermute | solution.py:38
  34.7 5.5 %collective-permute-start.9 = (bf16[144,512]{1,0:T(8,128)(2,1)S(1)}, bf16[144,512]{1,0:T(8,128)(2,1)S(1)}, u32[]{:S(2)}, u32[]{:S(2)}) collective-permute-start(bf16[144,512]{1,0:T(8,128)(2,1)S(1)} %collective-permute-done.8.refs_9_), channel_id=1, source_target_pairs={{0,224},{16,240},{32,0},{48,16},{64,32},{80,48},{96,64},{112,80},{... | collective-permute-start | bytes 442376 | tf_op jit(solution)/shard_map/ppermute | solution.py:38
  38.1 5.6 %collective-permute-start.2 = (bf16[128,512]{1,0:T(8,128)(2,1)S(1)}, bf16[128,512]{1,0:T(8,128)(2,1)S(1)}, u32[]{:S(2)}, u32[]{:S(2)}) collective-permute-start(bf16[128,512]{1,0:T(8,128)(2,1)S(1)} %collective-permute-done.1.refs_1_), channel_id=1, source_target_pairs={{0,224},{16,240},{32,0},{48,16},{64,32},{80,48},{96,64},{112,80},{... | collective-permute-start | bytes 393224 | tf_op jit(solution)/shard_map/ppermute | solution.py:38
  38.2 8.2 %collective-permute-start.13 = (bf16[144,512]{1,0:T(8,128)(2,1)S(1)}, bf16[144,512]{1,0:T(8,128)(2,1)S(1)}, u32[]{:S(2)}, u32[]{:S(2)}) collective-permute-start(bf16[144,512]{1,0:T(8,128)(2,1)S(1)} %collective-permute-done.12.refs_15_), channel_id=1, source_target_pairs={{0,32},{16,48},{32,64},{48,80},{64,96},{80,112},{96,128},{112,144}... | collective-permute-start | bytes 442376 | tf_op jit(solution)/shard_map/ppermute | solution.py:38
  39.6 6.9 %collective-permute-start.6 = (bf16[128,512]{1,0:T(8,128)(2,1)S(1)}, bf16[128,512]{1,0:T(8,128)(2,1)S(1)}, u32[]{:S(2)}, u32[]{:S(2)}) collective-permute-start(bf16[128,512]{1,0:T(8,128)(2,1)S(1)} %collective-permute-done.5.refs_6_), channel_id=1, source_target_pairs={{0,32},{16,48},{32,64},{48,80},{64,96},{80,112},{96,128},{112,144}... | collective-permute-start | bytes 393224 | tf_op jit(solution)/shard_map/ppermute | solution.py:38
  40.2 6.5 %collective-permute-start.10 = (bf16[144,512]{1,0:T(8,128)(2,1)S(1)}, bf16[144,512]{1,0:T(8,128)(2,1)S(1)}, u32[]{:S(2)}, u32[]{:S(2)}) collective-permute-start(bf16[144,512]{1,0:T(8,128)(2,1)S(1)} %collective-permute-done.9.refs_10_), channel_id=1, source_target_pairs={{0,224},{16,240},{32,0},{48,16},{64,32},{80,48},{96,64},{112,80},{... | collective-permute-start | bytes 442376 | tf_op jit(solution)/shard_map/ppermute | solution.py:38
  43.7 6.2 %collective-permute-start.3 = (bf16[128,512]{1,0:T(8,128)(2,1)S(1)}, bf16[128,512]{1,0:T(8,128)(2,1)S(1)}, u32[]{:S(2)}, u32[]{:S(2)}) collective-permute-start(bf16[128,512]{1,0:T(8,128)(2,1)S(1)} %collective-permute-done.2.refs_2_), channel_id=1, source_target_pairs={{0,224},{16,240},{32,0},{48,16},{64,32},{80,48},{96,64},{112,80},{... | collective-permute-start | bytes 393224 | tf_op jit(solution)/shard_map/ppermute | solution.py:38
  46.4 5.6 %collective-permute-start.14 = (bf16[144,512]{1,0:T(8,128)(2,1)S(1)}, bf16[144,512]{1,0:T(8,128)(2,1)S(1)}, u32[]{:S(2)}, u32[]{:S(2)}) collective-permute-start(bf16[144,512]{1,0:T(8,128)(2,1)S(1)} %collective-permute-done.13.refs_14_), channel_id=1, source_target_pairs={{0,32},{16,48},{32,64},{48,80},{64,96},{80,112},{96,128},{112,144}... | collective-permute-start | bytes 442376 | tf_op jit(solution)/shard_map/ppermute | solution.py:38
  46.4 7.0 %collective-permute-start.7 = (bf16[128,512]{1,0:T(8,128)(2,1)S(1)}, bf16[128,512]{1,0:T(8,128)(2,1)S(1)}, u32[]{:S(2)}, u32[]{:S(2)}) collective-permute-start(bf16[128,512]{1,0:T(8,128)(2,1)S(1)} %collective-permute-done.6.refs_5_), channel_id=1, source_target_pairs={{0,32},{16,48},{32,64},{48,80},{64,96},{80,112},{96,128},{112,144}... | collective-permute-start | bytes 393224 | tf_op jit(solution)/shard_map/ppermute | solution.py:38
  46.7 6.7 %collective-permute-start.11 = (bf16[144,512]{1,0:T(8,128)(2,1)S(1)}, bf16[144,512]{1,0:T(8,128)(2,1)S(1)}, u32[]{:S(2)}, u32[]{:S(2)}) collective-permute-start(bf16[144,512]{1,0:T(8,128)(2,1)S(1)} %collective-permute-done.10.refs_11_), channel_id=1, source_target_pairs={{0,224},{16,240},{32,0},{48,16},{64,32},{80,48},{96,64},{112,80},{... | collective-permute-start | bytes 442376 | tf_op jit(solution)/shard_map/ppermute | solution.py:38
  65.6 6.5 %collective-permute-start.17 = (bf16[4,32,128]{2,1,0:T(8,128)(2,1)S(1)}, bf16[4,32,128]{2,1,0:T(8,128)(2,1)S(1)}, u32[]{:S(2)}, u32[]{:S(2)}) collective-permute-start(bf16[4,32,128]{2,1,0:T(8,128)(2,1)S(1)} %get-tuple-element.28), channel_id=1, source_target_pairs={{0,2},{1,3},{2,0},{3,1},{4,6},{5,7},{6,4},{7,5},{8,10},{9,11},{10,... | collective-permute-start | bytes 98312 | tf_op jit(solution)/shard_map/ppermute | solution.py:52
  75.2 5.3 %collective-permute-start.19 = (bf16[4,32,128]{2,1,0:T(8,128)(2,1)S(1)}, bf16[4,32,128]{2,1,0:T(8,128)(2,1)S(1)}, u32[]{:S(2)}, u32[]{:S(2)}) collective-permute-start(bf16[4,32,128]{2,1,0:T(8,128)(2,1)S(1)} %add_convert_fusion.1), channel_id=1, source_target_pairs={{0,4},{1,5},{2,6},{3,7},{4,8},{5,9},{6,10},{7,11},{8,12},{9,13},{1... | collective-permute-start | bytes 98312 | tf_op jit(solution)/shard_map/ppermute | solution.py:52
  89.0 6.8 %collective-permute-start.26 = (bf16[7,32,512]{2,1,0:T(8,128)(2,1)S(1)}, bf16[7,32,512]{2,1,0:T(8,128)(2,1)S(1)}, u32[]{:S(2)}, u32[]{:S(2)}) collective-permute-start(bf16[7,32,512]{2,1,0:T(8,128)(2,1)S(1)} %get-tuple-element.35.refs_0_), channel_id=1, source_target_pairs={{0,32},{16,48},{32,64},{48,80},{64,96},{80,112},{96,128},{112,144}... | collective-permute-start | bytes 688136 | tf_op jit(solution)/shard_map/ppermute | solution.py:38
  90.3 6.0 %collective-permute-start.30 = (bf16[7,32,512]{2,1,0:T(8,128)(2,1)S(1)}, bf16[7,32,512]{2,1,0:T(8,128)(2,1)S(1)}, u32[]{:S(2)}, u32[]{:S(2)}) collective-permute-start(bf16[7,32,512]{2,1,0:T(8,128)(2,1)S(1)} %get-tuple-element.36.refs_7_), channel_id=1, source_target_pairs={{0,224},{16,240},{32,0},{48,16},{64,32},{80,48},{96,64},{112,80},{... | collective-permute-start | bytes 688136 | tf_op jit(solution)/shard_map/ppermute | solution.py:38
  92.0 6.7 %collective-permute-start.34 = (bf16[7,32,512]{2,1,0:T(8,128)(2,1)S(1)}, bf16[7,32,512]{2,1,0:T(8,128)(2,1)S(1)}, u32[]{:S(2)}, u32[]{:S(2)}) collective-permute-start(bf16[7,32,512]{2,1,0:T(8,128)(2,1)S(1)} %get-tuple-element.35.refs_0_), channel_id=1, source_target_pairs={{0,224},{16,240},{32,0},{48,16},{64,32},{80,48},{96,64},{112,80},{... | collective-permute-start | bytes 688136 | tf_op jit(solution)/shard_map/ppermute | solution.py:38
  93.5 8.2 %collective-permute-start.37 = (bf16[7,32,512]{2,1,0:T(8,128)(2,1)S(1)}, bf16[7,32,512]{2,1,0:T(8,128)(2,1)S(1)}, u32[]{:S(2)}, u32[]{:S(2)}) collective-permute-start(bf16[7,32,512]{2,1,0:T(8,128)(2,1)S(1)} %get-tuple-element.36.refs_7_), channel_id=1, source_target_pairs={{0,32},{16,48},{32,64},{48,80},{64,96},{80,112},{96,128},{112,144}... | collective-permute-start | bytes 688136 | tf_op jit(solution)/shard_map/ppermute | solution.py:38
  95.8 10.3 %collective-permute-start.27 = (bf16[7,32,512]{2,1,0:T(8,128)(2,1)S(1)}, bf16[7,32,512]{2,1,0:T(8,128)(2,1)S(1)}, u32[]{:S(2)}, u32[]{:S(2)}) collective-permute-start(bf16[7,32,512]{2,1,0:T(8,128)(2,1)S(1)} %collective-permute-done.26.refs_6_), channel_id=1, source_target_pairs={{0,32},{16,48},{32,64},{48,80},{64,96},{80,112},{96,128},{112,144}... | collective-permute-start | bytes 688136 | tf_op jit(solution)/shard_map/ppermute | solution.py:38
  96.2 9.8 %collective-permute-start.31 = (bf16[7,32,512]{2,1,0:T(8,128)(2,1)S(1)}, bf16[7,32,512]{2,1,0:T(8,128)(2,1)S(1)}, u32[]{:S(2)}, u32[]{:S(2)}) collective-permute-start(bf16[7,32,512]{2,1,0:T(8,128)(2,1)S(1)} %collective-permute-done.30.refs_8_), channel_id=1, source_target_pairs={{0,224},{16,240},{32,0},{48,16},{64,32},{80,48},{96,64},{112,80},{... | collective-permute-start | bytes 688136 | tf_op jit(solution)/shard_map/ppermute | solution.py:38
  98.7 19.7 %collective-permute-start.35 = (bf16[7,32,512]{2,1,0:T(8,128)(2,1)S(1)}, bf16[7,32,512]{2,1,0:T(8,128)(2,1)}, u32[]{:S(2)}, u32[]{:S(2)}) collective-permute-start(bf16[7,32,512]{2,1,0:T(8,128)(2,1)S(1)} %collective-permute-done.34.refs_1_), channel_id=1, source_target_pairs={{0,224},{16,240},{32,0},{48,16},{64,32},{80,48},{96,64},{112,80},{... | collective-permute-start | bytes 688136 | tf_op jit(solution)/shard_map/ppermute | solution.py:38
  101.7 16.8 %collective-permute-start.38 = (bf16[7,32,512]{2,1,0:T(8,128)(2,1)S(1)}, bf16[7,32,512]{2,1,0:T(8,128)(2,1)}, u32[]{:S(2)}, u32[]{:S(2)}) collective-permute-start(bf16[7,32,512]{2,1,0:T(8,128)(2,1)S(1)} %collective-permute-done.37.refs_13_), channel_id=1, source_target_pairs={{0,32},{16,48},{32,64},{48,80},{64,96},{80,112},{96,128},{112,144}... | collective-permute-start | bytes 688136 | tf_op jit(solution)/shard_map/ppermute | solution.py:38
  106.1 13.9 %collective-permute-start.28 = (bf16[7,32,512]{2,1,0:T(8,128)(2,1)S(1)}, bf16[7,32,512]{2,1,0:T(8,128)(2,1)}, u32[]{:S(2)}, u32[]{:S(2)}) collective-permute-start(bf16[7,32,512]{2,1,0:T(8,128)(2,1)S(1)} %collective-permute-done.27.refs_5_), channel_id=1, source_target_pairs={{0,32},{16,48},{32,64},{48,80},{64,96},{80,112},{96,128},{112,144}... | collective-permute-start | bytes 688136 | tf_op jit(solution)/shard_map/ppermute | solution.py:38
  106.1 14.0 %collective-permute-start.32 = (bf16[7,32,512]{2,1,0:T(8,128)(2,1)S(1)}, bf16[7,32,512]{2,1,0:T(8,128)(2,1)}, u32[]{:S(2)}, u32[]{:S(2)}) collective-permute-start(bf16[7,32,512]{2,1,0:T(8,128)(2,1)S(1)} %collective-permute-done.31.refs_9_), channel_id=1, source_target_pairs={{0,224},{16,240},{32,0},{48,16},{64,32},{80,48},{96,64},{112,80},{... | collective-permute-start | bytes 688136 | tf_op jit(solution)/shard_map/ppermute | solution.py:38
  109.5 13.7 %collective-permute-start.25 = (bf16[16,32,512]{2,1,0:T(8,128)(2,1)}, bf16[16,32,512]{2,1,0:T(8,128)(2,1)S(1)}, u32[]{:S(2)}, u32[]{:S(2)}) collective-permute-start(bf16[16,32,512]{2,1,0:T(8,128)(2,1)} %copy-done.11), channel_id=1, source_target_pairs={{0,16},{16,0},{32,48},{48,32},{64,80},{80,64},{96,112},{112,96},{1... | collective-permute-start | bytes 1572872 | tf_op jit(solution)/shard_map/ppermute | solution.py:43
  118.4 7.6 %collective-permute-start.36 = (bf16[7,32,512]{2,1,0:T(8,128)(2,1)}, bf16[7,32,512]{2,1,0:T(8,128)(2,1)}, u32[]{:S(2)}, u32[]{:S(2)}) collective-permute-start(bf16[7,32,512]{2,1,0:T(8,128)(2,1)} %collective-permute-done.35.refs_2_), channel_id=1, source_target_pairs={{0,224},{16,240},{32,0},{48,16},{64,32},{80,48},{96,64},{112,80},{... | collective-permute-start | bytes 688136 | tf_op jit(solution)/shard_map/ppermute | solution.py:38
  118.5 8.3 %collective-permute-start.39 = (bf16[7,32,512]{2,1,0:T(8,128)(2,1)}, bf16[7,32,512]{2,1,0:T(8,128)(2,1)}, u32[]{:S(2)}, u32[]{:S(2)}) collective-permute-start(bf16[7,32,512]{2,1,0:T(8,128)(2,1)} %collective-permute-done.38.refs_12_), channel_id=1, source_target_pairs={{0,32},{16,48},{32,64},{48,80},{64,96},{80,112},{96,128},{112,144}... | collective-permute-start | bytes 688136 | tf_op jit(solution)/shard_map/ppermute | solution.py:38
  120.0 11.8 %collective-permute-start.29 = (bf16[7,32,512]{2,1,0:T(8,128)(2,1)}, bf16[7,32,512]{2,1,0:T(8,128)(2,1)S(1)}, u32[]{:S(2)}, u32[]{:S(2)}) collective-permute-start(bf16[7,32,512]{2,1,0:T(8,128)(2,1)} %collective-permute-done.28.refs_4_), channel_id=1, source_target_pairs={{0,32},{16,48},{32,64},{48,80},{64,96},{80,112},{96,128},{112,144}... | collective-permute-start | bytes 688136 | tf_op jit(solution)/shard_map/ppermute | solution.py:38
  120.1 11.7 %collective-permute-start.33 = (bf16[7,32,512]{2,1,0:T(8,128)(2,1)}, bf16[7,32,512]{2,1,0:T(8,128)(2,1)S(1)}, u32[]{:S(2)}, u32[]{:S(2)}) collective-permute-start(bf16[7,32,512]{2,1,0:T(8,128)(2,1)} %collective-permute-done.32.refs_10_), channel_id=1, source_target_pairs={{0,224},{16,240},{32,0},{48,16},{64,32},{80,48},{96,64},{112,80},{... | collective-permute-start | bytes 688136 | tf_op jit(solution)/shard_map/ppermute | solution.py:38
  (25 other events, 237.3 us)
Sparse Core Ops, SparseCore 0:
  20.5 112.5 reduce-scatter.3

commit v4 on v2

--- a/solution.py
+++ b/solution.py
@@ -221,7 +221,7 @@
     return far_ref[place[at]].astype(F32) * used[at].astype(F32)
 
 
-def share_kernel(needs, place, used, far_a, far_b, near_ref, out_ref):
+def share_kernel(needs, place, used, far_a, far_b, near_ref, _, out_ref):
     @pl.loop(0, needs)
     def _(need):
         for k, far in enumerate((far_a, far_b)):
@@ -231,16 +231,16 @@
             ).astype(BF)
 
 
-def share(place, used, far_a, far_b, near):
+def share(place, used, far_a, far_b, near, token):
     return pl.pallas_call(
         functools.partial(share_kernel, near.shape[0] // 2),
         out_shape=jax.ShapeDtypeStruct(near.shape, BF),
-        in_specs=[SMEM()] * 2 + [VMEM()] * 3,
+        in_specs=[SMEM()] * 2 + [VMEM()] * 4,
         out_specs=VMEM(),
         compiler_params=PARAMS,
         cost_estimate=pl.CostEstimate(flops=0, bytes_accessed=4 * 2**20, transcendentals=0),
         name="gradient_share",
-    )(place, used, far_a, far_b, near)
+    )(place, used, far_a, far_b, near, token)
 
 
 def update_kernel(
@@ -314,22 +314,35 @@
     )(grad, weight)
 
 
-def finish_kernel(blocks, ranks_ref, chosen_ref, base_ref, out_ref):
+def finish_kernel(blocks, ranks_ref, chosen_ref, base_ref, out_ref, hold, done, came, left):
+    arriving, leaving = [], []
+    for n in range(blocks):
+        rows = pl.ds(n * BLOCK, BLOCK)
+        arriving.append(pltpu.make_async_copy(base_ref.at[rows], hold.at[rows], came.at[n]))
+        leaving.append(pltpu.make_async_copy(done.at[rows], out_ref.at[rows], left.at[n]))
+        arriving[n].start()
     for n in range(blocks):
         rows = pl.ds(n * BLOCK, BLOCK)
         term = lax.dot_general(
             ranks_ref[n], chosen_ref[n], (((0,), (0,)), ((), ())), preferred_element_type=F32
         )
-        out_ref[rows, :] = (base_ref[0, rows, :].astype(F32) + SCALE * term).astype(BF)
+        arriving[n].wait()
+        done[rows, :] = (hold[rows, :].astype(F32) + SCALE * term).astype(BF)
+        leaving[n].start()
+    for n in range(blocks):
+        leaving[n].wait()
 
 
 def finish(ranks, chosen, base):
     blocks = chosen.shape[0]
     return pl.pallas_call(
         functools.partial(finish_kernel, blocks),
-        out_shape=jax.ShapeDtypeStruct(base.shape[1:], BF),
-        in_specs=[VMEM()] * 3,
-        out_specs=VMEM(),
+        out_shape=jax.ShapeDtypeStruct(base.shape, BF),
+        in_specs=[VMEM()] * 2 + [ANY()],
+        out_specs=ANY(),
+        scratch_shapes=[pltpu.VMEM(base.shape, BF)] * 2
+        + [pltpu.SemaphoreType.DMA((blocks,))] * 2,
+        input_output_aliases={2: 0},
         compiler_params=PARAMS,
         cost_estimate=pl.CostEstimate(flops=0, bytes_accessed=4 * 2**20, transcendentals=0),
         name="input_gradient",
@@ -416,12 +429,12 @@
     mine_total, other_total = total(
         source, used, [parts_a[k] for k in near], [parts_b[k] for k in near], slots + rolls
     )
-    got_total = core_swap(share(source, used, parts_a[4], parts_b[4], other_total))
+    got_total = core_swap(share(source, used, parts_a[4], parts_b[4], other_total, got_roll))
     new_a, new_b, roll_a, roll_b = update(
         source, used, mine_own[blocks:], factor_a, factor_b, mine_roll, got_roll,
         parts_a[4], parts_b[4], mine_total, got_total,
     )
-    return finish(ranks, chosen_a, base), new_a, new_b, roll_a, roll_b
+    return finish(ranks, chosen_a, base[0]), new_a, new_b, roll_a, roll_b
 
 
 def solution(mesh):

time: 145 us -> 148 us (1.021)
  waiting for transfers between devices: 38.4 us -> 32.7 us
  starting transfers between devices: 62.7 us -> 67.8 us
  local copies, waits for them, and re-layouts: 4.42 us -> 6.52 us
  Pallas kernels: 24.1 us -> 25.8 us
    ppermute x4, starting transfers between devices: 11.2 us -> 16.2 us  [core_swap(): return lax.ppermute(x, 'dp', [(d, d ^ 1) for d in range(n)])]
    ppermute x28, waiting for transfers between devices: 21.7 us -> 17 us  [z_hop(): return lax.ppermute(x, 'dp', perm)]
    unnamed x23 -> x29, local copies, waits for them, and re-layouts: 3.66 us -> 5.75 us
    pallas_call x1, Pallas kernels: 1.34 us -> 2.99 us  [finish(): pl.pallas_call(functools.partial(finish_kernel, blocks), out_shape=jax.Sh...]
  transfers between devices with their start and end apart: 42 -> 42, of which waited for: 23 -> 18; matrix products, arithmetic and copies ran while one was open for 1% -> 1% of each run, Pallas kernels for 7% -> 7%
where the time goes in v4:
time: 148 us
  starting transfers between devices  67.8 us (46%)
  waiting for transfers between devices  32.7 us (22%)
  Pallas kernels  25.8 us (17%)
  between operations  14.3 us (10%)
  local copies, waits for them, and re-layouts  6.52 us (4%)
    ppermute x28, starting transfers between devices, z_hop(): return lax.ppermute(x, 'dp', perm)  39.6 us
    ppermute x28, waiting for transfers between devices, z_hop(): return lax.ppermute(x, 'dp', perm)  17 us
    ppermute x4, starting transfers between devices, core_swap(): return lax.ppermute(x, 'dp', [(d, d ^ 1) for d in range(n)])  16.2 us
    pallas_call x1, Pallas kernels, products(): pl.pallas_call(products_kernel, grid=(columns // tile,), out_shape=jax.Sh...  13.1 us
    ppermute x9, waiting for transfers between devices, plane_hop(): return lax.ppermute(x, 'tensor', perm)  12.1 us
    ppermute x9, starting transfers between devices, plane_hop(): return lax.ppermute(x, 'tensor', perm)  11.9 us
    unnamed x29, local copies, waits for them, and re-layouts  5.75 us
    pallas_call x1, Pallas kernels, total(): pl.pallas_call(functools.partial(total_kernel, needs), out_shape=(shape,...  3.75 us
  transfers between devices with their start and end apart: 42, of which 18 were waited for; matrix products, arithmetic and copies ran while one was open for 1% of the time, Pallas kernels for 7%

profile of v4, /device:TPU:1, one launch (start us, length us, event | category | flops | bytes accessed | tf_op | source)
XLA Modules:
  0.0 148.1 jit_solution(2923015509250653002)
XLA Ops:
  7.2 13.1 %base_products.1 = bf16[16,896,512]{2,1,0:T(8,128)(2,1)} custom-call(bf16[896,512]{1,0:T(8,128)(2,1)} %grad_ref.3, bf16[8192,512]{1,0:T(8,128)(2,1)} %weight_ref.1), custom_call_target="tpu_custom_call" | custom-call | flops 7516192768 | bytes 25165824 | tf_op jit(solution)/shard_map/base_products/pallas_call | solution.py:300
  21.2 2.5 %collective-permute-start.4 = (bf16[128,512]{1,0:T(8,128)(2,1)S(1)}, bf16[128,512]{1,0:T(8,128)(2,1)S(1)}, u32[]{:S(2)}, u32[]{:S(2)}) collective-permute-start(bf16[128,512]{1,0:T(8,128)(2,1)S(1)} %bitcast.15), channel_id=1, source_target_pairs={{0,32},{16,48},{32,64},{48,80},{64,96},{80,112},{96,128},{112,144}... | collective-permute-start | bytes 393224 | tf_op jit(solution)/shard_map/ppermute | solution.py:38
  23.7 3.9 %collective-permute-start.1 = (bf16[128,512]{1,0:T(8,128)(2,1)S(1)}, bf16[128,512]{1,0:T(8,128)(2,1)S(1)}, u32[]{:S(2)}, u32[]{:S(2)}) collective-permute-start(bf16[128,512]{1,0:T(8,128)(2,1)S(1)} %bitcast.16), channel_id=1, source_target_pairs={{0,224},{16,240},{32,0},{48,16},{64,32},{80,48},{96,64},{112,80},{... | collective-permute-start | bytes 393224 | tf_op jit(solution)/shard_map/ppermute | solution.py:38
  29.1 2.7 %collective-permute-start.8 = (bf16[144,512]{1,0:T(8,128)(2,1)S(1)}, bf16[144,512]{1,0:T(8,128)(2,1)S(1)}, u32[]{:S(2)}, u32[]{:S(2)}) collective-permute-start(bf16[144,512]{1,0:T(8,128)(2,1)S(1)} %fusion.1.refs_8_), channel_id=1, source_target_pairs={{0,224},{16,240},{32,0},{48,16},{64,32},{80,48},{96,64},{112,80},{... | collective-permute-start | bytes 442376 | tf_op jit(solution)/shard_map/ppermute | solution.py:38
  32.2 2.4 %collective-permute-done.8.refs_9_ = bf16[144,512]{1,0:T(8,128)(2,1)S(1)} collective-permute-done((bf16[144,512]{1,0:T(8,128)(2,1)S(1)}, bf16[144,512]{1,0:T(8,128)(2,1)S(1)}, u32[]{:S(2)}, u32[]{:S(2)}) %collective-permute-start.8) | collective-permute-done | bytes 147488 | tf_op jit(solution)/shard_map/ppermute | solution.py:38
  34.7 3.4 %collective-permute-start.9 = (bf16[144,512]{1,0:T(8,128)(2,1)S(1)}, bf16[144,512]{1,0:T(8,128)(2,1)S(1)}, u32[]{:S(2)}, u32[]{:S(2)}) collective-permute-start(bf16[144,512]{1,0:T(8,128)(2,1)S(1)} %collective-permute-done.8.refs_9_), channel_id=1, source_target_pairs={{0,224},{16,240},{32,0},{48,16},{64,32},{80,48},{96,64},{112,80},{... | collective-permute-start | bytes 442376 | tf_op jit(solution)/shard_map/ppermute | solution.py:38
  40.2 3.5 %collective-permute-start.10 = (bf16[144,512]{1,0:T(8,128)(2,1)S(1)}, bf16[144,512]{1,0:T(8,128)(2,1)S(1)}, u32[]{:S(2)}, u32[]{:S(2)}) collective-permute-start(bf16[144,512]{1,0:T(8,128)(2,1)S(1)} %collective-permute-done.9.refs_10_), channel_id=1, source_target_pairs={{0,224},{16,240},{32,0},{48,16},{64,32},{80,48},{96,64},{112,80},{... | collective-permute-start | bytes 442376 | tf_op jit(solution)/shard_map/ppermute | solution.py:38
  43.7 2.7 %collective-permute-start.3 = (bf16[128,512]{1,0:T(8,128)(2,1)S(1)}, bf16[128,512]{1,0:T(8,128)(2,1)S(1)}, u32[]{:S(2)}, u32[]{:S(2)}) collective-permute-start(bf16[128,512]{1,0:T(8,128)(2,1)S(1)} %collective-permute-done.2.refs_2_), channel_id=1, source_target_pairs={{0,224},{16,240},{32,0},{48,16},{64,32},{80,48},{96,64},{112,80},{... | collective-permute-start | bytes 393224 | tf_op jit(solution)/shard_map/ppermute | solution.py:38
  46.7 3.0 %collective-permute-start.11 = (bf16[144,512]{1,0:T(8,128)(2,1)S(1)}, bf16[144,512]{1,0:T(8,128)(2,1)S(1)}, u32[]{:S(2)}, u32[]{:S(2)}) collective-permute-start(bf16[144,512]{1,0:T(8,128)(2,1)S(1)} %collective-permute-done.10.refs_11_), channel_id=1, source_target_pairs={{0,224},{16,240},{32,0},{48,16},{64,32},{80,48},{96,64},{112,80},{... | collective-permute-start | bytes 442376 | tf_op jit(solution)/shard_map/ppermute | solution.py:38
  49.9 2.2 %collective-permute-done.14.refs_13_ = bf16[144,512]{1,0:T(8,128)(2,1)S(1)} collective-permute-done((bf16[144,512]{1,0:T(8,128)(2,1)S(1)}, bf16[144,512]{1,0:T(8,128)(2,1)S(1)}, u32[]{:S(2)}, u32[]{:S(2)}) %collective-permute-start.14) | collective-permute-done | bytes 147488 | tf_op jit(solution)/shard_map/ppermute | solution.py:38
  56.7 3.3 %collective-permute-start.15 = (bf16[16,32,512]{2,1,0:T(8,128)(2,1)}, bf16[16,32,512]{2,1,0:T(8,128)(2,1)S(1)}, u32[]{:S(2)}, u32[]{:S(2)}) collective-permute-start(bf16[16,32,512]{2,1,0:T(8,128)(2,1)} %get-tuple-element.25), channel_id=1, source_target_pairs={{0,16},{16,0},{32,48},{48,32},{64,80},{80,64},{96,112},{112,96},{1... | collective-permute-start | bytes 1572872 | tf_op jit(solution)/shard_map/ppermute | solution.py:43
  60.0 1.7 %collective-permute-done.15.other_ref = bf16[16,32,512]{2,1,0:T(8,128)(2,1)S(1)} collective-permute-done((bf16[16,32,512]{2,1,0:T(8,128)(2,1)}, bf16[16,32,512]{2,1,0:T(8,128)(2,1)S(1)}, u32[]{:S(2)}, u32[]{:S(2)}) %collective-permute-start.15) | collective-permute-done | bytes 524320 | tf_op jit(solution)/shard_map/ppermute | solution.py:43
  64.4 2.6 %collective-permute-start.17 = (bf16[4,32,128]{2,1,0:T(8,128)(2,1)S(1)}, bf16[4,32,128]{2,1,0:T(8,128)(2,1)S(1)}, u32[]{:S(2)}, u32[]{:S(2)}) collective-permute-start(bf16[4,32,128]{2,1,0:T(8,128)(2,1)S(1)} %get-tuple-element.28), channel_id=1, source_target_pairs={{0,2},{1,3},{2,0},{3,1},{4,6},{5,7},{6,4},{7,5},{8,10},{9,11},{10,... | collective-permute-start | bytes 98312 | tf_op jit(solution)/shard_map/ppermute | solution.py:52
  68.1 2.9 %collective-permute-done.17 = bf16[4,32,128]{2,1,0:T(8,128)(2,1)S(1)} collective-permute-done((bf16[4,32,128]{2,1,0:T(8,128)(2,1)S(1)}, bf16[4,32,128]{2,1,0:T(8,128)(2,1)S(1)}, u32[]{:S(2)}, u32[]{:S(2)}) %collective-permute-start.17) | collective-permute-done | bytes 32800 | tf_op jit(solution)/shard_map/ppermute | solution.py:52
  71.0 2.6 %collective-permute-start.21 = (bf16[4,32,128]{2,1,0:T(8,128)(2,1)S(1)}, bf16[4,32,128]{2,1,0:T(8,128)(2,1)S(1)}, u32[]{:S(2)}, u32[]{:S(2)}) collective-permute-start(bf16[4,32,128]{2,1,0:T(8,128)(2,1)S(1)} %add_convert_fusion.1), channel_id=1, source_target_pairs={{0,12},{1,13},{2,14},{3,15},{4,0},{5,1},{6,2},{7,3},{8,4},{9,5},{1... | collective-permute-start | bytes 98312 | tf_op jit(solution)/shard_map/ppermute | solution.py:52
  74.9 3.6 %collective-permute-done.20 = bf16[4,32,128]{2,1,0:T(8,128)(2,1)S(1)} collective-permute-done((bf16[4,32,128]{2,1,0:T(8,128)(2,1)S(1)}, bf16[4,32,128]{2,1,0:T(8,128)(2,1)S(1)}, u32[]{:S(2)}, u32[]{:S(2)}) %collective-permute-start.20) | collective-permute-done | bytes 32800 | tf_op jit(solution)/shard_map/ppermute | solution.py:52
  79.3 2.5 %collective-permute-start.24 = (bf16[4,32,128]{2,1,0:T(8,128)(2,1)S(1)}, bf16[4,32,128]{2,1,0:T(8,128)(2,1)S(1)}, u32[]{:S(2)}, u32[]{:S(2)}) collective-permute-start(bf16[4,32,128]{2,1,0:T(8,128)(2,1)S(1)} %add_convert_fusion.refs_0_), channel_id=1, source_target_pairs={{0,3},{1,0},{2,1},{3,2},{4,7},{5,4},{6,5},{7,6},{8,11},{9,8},{10,9... | collective-permute-start | bytes 98312 | tf_op jit(solution)/shard_map/ppermute | solution.py:52
  83.5 3.2 %collective-permute-done.23.refs_2_ = bf16[4,32,128]{2,1,0:T(8,128)(2,1)S(1)} collective-permute-done((bf16[4,32,128]{2,1,0:T(8,128)(2,1)S(1)}, bf16[4,32,128]{2,1,0:T(8,128)(2,1)S(1)}, u32[]{:S(2)}, u32[]{:S(2)}) %collective-permute-start.23) | collective-permute-done | bytes 32800 | tf_op jit(solution)/shard_map/ppermute | solution.py:52
  88.7 1.7 %collective-permute-start.30 = (bf16[7,32,512]{2,1,0:T(8,128)(2,1)S(1)}, bf16[7,32,512]{2,1,0:T(8,128)(2,1)S(1)}, u32[]{:S(2)}, u32[]{:S(2)}) collective-permute-start(bf16[7,32,512]{2,1,0:T(8,128)(2,1)S(1)} %get-tuple-element.36.refs_7_), channel_id=1, source_target_pairs={{0,224},{16,240},{32,0},{48,16},{64,32},{80,48},{96,64},{112,80},{... | collective-permute-start | bytes 688136 | tf_op jit(solution)/shard_map/ppermute | solution.py:38
  91.9 2.3 %collective-permute-done.26.refs_6_ = bf16[7,32,512]{2,1,0:T(8,128)(2,1)S(1)} collective-permute-done((bf16[7,32,512]{2,1,0:T(8,128)(2,1)S(1)}, bf16[7,32,512]{2,1,0:T(8,128)(2,1)S(1)}, u32[]{:S(2)}, u32[]{:S(2)}) %collective-permute-start.26) | collective-permute-done | bytes 229408 | tf_op jit(solution)/shard_map/ppermute | solution.py:38
  94.5 2.3 %collective-permute-start.31 = (bf16[7,32,512]{2,1,0:T(8,128)(2,1)S(1)}, bf16[7,32,512]{2,1,0:T(8,128)(2,1)}, u32[]{:S(2)}, u32[]{:S(2)}) collective-permute-start(bf16[7,32,512]{2,1,0:T(8,128)(2,1)S(1)} %collective-permute-done.30.refs_8_), channel_id=1, source_target_pairs={{0,224},{16,240},{32,0},{48,16},{64,32},{80,48},{96,64},{112,80},{... | collective-permute-start | bytes 688136 | tf_op jit(solution)/shard_map/ppermute | solution.py:38
  97.0 2.3 %collective-permute-start.35 = (bf16[7,32,512]{2,1,0:T(8,128)(2,1)S(1)}, bf16[7,32,512]{2,1,0:T(8,128)(2,1)}, u32[]{:S(2)}, u32[]{:S(2)}) collective-permute-start(bf16[7,32,512]{2,1,0:T(8,128)(2,1)S(1)} %collective-permute-done.34.refs_1_), channel_id=1, source_target_pairs={{0,224},{16,240},{32,0},{48,16},{64,32},{80,48},{96,64},{112,80},{... | collective-permute-start | bytes 688136 | tf_op jit(solution)/shard_map/ppermute | solution.py:38
  100.8 3.9 %collective-permute-done.27.refs_5_ = bf16[7,32,512]{2,1,0:T(8,128)(2,1)S(1)} collective-permute-done((bf16[7,32,512]{2,1,0:T(8,128)(2,1)S(1)}, bf16[7,32,512]{2,1,0:T(8,128)(2,1)S(1)}, u32[]{:S(2)}, u32[]{:S(2)}) %collective-permute-start.27) | collective-permute-done | bytes 229408 | tf_op jit(solution)/shard_map/ppermute | solution.py:38
  105.4 2.7 %collective-permute-start.32 = (bf16[7,32,512]{2,1,0:T(8,128)(2,1)}, bf16[7,32,512]{2,1,0:T(8,128)(2,1)}, u32[]{:S(2)}, u32[]{:S(2)}) collective-permute-start(bf16[7,32,512]{2,1,0:T(8,128)(2,1)} %collective-permute-done.31.refs_9_), channel_id=1, source_target_pairs={{0,224},{16,240},{32,0},{48,16},{64,32},{80,48},{96,64},{112,80},{... | collective-permute-start | bytes 688136 | tf_op jit(solution)/shard_map/ppermute | solution.py:38
  108.2 7.5 %collective-permute-start.25 = (bf16[16,32,512]{2,1,0:T(8,128)(2,1)}, bf16[16,32,512]{2,1,0:T(8,128)(2,1)S(1)}, u32[]{:S(2)}, u32[]{:S(2)}) collective-permute-start(bf16[16,32,512]{2,1,0:T(8,128)(2,1)} %copy-done.10), channel_id=1, source_target_pairs={{0,16},{16,0},{32,48},{48,32},{64,80},{80,64},{96,112},{112,96},{1... | collective-permute-start | bytes 1572872 | tf_op jit(solution)/shard_map/ppermute | solution.py:43
  117.3 2.6 %collective-permute-start.33 = (bf16[7,32,512]{2,1,0:T(8,128)(2,1)}, bf16[7,32,512]{2,1,0:T(8,128)(2,1)S(1)}, u32[]{:S(2)}, u32[]{:S(2)}) collective-permute-start(bf16[7,32,512]{2,1,0:T(8,128)(2,1)} %collective-permute-done.32.refs_10_), channel_id=1, source_target_pairs={{0,224},{16,240},{32,0},{48,16},{64,32},{80,48},{96,64},{112,80},{... | collective-permute-start | bytes 688136 | tf_op jit(solution)/shard_map/ppermute | solution.py:38
  120.4 3.1 %collective-permute-done.36.refs_3_ = bf16[7,32,512]{2,1,0:T(8,128)(2,1)} collective-permute-done((bf16[7,32,512]{2,1,0:T(8,128)(2,1)}, bf16[7,32,512]{2,1,0:T(8,128)(2,1)}, u32[]{:S(2)}, u32[]{:S(2)}) %collective-permute-start.36) | collective-permute-done | bytes 229408 | tf_op jit(solution)/shard_map/ppermute | solution.py:38
  125.4 3.7 %gradient_totals.1 = (f32[24,32,512]{2,1,0:T(8,128)S(1)}, f32[24,32,512]{2,1,0:T(8,128)S(1)}) custom-call(s32[192]{0:T(256)S(1)} %reshape.69.place, s32[192]{0:T(256)S(1)} %reshape.70.used, bf16[7,32,512]{2,1,0:T(8,128)(2,1)S(1)} %get-tuple-element.35.refs_0_, bf16[7,32,512]{2,1,0:T(8,128)(2,1)S(1)} %collective-permute-done.34.refs_1_, ...), custom_call_target="tpu_custom_call" | custom-call | bytes 16777216 | tf_op jit(solution)/shard_map/gradient_totals/pallas_call | solution.py:208
  130.0 4.4 %collective-permute-start.40 = (bf16[24,32,512]{2,1,0:T(8,128)(2,1)S(1)}, bf16[24,32,512]{2,1,0:T(8,128)(2,1)S(1)}, u32[]{:S(2)}, u32[]{:S(2)}) collective-permute-start(bf16[24,32,512]{2,1,0:T(8,128)(2,1)S(1)} %gradient_share.1), channel_id=1, source_target_pairs={{0,16},{16,0},{32,48},{48,32},{64,80},{80,64},{96,112},{112,96},{1... | collective-permute-start | bytes 2359304 | tf_op jit(solution)/shard_map/ppermute | solution.py:43
  134.5 1.8 %collective-permute-done.40.other_ref = bf16[24,32,512]{2,1,0:T(8,128)(2,1)S(1)} collective-permute-done((bf16[24,32,512]{2,1,0:T(8,128)(2,1)S(1)}, bf16[24,32,512]{2,1,0:T(8,128)(2,1)S(1)}, u32[]{:S(2)}, u32[]{:S(2)}) %collective-permute-start.40) | collective-permute-done | bytes 786464 | tf_op jit(solution)/shard_map/ppermute | solution.py:43
  136.4 1.9 %update_factors.1 = (bf16[4,32,512]{2,1,0:T(8,128)(2,1)}, bf16[4,32,512]{2,1,0:T(8,128)(2,1)}, bf16[8,32,512]{2,1,0:T(8,128)(2,1)}, bf16[8,32,512]{2,1,0:T(8,128)(2,1)}) custom-call(s32[192]{0:T(256)S(1)} %reshape.69.place, s32[192]{0:T(256)S(1)} %reshape.70.used, s32[8]{0:T(128)S(1)} %slice.76.own_ref, bf16[4,32,512]{2,1,0:T(8,128)(2,1)S(1)} %copy-done.2, ...), custom_call_target="tpu_custom_call" | custom-call | bytes 8388608 | tf_op jit(solution)/shard_map/update_factors/pallas_call | solution.py:275
  138.2 3.0 %input_gradient.1 = bf16[896,512]{1,0:T(8,128)(2,1)} custom-call(bf16[7,32,128]{2,1,0:T(8,128)(2,1)S(1)} %get-tuple-element.30.ranks_ref, bf16[7,32,512]{2,1,0:T(8,128)(2,1)S(1)} %get-tuple-element.31.chosen_ref, bf16[896,512]{1,0:T(8,128)(2,1)} %bitcast.20), custom_call_target="tpu_custom_call", output_to_operand_aliasing={{}: (2, {})} | custom-call | bytes 4194304 | tf_op jit(solution)/shard_map/input_gradient/pallas_call | solution.py:338
  (125 shorter events, 28.9 us)
Async XLA Ops:
  7.2 131.1 %reduce-scatter.4.cloned.1.call-start = ((), (), s32[]{:S(2)}) async-start(), calls=%async_computation.1 | async-start | bytes 15597568
  21.2 10.9 %collective-permute-start.4 = (bf16[128,512]{1,0:T(8,128)(2,1)S(1)}, bf16[128,512]{1,0:T(8,128)(2,1)S(1)}, u32[]{:S(2)}, u32[]{:S(2)}) collective-permute-start(bf16[128,512]{1,0:T(8,128)(2,1)S(1)} %bitcast.15), channel_id=1, source_target_pairs={{0,32},{16,48},{32,64},{48,80},{64,96},{80,112},{96,128},{112,144}... | collective-permute-start | bytes 393224 | tf_op jit(solution)/shard_map/ppermute | solution.py:38
  23.7 14.4 %collective-permute-start.1 = (bf16[128,512]{1,0:T(8,128)(2,1)S(1)}, bf16[128,512]{1,0:T(8,128)(2,1)S(1)}, u32[]{:S(2)}, u32[]{:S(2)}) collective-permute-start(bf16[128,512]{1,0:T(8,128)(2,1)S(1)} %bitcast.16), channel_id=1, source_target_pairs={{0,224},{16,240},{32,0},{48,16},{64,32},{80,48},{96,64},{112,80},{... | collective-permute-start | bytes 393224 | tf_op jit(solution)/shard_map/ppermute | solution.py:38
  29.0 9.2 %collective-permute-start.12 = (bf16[144,512]{1,0:T(8,128)(2,1)S(1)}, bf16[144,512]{1,0:T(8,128)(2,1)S(1)}, u32[]{:S(2)}, u32[]{:S(2)}) collective-permute-start(bf16[144,512]{1,0:T(8,128)(2,1)S(1)} %fusion.1.refs_8_), channel_id=1, source_target_pairs={{0,32},{16,48},{32,64},{48,80},{64,96},{80,112},{96,128},{112,144}... | collective-permute-start | bytes 442376 | tf_op jit(solution)/shard_map/ppermute | solution.py:38
  29.1 5.6 %collective-permute-start.8 = (bf16[144,512]{1,0:T(8,128)(2,1)S(1)}, bf16[144,512]{1,0:T(8,128)(2,1)S(1)}, u32[]{:S(2)}, u32[]{:S(2)}) collective-permute-start(bf16[144,512]{1,0:T(8,128)(2,1)S(1)} %fusion.1.refs_8_), channel_id=1, source_target_pairs={{0,224},{16,240},{32,0},{48,16},{64,32},{80,48},{96,64},{112,80},{... | collective-permute-start | bytes 442376 | tf_op jit(solution)/shard_map/ppermute | solution.py:38
  32.2 7.4 %collective-permute-start.5 = (bf16[128,512]{1,0:T(8,128)(2,1)S(1)}, bf16[128,512]{1,0:T(8,128)(2,1)S(1)}, u32[]{:S(2)}, u32[]{:S(2)}) collective-permute-start(bf16[128,512]{1,0:T(8,128)(2,1)S(1)} %collective-permute-done.4.refs_7_), channel_id=1, source_target_pairs={{0,32},{16,48},{32,64},{48,80},{64,96},{80,112},{96,128},{112,144}... | collective-permute-start | bytes 393224 | tf_op jit(solution)/shard_map/ppermute | solution.py:38
  34.7 5.5 %collective-permute-start.9 = (bf16[144,512]{1,0:T(8,128)(2,1)S(1)}, bf16[144,512]{1,0:T(8,128)(2,1)S(1)}, u32[]{:S(2)}, u32[]{:S(2)}) collective-permute-start(bf16[144,512]{1,0:T(8,128)(2,1)S(1)} %collective-permute-done.8.refs_9_), channel_id=1, source_target_pairs={{0,224},{16,240},{32,0},{48,16},{64,32},{80,48},{96,64},{112,80},{... | collective-permute-start | bytes 442376 | tf_op jit(solution)/shard_map/ppermute | solution.py:38
  38.1 5.6 %collective-permute-start.2 = (bf16[128,512]{1,0:T(8,128)(2,1)S(1)}, bf16[128,512]{1,0:T(8,128)(2,1)S(1)}, u32[]{:S(2)}, u32[]{:S(2)}) collective-permute-start(bf16[128,512]{1,0:T(8,128)(2,1)S(1)} %collective-permute-done.1.refs_1_), channel_id=1, source_target_pairs={{0,224},{16,240},{32,0},{48,16},{64,32},{80,48},{96,64},{112,80},{... | collective-permute-start | bytes 393224 | tf_op jit(solution)/shard_map/ppermute | solution.py:38
  38.2 8.2 %collective-permute-start.13 = (bf16[144,512]{1,0:T(8,128)(2,1)S(1)}, bf16[144,512]{1,0:T(8,128)(2,1)S(1)}, u32[]{:S(2)}, u32[]{:S(2)}) collective-permute-start(bf16[144,512]{1,0:T(8,128)(2,1)S(1)} %collective-permute-done.12.refs_15_), channel_id=1, source_target_pairs={{0,32},{16,48},{32,64},{48,80},{64,96},{80,112},{96,128},{112,144}... | collective-permute-start | bytes 442376 | tf_op jit(solution)/shard_map/ppermute | solution.py:38
  39.6 6.9 %collective-permute-start.6 = (bf16[128,512]{1,0:T(8,128)(2,1)S(1)}, bf16[128,512]{1,0:T(8,128)(2,1)S(1)}, u32[]{:S(2)}, u32[]{:S(2)}) collective-permute-start(bf16[128,512]{1,0:T(8,128)(2,1)S(1)} %collective-permute-done.5.refs_6_), channel_id=1, source_target_pairs={{0,32},{16,48},{32,64},{48,80},{64,96},{80,112},{96,128},{112,144}... | collective-permute-start | bytes 393224 | tf_op jit(solution)/shard_map/ppermute | solution.py:38
  40.2 6.5 %collective-permute-start.10 = (bf16[144,512]{1,0:T(8,128)(2,1)S(1)}, bf16[144,512]{1,0:T(8,128)(2,1)S(1)}, u32[]{:S(2)}, u32[]{:S(2)}) collective-permute-start(bf16[144,512]{1,0:T(8,128)(2,1)S(1)} %collective-permute-done.9.refs_10_), channel_id=1, source_target_pairs={{0,224},{16,240},{32,0},{48,16},{64,32},{80,48},{96,64},{112,80},{... | collective-permute-start | bytes 442376 | tf_op jit(solution)/shard_map/ppermute | solution.py:38
  43.7 6.2 %collective-permute-start.3 = (bf16[128,512]{1,0:T(8,128)(2,1)S(1)}, bf16[128,512]{1,0:T(8,128)(2,1)S(1)}, u32[]{:S(2)}, u32[]{:S(2)}) collective-permute-start(bf16[128,512]{1,0:T(8,128)(2,1)S(1)} %collective-permute-done.2.refs_2_), channel_id=1, source_target_pairs={{0,224},{16,240},{32,0},{48,16},{64,32},{80,48},{96,64},{112,80},{... | collective-permute-start | bytes 393224 | tf_op jit(solution)/shard_map/ppermute | solution.py:38
  46.4 5.6 %collective-permute-start.14 = (bf16[144,512]{1,0:T(8,128)(2,1)S(1)}, bf16[144,512]{1,0:T(8,128)(2,1)S(1)}, u32[]{:S(2)}, u32[]{:S(2)}) collective-permute-start(bf16[144,512]{1,0:T(8,128)(2,1)S(1)} %collective-permute-done.13.refs_14_), channel_id=1, source_target_pairs={{0,32},{16,48},{32,64},{48,80},{64,96},{80,112},{96,128},{112,144}... | collective-permute-start | bytes 442376 | tf_op jit(solution)/shard_map/ppermute | solution.py:38
  46.4 7.0 %collective-permute-start.7 = (bf16[128,512]{1,0:T(8,128)(2,1)S(1)}, bf16[128,512]{1,0:T(8,128)(2,1)S(1)}, u32[]{:S(2)}, u32[]{:S(2)}) collective-permute-start(bf16[128,512]{1,0:T(8,128)(2,1)S(1)} %collective-permute-done.6.refs_5_), channel_id=1, source_target_pairs={{0,32},{16,48},{32,64},{48,80},{64,96},{80,112},{96,128},{112,144}... | collective-permute-start | bytes 393224 | tf_op jit(solution)/shard_map/ppermute | solution.py:38
  46.7 6.7 %collective-permute-start.11 = (bf16[144,512]{1,0:T(8,128)(2,1)S(1)}, bf16[144,512]{1,0:T(8,128)(2,1)S(1)}, u32[]{:S(2)}, u32[]{:S(2)}) collective-permute-start(bf16[144,512]{1,0:T(8,128)(2,1)S(1)} %collective-permute-done.10.refs_11_), channel_id=1, source_target_pairs={{0,224},{16,240},{32,0},{48,16},{64,32},{80,48},{96,64},{112,80},{... | collective-permute-start | bytes 442376 | tf_op jit(solution)/shard_map/ppermute | solution.py:38
  64.4 6.6 %collective-permute-start.17 = (bf16[4,32,128]{2,1,0:T(8,128)(2,1)S(1)}, bf16[4,32,128]{2,1,0:T(8,128)(2,1)S(1)}, u32[]{:S(2)}, u32[]{:S(2)}) collective-permute-start(bf16[4,32,128]{2,1,0:T(8,128)(2,1)S(1)} %get-tuple-element.28), channel_id=1, source_target_pairs={{0,2},{1,3},{2,0},{3,1},{4,6},{5,7},{6,4},{7,5},{8,10},{9,11},{10,... | collective-permute-start | bytes 98312 | tf_op jit(solution)/shard_map/ppermute | solution.py:52
  87.5 6.6 %collective-permute-start.26 = (bf16[7,32,512]{2,1,0:T(8,128)(2,1)S(1)}, bf16[7,32,512]{2,1,0:T(8,128)(2,1)S(1)}, u32[]{:S(2)}, u32[]{:S(2)}) collective-permute-start(bf16[7,32,512]{2,1,0:T(8,128)(2,1)S(1)} %get-tuple-element.35.refs_0_), channel_id=1, source_target_pairs={{0,32},{16,48},{32,64},{48,80},{64,96},{80,112},{96,128},{112,144}... | collective-permute-start | bytes 688136 | tf_op jit(solution)/shard_map/ppermute | solution.py:38
  88.7 5.8 %collective-permute-start.30 = (bf16[7,32,512]{2,1,0:T(8,128)(2,1)S(1)}, bf16[7,32,512]{2,1,0:T(8,128)(2,1)S(1)}, u32[]{:S(2)}, u32[]{:S(2)}) collective-permute-start(bf16[7,32,512]{2,1,0:T(8,128)(2,1)S(1)} %get-tuple-element.36.refs_7_), channel_id=1, source_target_pairs={{0,224},{16,240},{32,0},{48,16},{64,32},{80,48},{96,64},{112,80},{... | collective-permute-start | bytes 688136 | tf_op jit(solution)/shard_map/ppermute | solution.py:38
  90.4 6.6 %collective-permute-start.34 = (bf16[7,32,512]{2,1,0:T(8,128)(2,1)S(1)}, bf16[7,32,512]{2,1,0:T(8,128)(2,1)S(1)}, u32[]{:S(2)}, u32[]{:S(2)}) collective-permute-start(bf16[7,32,512]{2,1,0:T(8,128)(2,1)S(1)} %get-tuple-element.35.refs_0_), channel_id=1, source_target_pairs={{0,224},{16,240},{32,0},{48,16},{64,32},{80,48},{96,64},{112,80},{... | collective-permute-start | bytes 688136 | tf_op jit(solution)/shard_map/ppermute | solution.py:38
  91.8 8.4 %collective-permute-start.37 = (bf16[7,32,512]{2,1,0:T(8,128)(2,1)S(1)}, bf16[7,32,512]{2,1,0:T(8,128)(2,1)S(1)}, u32[]{:S(2)}, u32[]{:S(2)}) collective-permute-start(bf16[7,32,512]{2,1,0:T(8,128)(2,1)S(1)} %get-tuple-element.36.refs_7_), channel_id=1, source_target_pairs={{0,32},{16,48},{32,64},{48,80},{64,96},{80,112},{96,128},{112,144}... | collective-permute-start | bytes 688136 | tf_op jit(solution)/shard_map/ppermute | solution.py:38
  94.1 10.6 %collective-permute-start.27 = (bf16[7,32,512]{2,1,0:T(8,128)(2,1)S(1)}, bf16[7,32,512]{2,1,0:T(8,128)(2,1)S(1)}, u32[]{:S(2)}, u32[]{:S(2)}) collective-permute-start(bf16[7,32,512]{2,1,0:T(8,128)(2,1)S(1)} %collective-permute-done.26.refs_6_), channel_id=1, source_target_pairs={{0,32},{16,48},{32,64},{48,80},{64,96},{80,112},{96,128},{112,144}... | collective-permute-start | bytes 688136 | tf_op jit(solution)/shard_map/ppermute | solution.py:38
  94.5 10.9 %collective-permute-start.31 = (bf16[7,32,512]{2,1,0:T(8,128)(2,1)S(1)}, bf16[7,32,512]{2,1,0:T(8,128)(2,1)}, u32[]{:S(2)}, u32[]{:S(2)}) collective-permute-start(bf16[7,32,512]{2,1,0:T(8,128)(2,1)S(1)} %collective-permute-done.30.refs_8_), channel_id=1, source_target_pairs={{0,224},{16,240},{32,0},{48,16},{64,32},{80,48},{96,64},{112,80},{... | collective-permute-start | bytes 688136 | tf_op jit(solution)/shard_map/ppermute | solution.py:38
  97.0 18.7 %collective-permute-start.35 = (bf16[7,32,512]{2,1,0:T(8,128)(2,1)S(1)}, bf16[7,32,512]{2,1,0:T(8,128)(2,1)}, u32[]{:S(2)}, u32[]{:S(2)}) collective-permute-start(bf16[7,32,512]{2,1,0:T(8,128)(2,1)S(1)} %collective-permute-done.34.refs_1_), channel_id=1, source_target_pairs={{0,224},{16,240},{32,0},{48,16},{64,32},{80,48},{96,64},{112,80},{... | collective-permute-start | bytes 688136 | tf_op jit(solution)/shard_map/ppermute | solution.py:38
  100.1 15.6 %collective-permute-start.38 = (bf16[7,32,512]{2,1,0:T(8,128)(2,1)S(1)}, bf16[7,32,512]{2,1,0:T(8,128)(2,1)}, u32[]{:S(2)}, u32[]{:S(2)}) collective-permute-start(bf16[7,32,512]{2,1,0:T(8,128)(2,1)S(1)} %collective-permute-done.37.refs_13_), channel_id=1, source_target_pairs={{0,32},{16,48},{32,64},{48,80},{64,96},{80,112},{96,128},{112,144}... | collective-permute-start | bytes 688136 | tf_op jit(solution)/shard_map/ppermute | solution.py:38
  104.7 12.5 %collective-permute-start.28 = (bf16[7,32,512]{2,1,0:T(8,128)(2,1)S(1)}, bf16[7,32,512]{2,1,0:T(8,128)(2,1)}, u32[]{:S(2)}, u32[]{:S(2)}) collective-permute-start(bf16[7,32,512]{2,1,0:T(8,128)(2,1)S(1)} %collective-permute-done.27.refs_5_), channel_id=1, source_target_pairs={{0,32},{16,48},{32,64},{48,80},{64,96},{80,112},{96,128},{112,144}... | collective-permute-start | bytes 688136 | tf_op jit(solution)/shard_map/ppermute | solution.py:38
  105.4 11.9 %collective-permute-start.32 = (bf16[7,32,512]{2,1,0:T(8,128)(2,1)}, bf16[7,32,512]{2,1,0:T(8,128)(2,1)}, u32[]{:S(2)}, u32[]{:S(2)}) collective-permute-start(bf16[7,32,512]{2,1,0:T(8,128)(2,1)} %collective-permute-done.31.refs_9_), channel_id=1, source_target_pairs={{0,224},{16,240},{32,0},{48,16},{64,32},{80,48},{96,64},{112,80},{... | collective-permute-start | bytes 688136 | tf_op jit(solution)/shard_map/ppermute | solution.py:38
  108.2 21.0 %collective-permute-start.25 = (bf16[16,32,512]{2,1,0:T(8,128)(2,1)}, bf16[16,32,512]{2,1,0:T(8,128)(2,1)S(1)}, u32[]{:S(2)}, u32[]{:S(2)}) collective-permute-start(bf16[16,32,512]{2,1,0:T(8,128)(2,1)} %copy-done.10), channel_id=1, source_target_pairs={{0,16},{16,0},{32,48},{48,32},{64,80},{80,64},{96,112},{112,96},{1... | collective-permute-start | bytes 1572872 | tf_op jit(solution)/shard_map/ppermute | solution.py:43
  115.7 7.8 %collective-permute-start.36 = (bf16[7,32,512]{2,1,0:T(8,128)(2,1)}, bf16[7,32,512]{2,1,0:T(8,128)(2,1)}, u32[]{:S(2)}, u32[]{:S(2)}) collective-permute-start(bf16[7,32,512]{2,1,0:T(8,128)(2,1)} %collective-permute-done.35.refs_2_), channel_id=1, source_target_pairs={{0,224},{16,240},{32,0},{48,16},{64,32},{80,48},{96,64},{112,80},{... | collective-permute-start | bytes 688136 | tf_op jit(solution)/shard_map/ppermute | solution.py:38
  115.8 7.7 %collective-permute-start.39 = (bf16[7,32,512]{2,1,0:T(8,128)(2,1)}, bf16[7,32,512]{2,1,0:T(8,128)(2,1)}, u32[]{:S(2)}, u32[]{:S(2)}) collective-permute-start(bf16[7,32,512]{2,1,0:T(8,128)(2,1)} %collective-permute-done.38.refs_12_), channel_id=1, source_target_pairs={{0,32},{16,48},{32,64},{48,80},{64,96},{80,112},{96,128},{112,144}... | collective-permute-start | bytes 688136 | tf_op jit(solution)/shard_map/ppermute | solution.py:38
  117.2 11.9 %collective-permute-start.29 = (bf16[7,32,512]{2,1,0:T(8,128)(2,1)}, bf16[7,32,512]{2,1,0:T(8,128)(2,1)S(1)}, u32[]{:S(2)}, u32[]{:S(2)}) collective-permute-start(bf16[7,32,512]{2,1,0:T(8,128)(2,1)} %collective-permute-done.28.refs_4_), channel_id=1, source_target_pairs={{0,32},{16,48},{32,64},{48,80},{64,96},{80,112},{96,128},{112,144}... | collective-permute-start | bytes 688136 | tf_op jit(solution)/shard_map/ppermute | solution.py:38
  117.3 11.8 %collective-permute-start.33 = (bf16[7,32,512]{2,1,0:T(8,128)(2,1)}, bf16[7,32,512]{2,1,0:T(8,128)(2,1)S(1)}, u32[]{:S(2)}, u32[]{:S(2)}) collective-permute-start(bf16[7,32,512]{2,1,0:T(8,128)(2,1)} %collective-permute-done.32.refs_10_), channel_id=1, source_target_pairs={{0,224},{16,240},{32,0},{48,16},{64,32},{80,48},{96,64},{112,80},{... | collective-permute-start | bytes 688136 | tf_op jit(solution)/shard_map/ppermute | solution.py:38
  130.0 6.3 %collective-permute-start.40 = (bf16[24,32,512]{2,1,0:T(8,128)(2,1)S(1)}, bf16[24,32,512]{2,1,0:T(8,128)(2,1)S(1)}, u32[]{:S(2)}, u32[]{:S(2)}) collective-permute-start(bf16[24,32,512]{2,1,0:T(8,128)(2,1)S(1)} %gradient_share.1), channel_id=1, source_target_pairs={{0,16},{16,0},{32,48},{48,32},{64,80},{80,64},{96,112},{112,96},{1... | collective-permute-start | bytes 2359304 | tf_op jit(solution)/shard_map/ppermute | solution.py:43
  (24 other events, 238.9 us)
Sparse Core Ops, SparseCore 0:
  20.5 112.7 reduce-scatter.3

commit v5 on v2

--- a/solution.py
+++ b/solution.py
@@ -287,25 +287,63 @@
     return lax.dot_general(grad, weight, (((1,), (1,)), ((), ())), preferred_element_type=F32)
 
 
-def products_kernel(grad_ref, weight_ref, out_ref):
-    value = product(grad_ref[...], weight_ref[...]).astype(BF)
-    width = out_ref.shape[2]
-    for k in range(out_ref.shape[0]):
-        out_ref[k] = value[:, k * width : (k + 1) * width]
+def products_kernel(grad_ref, weight_ref, out_ref, held, done, came, left):
+    step, steps = pl.program_id(0), held.shape[0]
+    tile, (slots, blocks, rows, width) = held.shape[1], done.shape
+    half = rows // 2
+
+    def arriving(at):
+        return pltpu.make_async_copy(weight_ref.at[pl.ds(at * tile, tile)], held.at[at], came.at[at])
+
+    def leaving(at, k, part):
+        slot, here = lax.rem(at, slots), pl.ds(part * half, half)
+        return pltpu.make_async_copy(
+            done.at[slot, k, here], out_ref.at[at * blocks + k, here], left.at[slot, k, part]
+        )
+
+    @pl.when(step == 0)
+    def _():
+        for at in range(steps):
+            arriving(at).start()
+
+    arriving(step).wait()
+
+    @pl.when(step >= slots)
+    def _():
+        for k in range(blocks):
+            for part in range(2):
+                leaving(step - slots, k, part).wait()
+
+    for k in range(blocks):
+        weight = held[step, k * width : (k + 1) * width, :]
+        done[lax.rem(step, slots), k] = product(grad_ref[...], weight).astype(BF)
+        for part in range(2):
+            leaving(step, k, part).start()
+
+    @pl.when(step == steps - 1)
+    def _():
+        for back in range(slots - 1, -1, -1):
+            for k in range(blocks):
+                for part in range(2):
+                    leaving(step - back, k, part).wait()
 
 
 def products(grad, weight, blocks):
     (rows, depth), columns = grad.shape, weight.shape[0]
     width, tile = columns // blocks, TILE
+    steps, each = columns // tile, tile // width
     return pl.pallas_call(
         products_kernel,
-        grid=(columns // tile,),
+        grid=(steps,),
         out_shape=jax.ShapeDtypeStruct((blocks, rows, width), BF),
-        in_specs=[
-            pl.BlockSpec((rows, depth), lambda j: (0, 0)),
-            pl.BlockSpec((tile, depth), lambda j: (j, 0)),
+        in_specs=[pl.BlockSpec((rows, depth), lambda j: (0, 0)), ANY()],
+        out_specs=ANY(),
+        scratch_shapes=[
+            pltpu.VMEM((steps, tile, depth), BF),
+            pltpu.VMEM((2, each, rows, width), BF),
+            pltpu.SemaphoreType.DMA((steps,)),
+            pltpu.SemaphoreType.DMA((2, each, 2)),
         ],
-        out_specs=pl.BlockSpec((tile // width, rows, width), lambda j: (j, 0, 0)),
         compiler_params=pltpu.CompilerParams(vmem_limit_bytes=BASE_VMEM),
         cost_estimate=pl.CostEstimate(
             flops=2 * rows * depth * columns, bytes_accessed=24 * 2**20, transcendentals=0

time: 145 us -> 145 us (level)
  starting transfers between devices: 62.7 us -> 64.3 us
  transfers between devices with their start and end apart: 42 -> 42, of which waited for: 23 -> 22; matrix products, arithmetic and copies ran while one was open for 1% -> 1% of each run, Pallas kernels for 7% -> 7%
where the time goes in v5:
time: 145 us; the launch traced here: 144 us
  starting transfers between devices  64.3 us (44%)
  waiting for transfers between devices  37.1 us (26%)
  Pallas kernels  23.4 us (16%)
  between operations  14.3 us (10%)
  local copies, waits for them, and re-layouts  4.41 us (3%)
    ppermute x28, starting transfers between devices, z_hop(): return lax.ppermute(x, 'dp', perm)  40.9 us
    ppermute x28, waiting for transfers between devices, z_hop(): return lax.ppermute(x, 'dp', perm)  21 us
    pallas_call x1, Pallas kernels, products(): pl.pallas_call(products_kernel, grid=(steps,), out_shape=jax.ShapeDtypeSt...  12.4 us
    ppermute x9, starting transfers between devices, plane_hop(): return lax.ppermute(x, 'tensor', perm)  12.1 us
    ppermute x9, waiting for transfers between devices, plane_hop(): return lax.ppermute(x, 'tensor', perm)  11.7 us
    ppermute x4, starting transfers between devices, core_swap(): return lax.ppermute(x, 'dp', [(d, d ^ 1) for d in range(n)])  11.2 us
    ppermute x4, waiting for transfers between devices, core_swap(): return lax.ppermute(x, 'dp', [(d, d ^ 1) for d in range(n)])  4.45 us
    pallas_call x1, Pallas kernels, total(): pl.pallas_call(functools.partial(total_kernel, needs), out_shape=(shape,...  3.66 us
  transfers between devices with their start and end apart: 42, of which 22 were waited for; matrix products, arithmetic and copies ran while one was open for 1% of the time, Pallas kernels for 7%

profile of v5, /device:TPU:1, one launch (start us, length us, event | category | flops | bytes accessed | tf_op | source)
XLA Modules:
  0.0 144.4 jit_solution(2608083508822754524)
XLA Ops:
  7.2 12.4 %base_products.1 = bf16[16,896,512]{2,1,0:T(8,128)(2,1)} custom-call(bf16[896,512]{1,0:T(8,128)(2,1)} %grad_ref.3, bf16[8192,512]{1,0:T(8,128)(2,1)} %weight_ref.1), custom_call_target="tpu_custom_call" | custom-call | flops 7516192768 | bytes 25165824 | tf_op jit(solution)/shard_map/base_products/pallas_call | solution.py:335
  20.6 2.5 %collective-permute-start.4 = (bf16[128,512]{1,0:T(8,128)(2,1)S(1)}, bf16[128,512]{1,0:T(8,128)(2,1)S(1)}, u32[]{:S(2)}, u32[]{:S(2)}) collective-permute-start(bf16[128,512]{1,0:T(8,128)(2,1)S(1)} %bitcast.14), channel_id=1, source_target_pairs={{0,32},{16,48},{32,64},{48,80},{64,96},{80,112},{96,128},{112,144}... | collective-permute-start | bytes 393224 | tf_op jit(solution)/shard_map/ppermute | solution.py:38
  23.0 3.9 %collective-permute-start.1 = (bf16[128,512]{1,0:T(8,128)(2,1)S(1)}, bf16[128,512]{1,0:T(8,128)(2,1)S(1)}, u32[]{:S(2)}, u32[]{:S(2)}) collective-permute-start(bf16[128,512]{1,0:T(8,128)(2,1)S(1)} %bitcast.15), channel_id=1, source_target_pairs={{0,224},{16,240},{32,0},{48,16},{64,32},{80,48},{96,64},{112,80},{... | collective-permute-start | bytes 393224 | tf_op jit(solution)/shard_map/ppermute | solution.py:38
  28.4 2.7 %collective-permute-start.8 = (bf16[144,512]{1,0:T(8,128)(2,1)S(1)}, bf16[144,512]{1,0:T(8,128)(2,1)S(1)}, u32[]{:S(2)}, u32[]{:S(2)}) collective-permute-start(bf16[144,512]{1,0:T(8,128)(2,1)S(1)} %fusion.1.refs_8_), channel_id=1, source_target_pairs={{0,224},{16,240},{32,0},{48,16},{64,32},{80,48},{96,64},{112,80},{... | collective-permute-start | bytes 442376 | tf_op jit(solution)/shard_map/ppermute | solution.py:38
  31.6 2.4 %collective-permute-done.8.refs_9_ = bf16[144,512]{1,0:T(8,128)(2,1)S(1)} collective-permute-done((bf16[144,512]{1,0:T(8,128)(2,1)S(1)}, bf16[144,512]{1,0:T(8,128)(2,1)S(1)}, u32[]{:S(2)}, u32[]{:S(2)}) %collective-permute-start.8) | collective-permute-done | bytes 147488 | tf_op jit(solution)/shard_map/ppermute | solution.py:38
  34.0 3.4 %collective-permute-start.9 = (bf16[144,512]{1,0:T(8,128)(2,1)S(1)}, bf16[144,512]{1,0:T(8,128)(2,1)S(1)}, u32[]{:S(2)}, u32[]{:S(2)}) collective-permute-start(bf16[144,512]{1,0:T(8,128)(2,1)S(1)} %collective-permute-done.8.refs_9_), channel_id=1, source_target_pairs={{0,224},{16,240},{32,0},{48,16},{64,32},{80,48},{96,64},{112,80},{... | collective-permute-start | bytes 442376 | tf_op jit(solution)/shard_map/ppermute | solution.py:38
  39.5 3.5 %collective-permute-start.10 = (bf16[144,512]{1,0:T(8,128)(2,1)S(1)}, bf16[144,512]{1,0:T(8,128)(2,1)S(1)}, u32[]{:S(2)}, u32[]{:S(2)}) collective-permute-start(bf16[144,512]{1,0:T(8,128)(2,1)S(1)} %collective-permute-done.9.refs_10_), channel_id=1, source_target_pairs={{0,224},{16,240},{32,0},{48,16},{64,32},{80,48},{96,64},{112,80},{... | collective-permute-start | bytes 442376 | tf_op jit(solution)/shard_map/ppermute | solution.py:38
  43.1 2.7 %collective-permute-start.3 = (bf16[128,512]{1,0:T(8,128)(2,1)S(1)}, bf16[128,512]{1,0:T(8,128)(2,1)S(1)}, u32[]{:S(2)}, u32[]{:S(2)}) collective-permute-start(bf16[128,512]{1,0:T(8,128)(2,1)S(1)} %collective-permute-done.2.refs_2_), channel_id=1, source_target_pairs={{0,224},{16,240},{32,0},{48,16},{64,32},{80,48},{96,64},{112,80},{... | collective-permute-start | bytes 393224 | tf_op jit(solution)/shard_map/ppermute | solution.py:38
  46.1 3.0 %collective-permute-start.11 = (bf16[144,512]{1,0:T(8,128)(2,1)S(1)}, bf16[144,512]{1,0:T(8,128)(2,1)S(1)}, u32[]{:S(2)}, u32[]{:S(2)}) collective-permute-start(bf16[144,512]{1,0:T(8,128)(2,1)S(1)} %collective-permute-done.10.refs_11_), channel_id=1, source_target_pairs={{0,224},{16,240},{32,0},{48,16},{64,32},{80,48},{96,64},{112,80},{... | collective-permute-start | bytes 442376 | tf_op jit(solution)/shard_map/ppermute | solution.py:38
  49.2 2.2 %collective-permute-done.14.refs_13_ = bf16[144,512]{1,0:T(8,128)(2,1)S(1)} collective-permute-done((bf16[144,512]{1,0:T(8,128)(2,1)S(1)}, bf16[144,512]{1,0:T(8,128)(2,1)S(1)}, u32[]{:S(2)}, u32[]{:S(2)}) %collective-permute-start.14) | collective-permute-done | bytes 147488 | tf_op jit(solution)/shard_map/ppermute | solution.py:38
  52.8 1.6 %pick_factors.1 = (bf16[16,32,512]{2,1,0:T(8,128)(2,1)S(1)}, bf16[16,32,512]{2,1,0:T(8,128)(2,1)}, bf16[16,32,512]{2,1,0:T(8,128)(2,1)S(1)}, bf16[16,32,512]{2,1,0:T(8,128)(2,1)S(1)}, bf16[8,16,128]{2,1,0:T(8,128)(2,1)S(1)}) custom-call(s32[8]{0:T(128)S(1)} %select_reduce_fusion.2.within_mine, s32[8]{0:T(128)S(1)} %select_reduce_fusion.1.within_other, ...), custom_call_target="tpu_custom_call" | custom-call | bytes 6291456 | tf_op jit(solution)/shard_map/pick_factors/pallas_call | solution.py:94
  56.0 3.3 %collective-permute-start.15 = (bf16[16,32,512]{2,1,0:T(8,128)(2,1)}, bf16[16,32,512]{2,1,0:T(8,128)(2,1)S(1)}, u32[]{:S(2)}, u32[]{:S(2)}) collective-permute-start(bf16[16,32,512]{2,1,0:T(8,128)(2,1)} %get-tuple-element.25), channel_id=1, source_target_pairs={{0,16},{16,0},{32,48},{48,32},{64,80},{80,64},{96,112},{112,96},{1... | collective-permute-start | bytes 1572872 | tf_op jit(solution)/shard_map/ppermute | solution.py:43
  59.3 1.7 %collective-permute-done.15.other_ref = bf16[16,32,512]{2,1,0:T(8,128)(2,1)S(1)} collective-permute-done((bf16[16,32,512]{2,1,0:T(8,128)(2,1)}, bf16[16,32,512]{2,1,0:T(8,128)(2,1)S(1)}, u32[]{:S(2)}, u32[]{:S(2)}) %collective-permute-start.15) | collective-permute-done | bytes 524320 | tf_op jit(solution)/shard_map/ppermute | solution.py:43
  63.7 2.6 %collective-permute-start.17 = (bf16[4,32,128]{2,1,0:T(8,128)(2,1)S(1)}, bf16[4,32,128]{2,1,0:T(8,128)(2,1)S(1)}, u32[]{:S(2)}, u32[]{:S(2)}) collective-permute-start(bf16[4,32,128]{2,1,0:T(8,128)(2,1)S(1)} %get-tuple-element.28), channel_id=1, source_target_pairs={{0,2},{1,3},{2,0},{3,1},{4,6},{5,7},{6,4},{7,5},{8,10},{9,11},{10,... | collective-permute-start | bytes 98312 | tf_op jit(solution)/shard_map/ppermute | solution.py:52
  67.5 2.8 %collective-permute-done.17 = bf16[4,32,128]{2,1,0:T(8,128)(2,1)S(1)} collective-permute-done((bf16[4,32,128]{2,1,0:T(8,128)(2,1)S(1)}, bf16[4,32,128]{2,1,0:T(8,128)(2,1)S(1)}, u32[]{:S(2)}, u32[]{:S(2)}) %collective-permute-start.17) | collective-permute-done | bytes 32800 | tf_op jit(solution)/shard_map/ppermute | solution.py:52
  70.3 2.5 %collective-permute-start.21 = (bf16[4,32,128]{2,1,0:T(8,128)(2,1)S(1)}, bf16[4,32,128]{2,1,0:T(8,128)(2,1)S(1)}, u32[]{:S(2)}, u32[]{:S(2)}) collective-permute-start(bf16[4,32,128]{2,1,0:T(8,128)(2,1)S(1)} %add_convert_fusion.1), channel_id=1, source_target_pairs={{0,12},{1,13},{2,14},{3,15},{4,0},{5,1},{6,2},{7,3},{8,4},{9,5},{1... | collective-permute-start | bytes 98312 | tf_op jit(solution)/shard_map/ppermute | solution.py:52
  74.2 3.5 %collective-permute-done.20 = bf16[4,32,128]{2,1,0:T(8,128)(2,1)S(1)} collective-permute-done((bf16[4,32,128]{2,1,0:T(8,128)(2,1)S(1)}, bf16[4,32,128]{2,1,0:T(8,128)(2,1)S(1)}, u32[]{:S(2)}, u32[]{:S(2)}) %collective-permute-start.20) | collective-permute-done | bytes 32800 | tf_op jit(solution)/shard_map/ppermute | solution.py:52
  78.6 2.5 %collective-permute-start.24 = (bf16[4,32,128]{2,1,0:T(8,128)(2,1)S(1)}, bf16[4,32,128]{2,1,0:T(8,128)(2,1)S(1)}, u32[]{:S(2)}, u32[]{:S(2)}) collective-permute-start(bf16[4,32,128]{2,1,0:T(8,128)(2,1)S(1)} %add_convert_fusion.refs_0_), channel_id=1, source_target_pairs={{0,3},{1,0},{2,1},{3,2},{4,7},{5,4},{6,5},{7,6},{8,11},{9,8},{10,9... | collective-permute-start | bytes 98312 | tf_op jit(solution)/shard_map/ppermute | solution.py:52
  82.5 3.4 %collective-permute-done.23.refs_2_ = bf16[4,32,128]{2,1,0:T(8,128)(2,1)S(1)} collective-permute-done((bf16[4,32,128]{2,1,0:T(8,128)(2,1)S(1)}, bf16[4,32,128]{2,1,0:T(8,128)(2,1)S(1)}, u32[]{:S(2)}, u32[]{:S(2)}) %collective-permute-start.23) | collective-permute-done | bytes 32800 | tf_op jit(solution)/shard_map/ppermute | solution.py:52
  88.2 1.9 %collective-permute-start.30 = (bf16[7,32,512]{2,1,0:T(8,128)(2,1)S(1)}, bf16[7,32,512]{2,1,0:T(8,128)(2,1)S(1)}, u32[]{:S(2)}, u32[]{:S(2)}) collective-permute-start(bf16[7,32,512]{2,1,0:T(8,128)(2,1)S(1)} %get-tuple-element.36.refs_7_), channel_id=1, source_target_pairs={{0,224},{16,240},{32,0},{48,16},{64,32},{80,48},{96,64},{112,80},{... | collective-permute-start | bytes 688136 | tf_op jit(solution)/shard_map/ppermute | solution.py:38
  91.5 2.3 %collective-permute-done.26.refs_6_ = bf16[7,32,512]{2,1,0:T(8,128)(2,1)S(1)} collective-permute-done((bf16[7,32,512]{2,1,0:T(8,128)(2,1)S(1)}, bf16[7,32,512]{2,1,0:T(8,128)(2,1)S(1)}, u32[]{:S(2)}, u32[]{:S(2)}) %collective-permute-start.26) | collective-permute-done | bytes 229408 | tf_op jit(solution)/shard_map/ppermute | solution.py:38
  93.8 2.7 %collective-permute-start.31 = (bf16[7,32,512]{2,1,0:T(8,128)(2,1)S(1)}, bf16[7,32,512]{2,1,0:T(8,128)(2,1)S(1)}, u32[]{:S(2)}, u32[]{:S(2)}) collective-permute-start(bf16[7,32,512]{2,1,0:T(8,128)(2,1)S(1)} %collective-permute-done.30.refs_8_), channel_id=1, source_target_pairs={{0,224},{16,240},{32,0},{48,16},{64,32},{80,48},{96,64},{112,80},{... | collective-permute-start | bytes 688136 | tf_op jit(solution)/shard_map/ppermute | solution.py:38
  96.7 2.4 %collective-permute-start.35 = (bf16[7,32,512]{2,1,0:T(8,128)(2,1)S(1)}, bf16[7,32,512]{2,1,0:T(8,128)(2,1)}, u32[]{:S(2)}, u32[]{:S(2)}) collective-permute-start(bf16[7,32,512]{2,1,0:T(8,128)(2,1)S(1)} %collective-permute-done.34.refs_1_), channel_id=1, source_target_pairs={{0,224},{16,240},{32,0},{48,16},{64,32},{80,48},{96,64},{112,80},{... | collective-permute-start | bytes 688136 | tf_op jit(solution)/shard_map/ppermute | solution.py:38
  100.0 4.4 %collective-permute-done.27.refs_5_ = bf16[7,32,512]{2,1,0:T(8,128)(2,1)S(1)} collective-permute-done((bf16[7,32,512]{2,1,0:T(8,128)(2,1)S(1)}, bf16[7,32,512]{2,1,0:T(8,128)(2,1)S(1)}, u32[]{:S(2)}, u32[]{:S(2)}) %collective-permute-start.27) | collective-permute-done | bytes 229408 | tf_op jit(solution)/shard_map/ppermute | solution.py:38
  104.4 2.7 %collective-permute-start.32 = (bf16[7,32,512]{2,1,0:T(8,128)(2,1)S(1)}, bf16[7,32,512]{2,1,0:T(8,128)(2,1)}, u32[]{:S(2)}, u32[]{:S(2)}) collective-permute-start(bf16[7,32,512]{2,1,0:T(8,128)(2,1)S(1)} %collective-permute-done.31.refs_9_), channel_id=1, source_target_pairs={{0,224},{16,240},{32,0},{48,16},{64,32},{80,48},{96,64},{112,80},{... | collective-permute-start | bytes 688136 | tf_op jit(solution)/shard_map/ppermute | solution.py:38
  107.2 1.8 %collective-permute-start.36 = (bf16[7,32,512]{2,1,0:T(8,128)(2,1)}, bf16[7,32,512]{2,1,0:T(8,128)(2,1)}, u32[]{:S(2)}, u32[]{:S(2)}) collective-permute-start(bf16[7,32,512]{2,1,0:T(8,128)(2,1)} %collective-permute-done.35.refs_2_), channel_id=1, source_target_pairs={{0,224},{16,240},{32,0},{48,16},{64,32},{80,48},{96,64},{112,80},{... | collective-permute-start | bytes 688136 | tf_op jit(solution)/shard_map/ppermute | solution.py:38
  109.4 3.6 %collective-permute-done.28.refs_4_ = bf16[7,32,512]{2,1,0:T(8,128)(2,1)} collective-permute-done((bf16[7,32,512]{2,1,0:T(8,128)(2,1)S(1)}, bf16[7,32,512]{2,1,0:T(8,128)(2,1)}, u32[]{:S(2)}, u32[]{:S(2)}) %collective-permute-start.28) | collective-permute-done | bytes 229408 | tf_op jit(solution)/shard_map/ppermute | solution.py:38
  113.0 2.7 %collective-permute-start.33 = (bf16[7,32,512]{2,1,0:T(8,128)(2,1)}, bf16[7,32,512]{2,1,0:T(8,128)(2,1)S(1)}, u32[]{:S(2)}, u32[]{:S(2)}) collective-permute-start(bf16[7,32,512]{2,1,0:T(8,128)(2,1)} %collective-permute-done.32.refs_10_), channel_id=1, source_target_pairs={{0,224},{16,240},{32,0},{48,16},{64,32},{80,48},{96,64},{112,80},{... | collective-permute-start | bytes 688136 | tf_op jit(solution)/shard_map/ppermute | solution.py:38
  118.6 3.7 %gradient_totals.1 = (f32[24,32,512]{2,1,0:T(8,128)S(1)}, f32[24,32,512]{2,1,0:T(8,128)S(1)}) custom-call(s32[192]{0:T(256)S(1)} %reshape.69.place, s32[192]{0:T(256)S(1)} %reshape.70.used, bf16[7,32,512]{2,1,0:T(8,128)(2,1)S(1)} %get-tuple-element.35.refs_0_, bf16[7,32,512]{2,1,0:T(8,128)(2,1)S(1)} %collective-permute-done.34.refs_1_, ...), custom_call_target="tpu_custom_call" | custom-call | bytes 16777216 | tf_op jit(solution)/shard_map/gradient_totals/pallas_call | solution.py:208
  123.5 6.7 %collective-permute-start.40 = (bf16[24,32,512]{2,1,0:T(8,128)(2,1)S(1)}, bf16[24,32,512]{2,1,0:T(8,128)(2,1)S(1)}, u32[]{:S(2)}, u32[]{:S(2)}) collective-permute-start(bf16[24,32,512]{2,1,0:T(8,128)(2,1)S(1)} %gradient_share.1), channel_id=1, source_target_pairs={{0,16},{16,0},{32,48},{48,32},{64,80},{80,64},{96,112},{112,96},{1... | collective-permute-start | bytes 2359304 | tf_op jit(solution)/shard_map/ppermute | solution.py:43
  130.5 2.7 %collective-permute-done.25.other_roll = bf16[16,32,512]{2,1,0:T(8,128)(2,1)S(1)} collective-permute-done((bf16[16,32,512]{2,1,0:T(8,128)(2,1)}, bf16[16,32,512]{2,1,0:T(8,128)(2,1)S(1)}, u32[]{:S(2)}, u32[]{:S(2)}) %collective-permute-start.25) | collective-permute-done | bytes 524320 | tf_op jit(solution)/shard_map/ppermute | solution.py:43
  133.2 1.8 %update_factors.1 = (bf16[4,32,512]{2,1,0:T(8,128)(2,1)}, bf16[4,32,512]{2,1,0:T(8,128)(2,1)}, bf16[8,32,512]{2,1,0:T(8,128)(2,1)}, bf16[8,32,512]{2,1,0:T(8,128)(2,1)}) custom-call(s32[192]{0:T(256)S(1)} %reshape.69.place, s32[192]{0:T(256)S(1)} %reshape.70.used, s32[8]{0:T(128)S(1)} %slice.76.own_ref, bf16[4,32,512]{2,1,0:T(8,128)(2,1)S(1)} %copy-done.3, ...), custom_call_target="tpu_custom_call" | custom-call | bytes 8388608 | tf_op jit(solution)/shard_map/update_factors/pallas_call | solution.py:275
  (119 shorter events, 27.9 us)
Async XLA Ops:
  7.2 127.8 %reduce-scatter.4.cloned.1.call-start = ((), (), s32[]{:S(2)}) async-start(), calls=%async_computation.1 | async-start | bytes 15597568
  20.6 10.9 %collective-permute-start.4 = (bf16[128,512]{1,0:T(8,128)(2,1)S(1)}, bf16[128,512]{1,0:T(8,128)(2,1)S(1)}, u32[]{:S(2)}, u32[]{:S(2)}) collective-permute-start(bf16[128,512]{1,0:T(8,128)(2,1)S(1)} %bitcast.14), channel_id=1, source_target_pairs={{0,32},{16,48},{32,64},{48,80},{64,96},{80,112},{96,128},{112,144}... | collective-permute-start | bytes 393224 | tf_op jit(solution)/shard_map/ppermute | solution.py:38
  23.0 14.4 %collective-permute-start.1 = (bf16[128,512]{1,0:T(8,128)(2,1)S(1)}, bf16[128,512]{1,0:T(8,128)(2,1)S(1)}, u32[]{:S(2)}, u32[]{:S(2)}) collective-permute-start(bf16[128,512]{1,0:T(8,128)(2,1)S(1)} %bitcast.15), channel_id=1, source_target_pairs={{0,224},{16,240},{32,0},{48,16},{64,32},{80,48},{96,64},{112,80},{... | collective-permute-start | bytes 393224 | tf_op jit(solution)/shard_map/ppermute | solution.py:38
  28.4 9.2 %collective-permute-start.12 = (bf16[144,512]{1,0:T(8,128)(2,1)S(1)}, bf16[144,512]{1,0:T(8,128)(2,1)S(1)}, u32[]{:S(2)}, u32[]{:S(2)}) collective-permute-start(bf16[144,512]{1,0:T(8,128)(2,1)S(1)} %fusion.1.refs_8_), channel_id=1, source_target_pairs={{0,32},{16,48},{32,64},{48,80},{64,96},{80,112},{96,128},{112,144}... | collective-permute-start | bytes 442376 | tf_op jit(solution)/shard_map/ppermute | solution.py:38
  28.4 5.6 %collective-permute-start.8 = (bf16[144,512]{1,0:T(8,128)(2,1)S(1)}, bf16[144,512]{1,0:T(8,128)(2,1)S(1)}, u32[]{:S(2)}, u32[]{:S(2)}) collective-permute-start(bf16[144,512]{1,0:T(8,128)(2,1)S(1)} %fusion.1.refs_8_), channel_id=1, source_target_pairs={{0,224},{16,240},{32,0},{48,16},{64,32},{80,48},{96,64},{112,80},{... | collective-permute-start | bytes 442376 | tf_op jit(solution)/shard_map/ppermute | solution.py:38
  31.5 7.4 %collective-permute-start.5 = (bf16[128,512]{1,0:T(8,128)(2,1)S(1)}, bf16[128,512]{1,0:T(8,128)(2,1)S(1)}, u32[]{:S(2)}, u32[]{:S(2)}) collective-permute-start(bf16[128,512]{1,0:T(8,128)(2,1)S(1)} %collective-permute-done.4.refs_7_), channel_id=1, source_target_pairs={{0,32},{16,48},{32,64},{48,80},{64,96},{80,112},{96,128},{112,144}... | collective-permute-start | bytes 393224 | tf_op jit(solution)/shard_map/ppermute | solution.py:38
  34.0 5.5 %collective-permute-start.9 = (bf16[144,512]{1,0:T(8,128)(2,1)S(1)}, bf16[144,512]{1,0:T(8,128)(2,1)S(1)}, u32[]{:S(2)}, u32[]{:S(2)}) collective-permute-start(bf16[144,512]{1,0:T(8,128)(2,1)S(1)} %collective-permute-done.8.refs_9_), channel_id=1, source_target_pairs={{0,224},{16,240},{32,0},{48,16},{64,32},{80,48},{96,64},{112,80},{... | collective-permute-start | bytes 442376 | tf_op jit(solution)/shard_map/ppermute | solution.py:38
  37.5 5.6 %collective-permute-start.2 = (bf16[128,512]{1,0:T(8,128)(2,1)S(1)}, bf16[128,512]{1,0:T(8,128)(2,1)S(1)}, u32[]{:S(2)}, u32[]{:S(2)}) collective-permute-start(bf16[128,512]{1,0:T(8,128)(2,1)S(1)} %collective-permute-done.1.refs_1_), channel_id=1, source_target_pairs={{0,224},{16,240},{32,0},{48,16},{64,32},{80,48},{96,64},{112,80},{... | collective-permute-start | bytes 393224 | tf_op jit(solution)/shard_map/ppermute | solution.py:38
  37.5 8.2 %collective-permute-start.13 = (bf16[144,512]{1,0:T(8,128)(2,1)S(1)}, bf16[144,512]{1,0:T(8,128)(2,1)S(1)}, u32[]{:S(2)}, u32[]{:S(2)}) collective-permute-start(bf16[144,512]{1,0:T(8,128)(2,1)S(1)} %collective-permute-done.12.refs_15_), channel_id=1, source_target_pairs={{0,32},{16,48},{32,64},{48,80},{64,96},{80,112},{96,128},{112,144}... | collective-permute-start | bytes 442376 | tf_op jit(solution)/shard_map/ppermute | solution.py:38
  38.9 6.9 %collective-permute-start.6 = (bf16[128,512]{1,0:T(8,128)(2,1)S(1)}, bf16[128,512]{1,0:T(8,128)(2,1)S(1)}, u32[]{:S(2)}, u32[]{:S(2)}) collective-permute-start(bf16[128,512]{1,0:T(8,128)(2,1)S(1)} %collective-permute-done.5.refs_6_), channel_id=1, source_target_pairs={{0,32},{16,48},{32,64},{48,80},{64,96},{80,112},{96,128},{112,144}... | collective-permute-start | bytes 393224 | tf_op jit(solution)/shard_map/ppermute | solution.py:38
  39.5 6.5 %collective-permute-start.10 = (bf16[144,512]{1,0:T(8,128)(2,1)S(1)}, bf16[144,512]{1,0:T(8,128)(2,1)S(1)}, u32[]{:S(2)}, u32[]{:S(2)}) collective-permute-start(bf16[144,512]{1,0:T(8,128)(2,1)S(1)} %collective-permute-done.9.refs_10_), channel_id=1, source_target_pairs={{0,224},{16,240},{32,0},{48,16},{64,32},{80,48},{96,64},{112,80},{... | collective-permute-start | bytes 442376 | tf_op jit(solution)/shard_map/ppermute | solution.py:38
  43.1 6.2 %collective-permute-start.3 = (bf16[128,512]{1,0:T(8,128)(2,1)S(1)}, bf16[128,512]{1,0:T(8,128)(2,1)S(1)}, u32[]{:S(2)}, u32[]{:S(2)}) collective-permute-start(bf16[128,512]{1,0:T(8,128)(2,1)S(1)} %collective-permute-done.2.refs_2_), channel_id=1, source_target_pairs={{0,224},{16,240},{32,0},{48,16},{64,32},{80,48},{96,64},{112,80},{... | collective-permute-start | bytes 393224 | tf_op jit(solution)/shard_map/ppermute | solution.py:38
  45.8 5.6 %collective-permute-start.14 = (bf16[144,512]{1,0:T(8,128)(2,1)S(1)}, bf16[144,512]{1,0:T(8,128)(2,1)S(1)}, u32[]{:S(2)}, u32[]{:S(2)}) collective-permute-start(bf16[144,512]{1,0:T(8,128)(2,1)S(1)} %collective-permute-done.13.refs_14_), channel_id=1, source_target_pairs={{0,32},{16,48},{32,64},{48,80},{64,96},{80,112},{96,128},{112,144}... | collective-permute-start | bytes 442376 | tf_op jit(solution)/shard_map/ppermute | solution.py:38
  45.8 7.0 %collective-permute-start.7 = (bf16[128,512]{1,0:T(8,128)(2,1)S(1)}, bf16[128,512]{1,0:T(8,128)(2,1)S(1)}, u32[]{:S(2)}, u32[]{:S(2)}) collective-permute-start(bf16[128,512]{1,0:T(8,128)(2,1)S(1)} %collective-permute-done.6.refs_5_), channel_id=1, source_target_pairs={{0,32},{16,48},{32,64},{48,80},{64,96},{80,112},{96,128},{112,144}... | collective-permute-start | bytes 393224 | tf_op jit(solution)/shard_map/ppermute | solution.py:38
  46.1 6.7 %collective-permute-start.11 = (bf16[144,512]{1,0:T(8,128)(2,1)S(1)}, bf16[144,512]{1,0:T(8,128)(2,1)S(1)}, u32[]{:S(2)}, u32[]{:S(2)}) collective-permute-start(bf16[144,512]{1,0:T(8,128)(2,1)S(1)} %collective-permute-done.10.refs_11_), channel_id=1, source_target_pairs={{0,224},{16,240},{32,0},{48,16},{64,32},{80,48},{96,64},{112,80},{... | collective-permute-start | bytes 442376 | tf_op jit(solution)/shard_map/ppermute | solution.py:38
  63.7 6.6 %collective-permute-start.17 = (bf16[4,32,128]{2,1,0:T(8,128)(2,1)S(1)}, bf16[4,32,128]{2,1,0:T(8,128)(2,1)S(1)}, u32[]{:S(2)}, u32[]{:S(2)}) collective-permute-start(bf16[4,32,128]{2,1,0:T(8,128)(2,1)S(1)} %get-tuple-element.28), channel_id=1, source_target_pairs={{0,2},{1,3},{2,0},{3,1},{4,6},{5,7},{6,4},{7,5},{8,10},{9,11},{10,... | collective-permute-start | bytes 98312 | tf_op jit(solution)/shard_map/ppermute | solution.py:52
  73.4 5.2 %collective-permute-start.19 = (bf16[4,32,128]{2,1,0:T(8,128)(2,1)S(1)}, bf16[4,32,128]{2,1,0:T(8,128)(2,1)S(1)}, u32[]{:S(2)}, u32[]{:S(2)}) collective-permute-start(bf16[4,32,128]{2,1,0:T(8,128)(2,1)S(1)} %add_convert_fusion.1), channel_id=1, source_target_pairs={{0,4},{1,5},{2,6},{3,7},{4,8},{5,9},{6,10},{7,11},{8,12},{9,13},{1... | collective-permute-start | bytes 98312 | tf_op jit(solution)/shard_map/ppermute | solution.py:52
  86.6 7.2 %collective-permute-start.26 = (bf16[7,32,512]{2,1,0:T(8,128)(2,1)S(1)}, bf16[7,32,512]{2,1,0:T(8,128)(2,1)S(1)}, u32[]{:S(2)}, u32[]{:S(2)}) collective-permute-start(bf16[7,32,512]{2,1,0:T(8,128)(2,1)S(1)} %get-tuple-element.35.refs_0_), channel_id=1, source_target_pairs={{0,32},{16,48},{32,64},{48,80},{64,96},{80,112},{96,128},{112,144}... | collective-permute-start | bytes 688136 | tf_op jit(solution)/shard_map/ppermute | solution.py:38
  88.2 5.6 %collective-permute-start.30 = (bf16[7,32,512]{2,1,0:T(8,128)(2,1)S(1)}, bf16[7,32,512]{2,1,0:T(8,128)(2,1)S(1)}, u32[]{:S(2)}, u32[]{:S(2)}) collective-permute-start(bf16[7,32,512]{2,1,0:T(8,128)(2,1)S(1)} %get-tuple-element.36.refs_7_), channel_id=1, source_target_pairs={{0,224},{16,240},{32,0},{48,16},{64,32},{80,48},{96,64},{112,80},{... | collective-permute-start | bytes 688136 | tf_op jit(solution)/shard_map/ppermute | solution.py:38
  90.0 6.6 %collective-permute-start.34 = (bf16[7,32,512]{2,1,0:T(8,128)(2,1)S(1)}, bf16[7,32,512]{2,1,0:T(8,128)(2,1)S(1)}, u32[]{:S(2)}, u32[]{:S(2)}) collective-permute-start(bf16[7,32,512]{2,1,0:T(8,128)(2,1)S(1)} %get-tuple-element.35.refs_0_), channel_id=1, source_target_pairs={{0,224},{16,240},{32,0},{48,16},{64,32},{80,48},{96,64},{112,80},{... | collective-permute-start | bytes 688136 | tf_op jit(solution)/shard_map/ppermute | solution.py:38
  91.4 8.6 %collective-permute-start.37 = (bf16[7,32,512]{2,1,0:T(8,128)(2,1)S(1)}, bf16[7,32,512]{2,1,0:T(8,128)(2,1)S(1)}, u32[]{:S(2)}, u32[]{:S(2)}) collective-permute-start(bf16[7,32,512]{2,1,0:T(8,128)(2,1)S(1)} %get-tuple-element.36.refs_7_), channel_id=1, source_target_pairs={{0,32},{16,48},{32,64},{48,80},{64,96},{80,112},{96,128},{112,144}... | collective-permute-start | bytes 688136 | tf_op jit(solution)/shard_map/ppermute | solution.py:38
  93.8 10.7 %collective-permute-start.27 = (bf16[7,32,512]{2,1,0:T(8,128)(2,1)S(1)}, bf16[7,32,512]{2,1,0:T(8,128)(2,1)S(1)}, u32[]{:S(2)}, u32[]{:S(2)}) collective-permute-start(bf16[7,32,512]{2,1,0:T(8,128)(2,1)S(1)} %collective-permute-done.26.refs_6_), channel_id=1, source_target_pairs={{0,32},{16,48},{32,64},{48,80},{64,96},{80,112},{96,128},{112,144}... | collective-permute-start | bytes 688136 | tf_op jit(solution)/shard_map/ppermute | solution.py:38
  93.8 10.7 %collective-permute-start.31 = (bf16[7,32,512]{2,1,0:T(8,128)(2,1)S(1)}, bf16[7,32,512]{2,1,0:T(8,128)(2,1)S(1)}, u32[]{:S(2)}, u32[]{:S(2)}) collective-permute-start(bf16[7,32,512]{2,1,0:T(8,128)(2,1)S(1)} %collective-permute-done.30.refs_8_), channel_id=1, source_target_pairs={{0,224},{16,240},{32,0},{48,16},{64,32},{80,48},{96,64},{112,80},{... | collective-permute-start | bytes 688136 | tf_op jit(solution)/shard_map/ppermute | solution.py:38
  96.7 10.6 %collective-permute-start.35 = (bf16[7,32,512]{2,1,0:T(8,128)(2,1)S(1)}, bf16[7,32,512]{2,1,0:T(8,128)(2,1)}, u32[]{:S(2)}, u32[]{:S(2)}) collective-permute-start(bf16[7,32,512]{2,1,0:T(8,128)(2,1)S(1)} %collective-permute-done.34.refs_1_), channel_id=1, source_target_pairs={{0,224},{16,240},{32,0},{48,16},{64,32},{80,48},{96,64},{112,80},{... | collective-permute-start | bytes 688136 | tf_op jit(solution)/shard_map/ppermute | solution.py:38
  100.0 9.3 %collective-permute-start.38 = (bf16[7,32,512]{2,1,0:T(8,128)(2,1)S(1)}, bf16[7,32,512]{2,1,0:T(8,128)(2,1)}, u32[]{:S(2)}, u32[]{:S(2)}) collective-permute-start(bf16[7,32,512]{2,1,0:T(8,128)(2,1)S(1)} %collective-permute-done.37.refs_13_), channel_id=1, source_target_pairs={{0,32},{16,48},{32,64},{48,80},{64,96},{80,112},{96,128},{112,144}... | collective-permute-start | bytes 688136 | tf_op jit(solution)/shard_map/ppermute | solution.py:38
  104.4 8.5 %collective-permute-start.28 = (bf16[7,32,512]{2,1,0:T(8,128)(2,1)S(1)}, bf16[7,32,512]{2,1,0:T(8,128)(2,1)}, u32[]{:S(2)}, u32[]{:S(2)}) collective-permute-start(bf16[7,32,512]{2,1,0:T(8,128)(2,1)S(1)} %collective-permute-done.27.refs_5_), channel_id=1, source_target_pairs={{0,32},{16,48},{32,64},{48,80},{64,96},{80,112},{96,128},{112,144}... | collective-permute-start | bytes 688136 | tf_op jit(solution)/shard_map/ppermute | solution.py:38
  104.4 8.5 %collective-permute-start.32 = (bf16[7,32,512]{2,1,0:T(8,128)(2,1)S(1)}, bf16[7,32,512]{2,1,0:T(8,128)(2,1)}, u32[]{:S(2)}, u32[]{:S(2)}) collective-permute-start(bf16[7,32,512]{2,1,0:T(8,128)(2,1)S(1)} %collective-permute-done.31.refs_9_), channel_id=1, source_target_pairs={{0,224},{16,240},{32,0},{48,16},{64,32},{80,48},{96,64},{112,80},{... | collective-permute-start | bytes 688136 | tf_op jit(solution)/shard_map/ppermute | solution.py:38
  107.2 9.7 %collective-permute-start.36 = (bf16[7,32,512]{2,1,0:T(8,128)(2,1)}, bf16[7,32,512]{2,1,0:T(8,128)(2,1)}, u32[]{:S(2)}, u32[]{:S(2)}) collective-permute-start(bf16[7,32,512]{2,1,0:T(8,128)(2,1)} %collective-permute-done.35.refs_2_), channel_id=1, source_target_pairs={{0,224},{16,240},{32,0},{48,16},{64,32},{80,48},{96,64},{112,80},{... | collective-permute-start | bytes 688136 | tf_op jit(solution)/shard_map/ppermute | solution.py:38
  109.4 9.2 %collective-permute-start.39 = (bf16[7,32,512]{2,1,0:T(8,128)(2,1)}, bf16[7,32,512]{2,1,0:T(8,128)(2,1)}, u32[]{:S(2)}, u32[]{:S(2)}) collective-permute-start(bf16[7,32,512]{2,1,0:T(8,128)(2,1)} %collective-permute-done.38.refs_12_), channel_id=1, source_target_pairs={{0,32},{16,48},{32,64},{48,80},{64,96},{80,112},{96,128},{112,144}... | collective-permute-start | bytes 688136 | tf_op jit(solution)/shard_map/ppermute | solution.py:38
  113.0 9.7 %collective-permute-start.29 = (bf16[7,32,512]{2,1,0:T(8,128)(2,1)}, bf16[7,32,512]{2,1,0:T(8,128)(2,1)S(1)}, u32[]{:S(2)}, u32[]{:S(2)}) collective-permute-start(bf16[7,32,512]{2,1,0:T(8,128)(2,1)} %collective-permute-done.28.refs_4_), channel_id=1, source_target_pairs={{0,32},{16,48},{32,64},{48,80},{64,96},{80,112},{96,128},{112,144}... | collective-permute-start | bytes 688136 | tf_op jit(solution)/shard_map/ppermute | solution.py:38
  113.0 9.7 %collective-permute-start.33 = (bf16[7,32,512]{2,1,0:T(8,128)(2,1)}, bf16[7,32,512]{2,1,0:T(8,128)(2,1)S(1)}, u32[]{:S(2)}, u32[]{:S(2)}) collective-permute-start(bf16[7,32,512]{2,1,0:T(8,128)(2,1)} %collective-permute-done.32.refs_10_), channel_id=1, source_target_pairs={{0,224},{16,240},{32,0},{48,16},{64,32},{80,48},{96,64},{112,80},{... | collective-permute-start | bytes 688136 | tf_op jit(solution)/shard_map/ppermute | solution.py:38
  123.5 9.6 %collective-permute-start.40 = (bf16[24,32,512]{2,1,0:T(8,128)(2,1)S(1)}, bf16[24,32,512]{2,1,0:T(8,128)(2,1)S(1)}, u32[]{:S(2)}, u32[]{:S(2)}) collective-permute-start(bf16[24,32,512]{2,1,0:T(8,128)(2,1)S(1)} %gradient_share.1), channel_id=1, source_target_pairs={{0,16},{16,0},{32,48},{48,32},{64,80},{80,64},{96,112},{112,96},{1... | collective-permute-start | bytes 2359304 | tf_op jit(solution)/shard_map/ppermute | solution.py:43
  (21 other events, 231.3 us)
Sparse Core Ops, SparseCore 0:
  19.9 112.7 reduce-scatter.3
